TPU v7x, 32 devices: a whole 2x2x4 slice. The times are simulated.
32 devices in a mesh: blk: 8 (over z, x), pair: 4 (over y, core).
Axes of the slice: x: 2, y: 2, z: 4, core: 2. Of those that a mesh axis runs over, the one named last changes fastest.
Arguments:
- features: float32 [64, 65536], P(None, 'blk'), may hold values from -6 to 6
- inv_scale: float32 [64], replicated, may hold values from 0.03125 to 20
- signal: float32 [1], replicated, may hold values from 0.110485435 to 0.44194174
- noise_var: float32 [65536], P('blk'), may hold values from 0.5 to 2
- right_side: float32 [32, 65536], P(None, 'blk'), may hold values from -30 to 30
- block_pairs: int32 [128, 2], P(('blk', 'pair')), may hold values from -1 to 31, as said below
Outputs:
- solution: float32 [32, 65536], P(None, 'blk')
- residual: float32 [32, 65536], P(None, 'blk')
Inputs may be any that keep to these rules, and one draw needn't show every extreme that they name: `block_pairs`: rows run over the blk index, then the pair index, then 4 slots of one device. In each device's slots the live pairs come first; dead slots hold -1 in both columns. A live pair (i, j) has block i among blocks blk index * 4 to blk index * 4 + 3 of the device's blk index, and j equal to i or i + 1. Every block's pair (i, i) is listed once and no pair twice. In each blk index some device has all its slots live.
All inputs are finite; a program needn't handle non-finite values.
Results may differ from a plain program's by a relative error of at most 0.0011.
Values sent between devices are 32-bit elements; how exact they have to be, the bound alone decides.
No kernel may reach another device: no remote copies, remote signals or barrier semaphores. Data moves between devices by JAX's collectives and lax.ppermute only.
A program may use at most 64 MiB of HBM per device.

v0:
```python
import jax
import jax.numpy as jnp
from jax import lax
from jax.sharding import PartitionSpec as P

BS = 2048
ITERS = 2


root_three = 1.7320508075688772
taper_radius = 2.0


def passed_along(block, axis, distance):
    devices = range(lax.axis_size(axis))
    route = [(i - distance, i) for i in devices if i - distance in devices]
    return lax.ppermute(block, axis, route)


def kernel_tile(left_scaled, right_scaled, amplitude):
    cross = lax.dot_general(
        left_scaled,
        right_scaled,
        (((0,), (0,)), ((), ())),
        precision=lax.Precision.HIGHEST,
        preferred_element_type=jnp.float32,
    )
    left_norms = jnp.sum(left_scaled * left_scaled, axis=0)
    right_norms = jnp.sum(right_scaled * right_scaled, axis=0)
    squared = (left_norms[:, None] + right_norms[None, :] - 2.0 * cross) / left_scaled.shape[0]
    distance = jnp.sqrt(jnp.maximum(squared, 0.0))
    stretched = root_three * distance
    ratio = distance / taper_radius
    taper = jnp.maximum(1.0 - ratio, 0.0) ** 4 * (1.0 + 4.0 * ratio)
    return amplitude * (1.0 + stretched) * jnp.exp(-stretched) * taper


def block_terms(left_scaled, right_scaled, left_dir, right_dir, amplitude):
    block_rows = left_scaled.shape[1]
    row_step = min(512, block_rows)
    left_half = left_dir.astype(jnp.bfloat16)
    right_half = right_dir.astype(jnp.bfloat16)

    def rows_visit(position, carried):
        toward_left, toward_right, row_sums, col_sums = carried
        offset = position * row_step
        kernel_rows = kernel_tile(
            lax.dynamic_slice_in_dim(left_scaled, offset, row_step, 1), right_scaled, amplitude
        )
        rows_half = kernel_rows.astype(jnp.bfloat16)
        product = lax.dot_general(
            right_half, rows_half, (((1,), (1,)), ((), ())), preferred_element_type=jnp.float32
        )
        toward_left = lax.dynamic_update_slice_in_dim(toward_left, product, offset, 1)
        toward_right = toward_right + jnp.dot(
            lax.dynamic_slice_in_dim(left_half, offset, row_step, 1),
            rows_half,
            preferred_element_type=jnp.float32,
        )
        row_sums = lax.dynamic_update_slice_in_dim(
            row_sums, jnp.sum(kernel_rows, axis=1), offset, 0
        )
        col_sums = col_sums + jnp.sum(kernel_rows, axis=0)
        return (toward_left, toward_right, row_sums, col_sums)

    zeros_dir = jnp.zeros(left_dir.shape, jnp.float32)
    zeros_row = jnp.zeros((block_rows,), jnp.float32)
    return lax.fori_loop(
        0, block_rows // row_step, rows_visit, (zeros_dir, zeros_dir, zeros_row, zeros_row)
    )


def body(features, inv_scale, signal, noise_var, right_side, block_pairs):
    local_rows = features.shape[1]
    blocks_here = local_rows // BS
    amplitude = signal[0]
    scaled = features * inv_scale[:, None]
    beyond = passed_along(scaled[:, :BS], "blk", -1)
    reach_scaled = jnp.concatenate([scaled, beyond], axis=1)
    base_block = lax.axis_index("blk") * blocks_here
    members = lax.axis_size("pair")
    listing = lax.all_gather(block_pairs, "pair", axis=0, tiled=True)
    living = (listing[:, 0] >= 0).astype(jnp.int32)
    ranked = jnp.cumsum(living) - living
    wanted = lax.axis_index("pair") + members * jnp.arange(block_pairs.shape[0], dtype=jnp.int32)
    matched = (ranked[None, :] == wanted[:, None]) & (living[None, :] > 0)
    chosen = jnp.sum(jnp.where(matched[:, :, None], listing[None, :, :], 0), axis=1)
    my_pairs = jnp.where(jnp.any(matched, axis=1)[:, None], chosen, -1)
    active = jnp.maximum((jnp.sum(living) - lax.axis_index("pair") + members - 1) // members, 0)
    row_local = my_pairs[:, 0] - base_block
    col_local = my_pairs[:, 1] - base_block
    solution = jnp.zeros_like(right_side)
    residual = right_side
    direction = right_side
    norm_now = lax.psum(jnp.sum(residual * residual, axis=1), "blk")
    for iteration in range(ITERS):
        ahead_dir = passed_along(direction[:, :BS], "blk", -1)
        reach_dir = jnp.concatenate([direction, ahead_dir], axis=1)

        def visit(slot_index, summed):
            row_start = row_local[slot_index] * BS
            col_start = col_local[slot_index] * BS
            crossing = (row_local[slot_index] != col_local[slot_index]).astype(jnp.float32)
            left_dir = lax.dynamic_slice_in_dim(reach_dir, row_start, BS, 1)
            right_dir = lax.dynamic_slice_in_dim(reach_dir, col_start, BS, 1)
            toward_left, toward_right, row_sums, col_sums = block_terms(
                lax.dynamic_slice_in_dim(reach_scaled, row_start, BS, 1),
                lax.dynamic_slice_in_dim(reach_scaled, col_start, BS, 1),
                left_dir,
                right_dir,
                amplitude,
            )
            term_left = toward_left + crossing * row_sums[None, :] * left_dir
            term_right = crossing * (toward_right + col_sums[None, :] * right_dir)
            summed = lax.dynamic_update_slice_in_dim(
                summed, lax.dynamic_slice_in_dim(summed, row_start, BS, 1) + term_left, row_start, 1
            )
            summed = lax.dynamic_update_slice_in_dim(
                summed,
                lax.dynamic_slice_in_dim(summed, col_start, BS, 1) + term_right,
                col_start,
                1,
            )
            return summed

        summed = lax.fori_loop(0, active, visit, jnp.zeros(reach_dir.shape, jnp.float32))
        own_part = summed[:, :local_rows]
        next_part = summed[:, local_rows:]
        own_sum, next_sum = lax.psum((own_part, next_part), "pair")
        entering = passed_along(next_sum, "blk", 1)
        coupled = jnp.concatenate([own_sum[:, :BS] + entering, own_sum[:, BS:]], axis=1)
        applied = noise_var[None, :] * direction + coupled
        last_turn = iteration + 1 == ITERS
        curvature = lax.psum(jnp.sum(direction * applied, axis=1), "blk")
        step_size = norm_now / curvature
        solution = solution + step_size[:, None] * direction
        residual = residual - step_size[:, None] * applied
        if not last_turn:
            norm_next = lax.psum(jnp.sum(residual * residual, axis=1), "blk")
            direction = residual + (norm_next / norm_now)[:, None] * direction
            norm_now = norm_next
    return (solution, residual)


def solution(mesh):
    placed = (P(None, "blk"), P(), P(), P("blk"), P(None, "blk"), P(("blk", "pair"), None))
    return jax.shard_map(
        body,
        mesh=mesh,
        in_specs=placed,
        out_specs=(P(None, "blk"), P(None, "blk")),
        check_vma=False,
    )
```

profile of v0, /device:TPU:0, one launch (start us, length us, event | category | flops | bytes accessed | tf_op | source)
XLA Modules:
  0.0 444.4 jit_solution(433709531830236693)
XLA Ops:
  7.2 1.7 slice.46
  8.9 1.4 collective-permute-start.1
  10.3 1.8 broadcast_multiply_fusion.2
  12.9 1.3 collective-permute-start
  14.3 6.0 %all-gather = s32[4,4,2]{1,2,0:T(2,128)S(1)} all-gather(s32[1,4,2]{1,2,0:T(2,128)S(1)} %bitcast.62), channel_id=1, replica_groups=mesh['blk'=8,'pair'=4] {'pair'}, dimensions={0}, use_global_device_ids=true | all-gather | bytes 160 | tf_op jit(solution)/shard_map/all_gather | solution.py:82
  22.2 1.2 pad_maximum_fusion.1
  23.4 8.3 %collective-permute-done = f32[64,2048]{1,0:T(8,128)} collective-permute-done((f32[64,2048]{1,0:T(8,128)}, f32[64,2048]{1,0:T(8,128)}, u32[]{:S(2)}, u32[]{:S(2)}) %collective-permute-start) | collective-permute-done | bytes 524320 | tf_op jit(solution)/shard_map/ppermute | solution.py:17
  31.7 2.7 pad_maximum_fusion
  34.4 1.2 broadcast.245.clone
  35.6 110.4 %while.101 = (s32[]{:T(128)}, f32[32,10240]{1,0:T(8,128)}, s32[]{:T(128)}, s32[4]{0:T(128)S(1)}, f32[64,10240]{1,0:T(8,128)}, /*index=5*/s32[4]{0:T(128)S(1)}, f...) while((s32[]{:T(128)}, f32[32,10240]{1,0:T(8,128)}, ...), condition=%wide.region_13.14_spmd, body=%wide.region_6.13_spmd.sunk | while | flops 963511296 | bytes 12913883 | solution.py:126
  39.6 1.1 dynamic-slice_convert_fusion.6
  40.6 2.1 multiply_reduce_fusion.12
  42.8 44.5 %while.104 = (s32[]{:T(128)}, f32[32,2048]{1,0:T(8,128)S(1)}, f32[32,2048]{1,0:T(8,128)S(1)}, f32[2048]{0:T(1024)S(1)}, f32[2048]{0:T(1024)S(1)}, /*index=5*/f32...) while((s32[]{:T(128)}, f32[32,2048]{1,0:T(8,128)S(1)}, ...), condition=%wide.region_12.12_spmd.clone, body=%wide.region_8.11_spmd.clone.sunk | while | flops 962790400 | bytes 7882982 | solution.py:68
  42.8 9.6 %fusion.53 = (f32[2048]{0:T(1024)S(1)}, f32[512]{0:T(512)S(1)}, bf16[512,2048]{1,0:T(8,128)(2,1)S(1)}) fusion(f32[64,2048]{1,0:T(8,128)} %get-tuple-element.1379, f32[64,2048]{1,0:T(8,128)S(1)} %get-tuple-element.1377, s32[]{:T(128)S(6)} %select_n.115, f32[2048]{0:T(1024)S(1)} %get-tuple-element.1378, f32[512]{0:T(512)S(1)} %multiply_reduce_fusion.15, ...), kind=kOutput, calls=%fused_computation.68.clone.1 | convolution fusion | flops 828372480 | bytes 2773000 | tf_op jit(solution)/shard_map/while/body/while/body/eval_jaxpr/dot_general | solution.py:21
  53.9 9.6 %fusion.53 = (f32[2048]{0:T(1024)S(1)}, f32[512]{0:T(512)S(1)}, bf16[512,2048]{1,0:T(8,128)(2,1)S(1)}) fusion(f32[64,2048]{1,0:T(8,128)} %get-tuple-element.1379, f32[64,2048]{1,0:T(8,128)S(1)} %get-tuple-element.1377, s32[]{:T(128)S(6)} %select_n.115, f32[2048]{0:T(1024)S(1)} %get-tuple-element.1378, f32[512]{0:T(512)S(1)} %multiply_reduce_fusion.15, ...), kind=kOutput, calls=%fused_computation.68.clone.1 | convolution fusion | flops 828372480 | bytes 2773000 | tf_op jit(solution)/shard_map/while/body/while/body/eval_jaxpr/dot_general | solution.py:21
  65.1 9.6 %fusion.53 = (f32[2048]{0:T(1024)S(1)}, f32[512]{0:T(512)S(1)}, bf16[512,2048]{1,0:T(8,128)(2,1)S(1)}) fusion(f32[64,2048]{1,0:T(8,128)} %get-tuple-element.1379, f32[64,2048]{1,0:T(8,128)S(1)} %get-tuple-element.1377, s32[]{:T(128)S(6)} %select_n.115, f32[2048]{0:T(1024)S(1)} %get-tuple-element.1378, f32[512]{0:T(512)S(1)} %multiply_reduce_fusion.15, ...), kind=kOutput, calls=%fused_computation.68.clone.1 | convolution fusion | flops 828372480 | bytes 2773000 | tf_op jit(solution)/shard_map/while/body/while/body/eval_jaxpr/dot_general | solution.py:21
  76.2 9.6 %fusion.53 = (f32[2048]{0:T(1024)S(1)}, f32[512]{0:T(512)S(1)}, bf16[512,2048]{1,0:T(8,128)(2,1)S(1)}) fusion(f32[64,2048]{1,0:T(8,128)} %get-tuple-element.1379, f32[64,2048]{1,0:T(8,128)S(1)} %get-tuple-element.1377, s32[]{:T(128)S(6)} %select_n.115, f32[2048]{0:T(1024)S(1)} %get-tuple-element.1378, f32[512]{0:T(512)S(1)} %multiply_reduce_fusion.15, ...), kind=kOutput, calls=%fused_computation.68.clone.1 | convolution fusion | flops 828372480 | bytes 2773000 | tf_op jit(solution)/shard_map/while/body/while/body/eval_jaxpr/dot_general | solution.py:21
  87.2 1.8 add_dynamic-update-slice_fusion.8
  89.0 1.8 add_dynamic-update-slice_fusion.9
  95.9 2.1 multiply_reduce_fusion.12
  98.0 44.5 %while.104 = (s32[]{:T(128)}, f32[32,2048]{1,0:T(8,128)S(1)}, f32[32,2048]{1,0:T(8,128)S(1)}, f32[2048]{0:T(1024)S(1)}, f32[2048]{0:T(1024)S(1)}, /*index=5*/f32...) while((s32[]{:T(128)}, f32[32,2048]{1,0:T(8,128)S(1)}, ...), condition=%wide.region_12.12_spmd.clone, body=%wide.region_8.11_spmd.clone.sunk | while | flops 962790400 | bytes 7882982 | solution.py:68
  98.1 9.6 %fusion.53 = (f32[2048]{0:T(1024)S(1)}, f32[512]{0:T(512)S(1)}, bf16[512,2048]{1,0:T(8,128)(2,1)S(1)}) fusion(f32[64,2048]{1,0:T(8,128)} %get-tuple-element.1379, f32[64,2048]{1,0:T(8,128)S(1)} %get-tuple-element.1377, s32[]{:T(128)S(6)} %select_n.115, f32[2048]{0:T(1024)S(1)} %get-tuple-element.1378, f32[512]{0:T(512)S(1)} %multiply_reduce_fusion.15, ...), kind=kOutput, calls=%fused_computation.68.clone.1 | convolution fusion | flops 828372480 | bytes 2773000 | tf_op jit(solution)/shard_map/while/body/while/body/eval_jaxpr/dot_general | solution.py:21
  109.2 9.6 %fusion.53 = (f32[2048]{0:T(1024)S(1)}, f32[512]{0:T(512)S(1)}, bf16[512,2048]{1,0:T(8,128)(2,1)S(1)}) fusion(f32[64,2048]{1,0:T(8,128)} %get-tuple-element.1379, f32[64,2048]{1,0:T(8,128)S(1)} %get-tuple-element.1377, s32[]{:T(128)S(6)} %select_n.115, f32[2048]{0:T(1024)S(1)} %get-tuple-element.1378, f32[512]{0:T(512)S(1)} %multiply_reduce_fusion.15, ...), kind=kOutput, calls=%fused_computation.68.clone.1 | convolution fusion | flops 828372480 | bytes 2773000 | tf_op jit(solution)/shard_map/while/body/while/body/eval_jaxpr/dot_general | solution.py:21
  120.3 9.6 %fusion.53 = (f32[2048]{0:T(1024)S(1)}, f32[512]{0:T(512)S(1)}, bf16[512,2048]{1,0:T(8,128)(2,1)S(1)}) fusion(f32[64,2048]{1,0:T(8,128)} %get-tuple-element.1379, f32[64,2048]{1,0:T(8,128)S(1)} %get-tuple-element.1377, s32[]{:T(128)S(6)} %select_n.115, f32[2048]{0:T(1024)S(1)} %get-tuple-element.1378, f32[512]{0:T(512)S(1)} %multiply_reduce_fusion.15, ...), kind=kOutput, calls=%fused_computation.68.clone.1 | convolution fusion | flops 828372480 | bytes 2773000 | tf_op jit(solution)/shard_map/while/body/while/body/eval_jaxpr/dot_general | solution.py:21
  131.4 9.6 %fusion.53 = (f32[2048]{0:T(1024)S(1)}, f32[512]{0:T(512)S(1)}, bf16[512,2048]{1,0:T(8,128)(2,1)S(1)}) fusion(f32[64,2048]{1,0:T(8,128)} %get-tuple-element.1379, f32[64,2048]{1,0:T(8,128)S(1)} %get-tuple-element.1377, s32[]{:T(128)S(6)} %select_n.115, f32[2048]{0:T(1024)S(1)} %get-tuple-element.1378, f32[512]{0:T(512)S(1)} %multiply_reduce_fusion.15, ...), kind=kOutput, calls=%fused_computation.68.clone.1 | convolution fusion | flops 828372480 | bytes 2773000 | tf_op jit(solution)/shard_map/while/body/while/body/eval_jaxpr/dot_general | solution.py:21
  142.5 1.8 add_dynamic-update-slice_fusion.8
  144.3 1.8 add_dynamic-update-slice_fusion.9
  146.0 1.7 slice.49
  147.7 2.4 slice.47
  150.1 39.6 %all-reduce.8.cloned.1.call-done = (f32[32,8192]{1,0:T(8,128)}, f32[32,2048]{1,0:T(8,128)}) async-done(((f32[32,8192]{1,0:T(8,128)}, f32[32,2048]{1,0:T(8,128)}), (f32[32,8192]{1,0:T(8,128)}, f32[32,2048]{1,0:T(8,128)})) %all-reduce.8.cloned.1.call-update) | async-done | bytes 1310736 | tf_op jit(solution)/shard_map/psum | solution.py:129
  189.7 3.4 collective-permute-start.2
  193.1 1.2 slice.58
  194.3 4.6 %collective-permute-done.2 = f32[32,2048]{1,0:T(8,128)S(1)} collective-permute-done((f32[32,2048]{1,0:T(8,128)}, f32[32,2048]{1,0:T(8,128)S(1)}, u32[]{:S(2)}, u32[]{:S(2)}) %collective-permute-start.2) | collective-permute-done | bytes 262176 | tf_op jit(solution)/shard_map/ppermute | solution.py:17
  200.3 22.3 %all-reduce = (f32[32]{0:T(128)S(1)}, f32[32]{0:T(128)S(1)}) all-reduce(f32[32]{0:T(128)S(1)} %get-tuple-element.857, f32[32]{0:T(128)S(1)} %get-tuple-element.856), channel_id=1, replica_groups=mesh['blk'=8,'pair'=4] {'blk'}, use_global_device_ids=true, to_apply=%region_1.2 | all-reduce | flops 64 | bytes 512 | tf_op jit(solution)/shard_map/psum | solution.py:95
  223.0 17.1 %psum.60 = f32[32]{0:T(128)S(1)} all-reduce(f32[32]{0:T(128)S(1)} %multiply_reduce_fusion.5), channel_id=1, replica_groups=mesh['blk'=8,'pair'=4] {'blk'}, use_global_device_ids=true, to_apply=%region_19.20 | all-reduce | flops 32 | bytes 256 | tf_op jit(solution)/shard_map/psum | solution.py:139
  240.4 1.3 collective-permute-start.3
  241.7 7.4 %collective-permute-done.3 = f32[32,2048]{1,0:T(8,128)S(1)} collective-permute-done((f32[32,2048]{1,0:T(8,128)S(1)}, f32[32,2048]{1,0:T(8,128)S(1)}, u32[]{:S(2)}, u32[]{:S(2)}) %collective-permute-start.3) | collective-permute-done | bytes 262176 | tf_op jit(solution)/shard_map/ppermute | solution.py:17
  249.1 1.2 pad_maximum_fusion.2
  250.3 1.2 broadcast.245
  251.5 110.1 %while.103 = (s32[]{:T(128)}, f32[32,10240]{1,0:T(8,128)}, s32[]{:T(128)}, s32[4]{0:T(128)S(1)}, f32[64,10240]{1,0:T(8,128)}, /*index=5*/s32[4]{0:T(128)S(1)}, f...) while((s32[]{:T(128)}, f32[32,10240]{1,0:T(8,128)}, ...), condition=%wide.region_27.28_spmd, body=%wide.region_20.27_spmd.sunk | while | flops 963511296 | bytes 12913883 | solution.py:126
  256.3 2.1 multiply_reduce_fusion.13
  258.5 44.4 %while.105 = (s32[]{:T(128)}, f32[32,2048]{1,0:T(8,128)S(1)}, f32[32,2048]{1,0:T(8,128)S(1)}, f32[2048]{0:T(1024)S(1)}, f32[2048]{0:T(1024)S(1)}, /*index=5*/f32...) while((s32[]{:T(128)}, f32[32,2048]{1,0:T(8,128)S(1)}, ...), condition=%wide.region_26.26_spmd.clone, body=%wide.region_22.25_spmd.clone.sunk | while | flops 962790400 | bytes 7882982 | solution.py:68
  258.5 9.6 %fusion.46 = (f32[2048]{0:T(1024)S(1)}, f32[512]{0:T(512)S(1)}, bf16[512,2048]{1,0:T(8,128)(2,1)S(1)}) fusion(f32[64,2048]{1,0:T(8,128)} %get-tuple-element.1334, f32[64,2048]{1,0:T(8,128)S(1)} %get-tuple-element.1332, s32[]{:T(128)S(6)} %select_n.114, f32[2048]{0:T(1024)S(1)} %get-tuple-element.1333, f32[512]{0:T(512)S(1)} %multiply_reduce_fusion.14, ...), kind=kOutput, calls=%fused_computation.69.clone.1 | convolution fusion | flops 828372480 | bytes 2773000 | tf_op jit(solution)/shard_map/while/body/while/body/eval_jaxpr/dot_general | solution.py:21
  269.6 9.6 %fusion.46 = (f32[2048]{0:T(1024)S(1)}, f32[512]{0:T(512)S(1)}, bf16[512,2048]{1,0:T(8,128)(2,1)S(1)}) fusion(f32[64,2048]{1,0:T(8,128)} %get-tuple-element.1334, f32[64,2048]{1,0:T(8,128)S(1)} %get-tuple-element.1332, s32[]{:T(128)S(6)} %select_n.114, f32[2048]{0:T(1024)S(1)} %get-tuple-element.1333, f32[512]{0:T(512)S(1)} %multiply_reduce_fusion.14, ...), kind=kOutput, calls=%fused_computation.69.clone.1 | convolution fusion | flops 828372480 | bytes 2773000 | tf_op jit(solution)/shard_map/while/body/while/body/eval_jaxpr/dot_general | solution.py:21
  280.7 9.6 %fusion.46 = (f32[2048]{0:T(1024)S(1)}, f32[512]{0:T(512)S(1)}, bf16[512,2048]{1,0:T(8,128)(2,1)S(1)}) fusion(f32[64,2048]{1,0:T(8,128)} %get-tuple-element.1334, f32[64,2048]{1,0:T(8,128)S(1)} %get-tuple-element.1332, s32[]{:T(128)S(6)} %select_n.114, f32[2048]{0:T(1024)S(1)} %get-tuple-element.1333, f32[512]{0:T(512)S(1)} %multiply_reduce_fusion.14, ...), kind=kOutput, calls=%fused_computation.69.clone.1 | convolution fusion | flops 828372480 | bytes 2773000 | tf_op jit(solution)/shard_map/while/body/while/body/eval_jaxpr/dot_general | solution.py:21
  291.8 9.6 %fusion.46 = (f32[2048]{0:T(1024)S(1)}, f32[512]{0:T(512)S(1)}, bf16[512,2048]{1,0:T(8,128)(2,1)S(1)}) fusion(f32[64,2048]{1,0:T(8,128)} %get-tuple-element.1334, f32[64,2048]{1,0:T(8,128)S(1)} %get-tuple-element.1332, s32[]{:T(128)S(6)} %select_n.114, f32[2048]{0:T(1024)S(1)} %get-tuple-element.1333, f32[512]{0:T(512)S(1)} %multiply_reduce_fusion.14, ...), kind=kOutput, calls=%fused_computation.69.clone.1 | convolution fusion | flops 828372480 | bytes 2773000 | tf_op jit(solution)/shard_map/while/body/while/body/eval_jaxpr/dot_general | solution.py:21
  302.9 1.8 add_dynamic-update-slice_fusion.10
  304.7 1.8 add_dynamic-update-slice_fusion.11
  311.4 2.1 multiply_reduce_fusion.13
  313.5 44.5 %while.105 = (s32[]{:T(128)}, f32[32,2048]{1,0:T(8,128)S(1)}, f32[32,2048]{1,0:T(8,128)S(1)}, f32[2048]{0:T(1024)S(1)}, f32[2048]{0:T(1024)S(1)}, /*index=5*/f32...) while((s32[]{:T(128)}, f32[32,2048]{1,0:T(8,128)S(1)}, ...), condition=%wide.region_26.26_spmd.clone, body=%wide.region_22.25_spmd.clone.sunk | while | flops 962790400 | bytes 7882982 | solution.py:68
  313.6 9.6 %fusion.46 = (f32[2048]{0:T(1024)S(1)}, f32[512]{0:T(512)S(1)}, bf16[512,2048]{1,0:T(8,128)(2,1)S(1)}) fusion(f32[64,2048]{1,0:T(8,128)} %get-tuple-element.1334, f32[64,2048]{1,0:T(8,128)S(1)} %get-tuple-element.1332, s32[]{:T(128)S(6)} %select_n.114, f32[2048]{0:T(1024)S(1)} %get-tuple-element.1333, f32[512]{0:T(512)S(1)} %multiply_reduce_fusion.14, ...), kind=kOutput, calls=%fused_computation.69.clone.1 | convolution fusion | flops 828372480 | bytes 2773000 | tf_op jit(solution)/shard_map/while/body/while/body/eval_jaxpr/dot_general | solution.py:21
  324.7 9.6 %fusion.46 = (f32[2048]{0:T(1024)S(1)}, f32[512]{0:T(512)S(1)}, bf16[512,2048]{1,0:T(8,128)(2,1)S(1)}) fusion(f32[64,2048]{1,0:T(8,128)} %get-tuple-element.1334, f32[64,2048]{1,0:T(8,128)S(1)} %get-tuple-element.1332, s32[]{:T(128)S(6)} %select_n.114, f32[2048]{0:T(1024)S(1)} %get-tuple-element.1333, f32[512]{0:T(512)S(1)} %multiply_reduce_fusion.14, ...), kind=kOutput, calls=%fused_computation.69.clone.1 | convolution fusion | flops 828372480 | bytes 2773000 | tf_op jit(solution)/shard_map/while/body/while/body/eval_jaxpr/dot_general | solution.py:21
  335.8 9.6 %fusion.46 = (f32[2048]{0:T(1024)S(1)}, f32[512]{0:T(512)S(1)}, bf16[512,2048]{1,0:T(8,128)(2,1)S(1)}) fusion(f32[64,2048]{1,0:T(8,128)} %get-tuple-element.1334, f32[64,2048]{1,0:T(8,128)S(1)} %get-tuple-element.1332, s32[]{:T(128)S(6)} %select_n.114, f32[2048]{0:T(1024)S(1)} %get-tuple-element.1333, f32[512]{0:T(512)S(1)} %multiply_reduce_fusion.14, ...), kind=kOutput, calls=%fused_computation.69.clone.1 | convolution fusion | flops 828372480 | bytes 2773000 | tf_op jit(solution)/shard_map/while/body/while/body/eval_jaxpr/dot_general | solution.py:21
  346.9 9.6 %fusion.46 = (f32[2048]{0:T(1024)S(1)}, f32[512]{0:T(512)S(1)}, bf16[512,2048]{1,0:T(8,128)(2,1)S(1)}) fusion(f32[64,2048]{1,0:T(8,128)} %get-tuple-element.1334, f32[64,2048]{1,0:T(8,128)S(1)} %get-tuple-element.1332, s32[]{:T(128)S(6)} %select_n.114, f32[2048]{0:T(1024)S(1)} %get-tuple-element.1333, f32[512]{0:T(512)S(1)} %multiply_reduce_fusion.14, ...), kind=kOutput, calls=%fused_computation.69.clone.1 | convolution fusion | flops 828372480 | bytes 2773000 | tf_op jit(solution)/shard_map/while/body/while/body/eval_jaxpr/dot_general | solution.py:21
  358.0 1.8 add_dynamic-update-slice_fusion.10
  359.8 1.8 add_dynamic-update-slice_fusion.11
  361.6 1.7 slice.54
  363.2 2.4 slice.52
  365.6 36.2 %all-reduce.6.cloned.1.call-done = (f32[32,8192]{1,0:T(8,128)}, f32[32,2048]{1,0:T(8,128)}) async-done(((f32[32,8192]{1,0:T(8,128)}, f32[32,2048]{1,0:T(8,128)}), (f32[32,8192]{1,0:T(8,128)}, f32[32,2048]{1,0:T(8,128)})) %all-reduce.6.cloned.1.call-update) | async-done | bytes 1310736 | tf_op jit(solution)/shard_map/psum | solution.py:129
  401.9 3.4 collective-permute-start.4
  405.3 1.2 slice.61
  406.5 4.6 %collective-permute-done.4 = f32[32,2048]{1,0:T(8,128)S(1)} collective-permute-done((f32[32,2048]{1,0:T(8,128)}, f32[32,2048]{1,0:T(8,128)S(1)}, u32[]{:S(2)}, u32[]{:S(2)}) %collective-permute-start.4) | collective-permute-done | bytes 262176 | tf_op jit(solution)/shard_map/ppermute | solution.py:17
  412.4 22.3 %psum.63 = f32[32]{0:T(128)S(1)} all-reduce(f32[32]{0:T(128)S(1)} %multiply_reduce_fusion.4), channel_id=1, replica_groups=mesh['blk'=8,'pair'=4] {'blk'}, use_global_device_ids=true, to_apply=%region_31.32 | all-reduce | flops 32 | bytes 256 | tf_op jit(solution)/shard_map/psum | solution.py:134
  434.7 2.9 multiply_subtract_fusion
  (174 shorter events, 38.2 us)
Async XLA Ops:
  7.2 182.6 %all-reduce.8.cloned.1.call-start = ((), (), s32[]{:S(2)}) async-start(), calls=%async_computation.1 | async-start | bytes 2621440 | tf_op jit(solution)/shard_map/psum | solution.py:129
  8.9 5.4 %copy-start.14 = (s32[4,2]{0,1:T(2,128)S(1)}, s32[4,2]{0,1:T(2,128)}, u32[]{:S(2)}) copy-start(s32[4,2]{0,1:T(2,128)} %param.19) | copy-start | bytes 100
  8.9 13.3 %copy-start = (f32[32,8192]{1,0:T(8,128)S(1)}, f32[32,8192]{1,0:T(8,128)}, u32[]{:S(2)}) copy-start(f32[32,8192]{1,0:T(8,128)} %param.18) | copy-start | bytes 3145732
  8.9 13.3 %collective-permute-start.1 = (f32[32,2048]{1,0:T(8,128)}, f32[32,2048]{1,0:T(8,128)S(1)}, u32[]{:S(2)}, u32[]{:S(2)}) collective-permute-start(f32[32,2048]{1,0:T(8,128)} %slice.46), channel_id=1, source_target_pairs={{4,0},{8,4},{12,8},{16,12},{20,16},{24,20},{28,24},{5,1},{9,5},{13... | collective-permute-start | bytes 786440 | tf_op jit(solution)/shard_map/ppermute | solution.py:17
  12.9 18.8 %collective-permute-start = (f32[64,2048]{1,0:T(8,128)}, f32[64,2048]{1,0:T(8,128)}, u32[]{:S(2)}, u32[]{:S(2)}) collective-permute-start(f32[64,2048]{1,0:T(8,128)} %slice.56), channel_id=1, source_target_pairs={{4,0},{8,4},{12,8},{16,12},{20,16},{24,20},{28,24},{5,1},{9,5},{13... | collective-permute-start | bytes 1572872 | tf_op jit(solution)/shard_map/ppermute | solution.py:17
  147.7 52.2 %copy-start.1 = (f32[32,8192]{1,0:T(8,128)S(1)}, f32[32,8192]{1,0:T(8,128)}, u32[]{:S(2)}) copy-start(f32[32,8192]{1,0:T(8,128)} %param.18) | copy-start | bytes 3145732
  147.7 52.2 %copy-start.10 = (f32[8192]{0:T(1024)S(1)}, f32[8192]{0:T(1024)}, u32[]{:S(2)}) copy-start(f32[8192]{0:T(1024)} %param.17) | copy-start | bytes 98308
  150.1 251.8 %all-reduce.6.cloned.1.call-start = ((), (), s32[]{:S(2)}) async-start(), calls=%async_computation | async-start | bytes 2621440 | tf_op jit(solution)/shard_map/psum | solution.py:129
  189.7 9.2 %collective-permute-start.2 = (f32[32,2048]{1,0:T(8,128)}, f32[32,2048]{1,0:T(8,128)S(1)}, u32[]{:S(2)}, u32[]{:S(2)}) collective-permute-start(f32[32,2048]{1,0:T(8,128)} %get-tuple-element.941), channel_id=1, source_target_pairs={{0,4},{4,8},{8,12},{12,16},{16,20},{20,24},{24,28},{1,5},{5,9},{9,... | collective-permute-start | bytes 786440 | tf_op jit(solution)/shard_map/ppermute | solution.py:17
  194.3 46.1 %copy-start.3 = (f32[32,6144]{1,0:T(8,128)}, f32[32,6144]{1,0:T(8,128)S(1)}, u32[]{:S(2)}) copy-start(f32[32,6144]{1,0:T(8,128)S(1)} %slice.58) | copy-start | bytes 2359300
  199.9 40.4 %copy-start.8 = (f32[32,2048]{1,0:T(8,128)}, f32[32,2048]{1,0:T(8,128)S(1)}, u32[]{:S(2)}) copy-start(f32[32,2048]{1,0:T(8,128)S(1)} %slice_add_fusion.1) | copy-start | bytes 786436
  222.6 17.8 %copy-start.12 = (f32[32]{0:T(128)}, f32[32]{0:T(128)S(1)}, u32[]{:S(2)}) copy-start(f32[32]{0:T(128)S(1)} %div.40) | copy-start | bytes 388
  240.1 10.2 %copy-start.15 = (f32[32]{0:T(128)}, f32[32]{0:T(128)S(1)}, u32[]{:S(2)}) copy-start(f32[32]{0:T(128)S(1)} %psum.60) | copy-start | bytes 388
  240.4 11.1 %copy-start.5 = (f32[32,8192]{1,0:T(8,128)}, f32[32,8192]{1,0:T(8,128)S(1)}, u32[]{:S(2)}) copy-start(f32[32,8192]{1,0:T(8,128)S(1)} %multiply_add_fusion.1) | copy-start | bytes 3145732
  240.4 8.7 %collective-permute-start.3 = (f32[32,2048]{1,0:T(8,128)S(1)}, f32[32,2048]{1,0:T(8,128)S(1)}, u32[]{:S(2)}, u32[]{:S(2)}) collective-permute-start(f32[32,2048]{1,0:T(8,128)S(1)} %slice.59), channel_id=1, source_target_pairs={{4,0},{8,4},{12,8},{16,12},{20,16},{24,20},{28,24},{5,1},{9,5},{13... | collective-permute-start | bytes 786440 | tf_op jit(solution)/shard_map/ppermute | solution.py:17
  363.2 48.9 %copy-start.6 = (f32[32,8192]{1,0:T(8,128)S(1)}, f32[32,8192]{1,0:T(8,128)}, u32[]{:S(2)}) copy-start(f32[32,8192]{1,0:T(8,128)} %copy-done.5) | copy-start | bytes 3145732
  363.2 48.9 %copy-start.11 = (f32[8192]{0:T(1024)S(1)}, f32[8192]{0:T(1024)}, u32[]{:S(2)}) copy-start(f32[8192]{0:T(1024)} %param.17) | copy-start | bytes 98308
  365.6 69.0 %copy-start.16 = (f32[32]{0:T(128)S(1)}, f32[32]{0:T(128)}, u32[]{:S(2)}) copy-start(f32[32]{0:T(128)} %copy-done.15) | copy-start | bytes 388
  365.6 69.0 %copy-start.2 = (f32[32,8192]{1,0:T(8,128)S(1)}, f32[32,8192]{1,0:T(8,128)}, u32[]{:S(2)}) copy-start(f32[32,8192]{1,0:T(8,128)} %param.18) | copy-start | bytes 3145732
  365.6 69.1 %copy-start.4 = (f32[32,6144]{1,0:T(8,128)S(1)}, f32[32,6144]{1,0:T(8,128)}, u32[]{:S(2)}) copy-start(f32[32,6144]{1,0:T(8,128)} %copy-done.3) | copy-start | bytes 2359300
  365.6 69.1 %copy-start.9 = (f32[32,2048]{1,0:T(8,128)S(1)}, f32[32,2048]{1,0:T(8,128)}, u32[]{:S(2)}) copy-start(f32[32,2048]{1,0:T(8,128)} %copy-done.8) | copy-start | bytes 786436
  365.6 69.1 %copy-start.13 = (f32[32]{0:T(128)S(1)}, f32[32]{0:T(128)}, u32[]{:S(2)}) copy-start(f32[32]{0:T(128)} %copy-done.12) | copy-start | bytes 388
  401.9 9.2 %collective-permute-start.4 = (f32[32,2048]{1,0:T(8,128)}, f32[32,2048]{1,0:T(8,128)S(1)}, u32[]{:S(2)}, u32[]{:S(2)}) collective-permute-start(f32[32,2048]{1,0:T(8,128)} %get-tuple-element.939), channel_id=1, source_target_pairs={{0,4},{4,8},{8,12},{12,16},{16,20},{20,24},{24,28},{1,5},{5,9},{9,... | collective-permute-start | bytes 786440 | tf_op jit(solution)/shard_map/ppermute | solution.py:17
  406.4 5.6 %copy-start.7 = (f32[32,6144]{1,0:T(8,128)}, f32[32,6144]{1,0:T(8,128)S(1)}, u32[]{:S(2)}) copy-start(f32[32,6144]{1,0:T(8,128)S(1)} %slice.61) | copy-start | bytes 2359300
Sparse Core Ops, SparseCore 0:
  150.2 39.4 all-reduce.7
  365.8 36.0 all-reduce.5
where the time goes:
time: 447 us; the launch traced here: 444 us
  matrix products  172 us (38%)
  waiting for transfers between devices  101 us (23%)
  blocking collectives  67.7 us (15%)
  other arithmetic  37.6 us (8%)
  local copies, waits for them, and re-layouts  29.1 us (7%)
  between operations  14.9 us (3%)
  loops' own time  11 us (2%)
  starting transfers between devices  10.8 us (2%)
    dot_general x16, matrix products, kernel_tile(): lax.dot_general(left_scaled, right_scaled, (((0,), (0,)), ((), ())), prec...  153 us
    psum x2, waiting for transfers between devices, body(): own_sum, next_sum = lax.psum((own_part, next_part), 'pair')  75.8 us
    ppermute x5, waiting for transfers between devices, passed_along(): return lax.ppermute(block, axis, route)  25 us
    psum x1, blocking collectives, body(): curvature = lax.psum(jnp.sum(direction * applied, axis=1), 'blk')  22.3 us
    psum x1, blocking collectives, body(): norm_now = lax.psum(jnp.sum(residual * residual, axis=1), 'blk')  22.3 us
    psum x1, blocking collectives, body(): norm_next = lax.psum(jnp.sum(residual * residual, axis=1), 'blk')  17.1 us
    dynamic_update_slice x8, other arithmetic, visit(): lax.dynamic_update_slice_in_dim(summed, lax.dynamic_slice_in_dim(summed,...  14.3 us
    dot_general x16, matrix products, rows_visit(): lax.dot_general(right_half, rows_half, (((1,), (1,)), ((), ())), preferre...  11.6 us
  transfers between devices with their start and end apart: 7, of which 6 were waited for; matrix products, arithmetic and copies ran while one was open for 2% of the time, Pallas kernels for 0%

commit v1 on v0

--- a/solution.py
+++ b/solution.py
@@ -1,14 +1,619 @@
+import functools
+import math
+
 import jax
 import jax.numpy as jnp
 from jax import lax
+from jax.experimental import pallas as pl
+from jax.experimental.pallas import tpu as pltpu
 from jax.sharding import PartitionSpec as P
 
 BS = 2048
 ITERS = 2
 
-
+f32 = jnp.float32
+bf16 = jnp.bfloat16
 root_three = 1.7320508075688772
 taper_radius = 2.0
+BOTH = ("blk", "pair")
+NT = (((1,), (1,)), ((), ()))
+STRIP = 512
+VMEM_LIMIT = 48 << 20
+
+
+def parts_of(x):
+    high = x.astype(bf16)
+    rest = x - high.astype(f32)
+    middle = rest.astype(bf16)
+    low = (rest - middle.astype(f32)).astype(bf16)
+    return high, middle, low
+
+
+def left_parts(scaled, shrink):
+    turned = scaled.T
+    high, middle, _ = parts_of(turned)
+    norms = jnp.sum(turned * turned, axis=1, keepdims=True) * shrink
+    n_high, n_middle, n_low = (x.astype(f32) for x in parts_of(norms))
+    lane = lax.broadcasted_iota(jnp.int32, turned.shape, 1)
+    extra = jnp.where(
+        lane == 0,
+        n_high,
+        jnp.where(lane == 1, n_middle, jnp.where(lane == 2, n_low, jnp.where(lane < 6, 1.0, 0.0))),
+    ).astype(bf16)
+    return jnp.concatenate([high, high, middle, extra], axis=1)
+
+
+def right_parts(scaled, shrink):
+    high, middle, _ = parts_of(scaled * (-2.0 * shrink))
+    norms = jnp.sum(scaled * scaled, axis=0, keepdims=True) * shrink
+    n_high, n_middle, n_low = (x.astype(f32) for x in parts_of(norms))
+    row = lax.broadcasted_iota(jnp.int32, scaled.shape, 0)
+    extra = jnp.where(
+        row < 3,
+        1.0,
+        jnp.where(
+            row == 3,
+            n_high,
+            jnp.where(row == 4, n_middle, jnp.where(row == 5, n_low, 0.0)),
+        ),
+    ).astype(bf16)
+    return jnp.concatenate([high, middle, high, extra], axis=0)
+
+
+def kernel_values(q, amplitude):
+    q = jnp.maximum(q, 1e-30)
+    t = q * lax.rsqrt(q)
+    slope = taper_radius * root_three
+    u = jnp.maximum(1.0 - t, 0.0)
+    u2 = u * u
+    poly = amplitude + t * (amplitude * (4.0 + slope) + (amplitude * (4.0 * slope)) * t)
+    decay = jnp.exp2(t * (-slope * math.log2(math.e)))
+    return (poly * decay) * (u2 * u2)
+
+
+def dot(a, b):
+    return jnp.dot(a, b, preferred_element_type=f32)
+
+
+def dot_nt(a, b):
+    return lax.dot_general(a, b, NT, preferred_element_type=f32)
+
+
+def lanes_of(columns, rows):
+    lane = lax.broadcasted_iota(jnp.int32, (rows, 128), 1)
+    out = jnp.zeros((rows, 128), f32)
+    for at, column in enumerate(columns):
+        out = jnp.where(lane == at, column, out)
+    return out
+
+
+def row_dot(a, b):
+    return jnp.sum(a * b, axis=1, keepdims=True)
+
+
+def diagonal_kernel(place, signal, features, inv_scale, direction, tile, own, left, right, half):
+    step = pl.program_id(0)
+    strip = tile.shape[0]
+    size = tile.shape[1]
+    amplitude = signal[0]
+    shrink = 1.0 / (taper_radius * taper_radius * features.shape[0])
+
+    @pl.when(step == 0)
+    def _():
+        scaled = features[...] * inv_scale[...]
+        left[...] = left_parts(scaled, shrink)
+        right[...] = right_parts(scaled, shrink)
+        half[...] = direction[...].astype(bf16)
+        own[...] = jnp.zeros_like(own)
+
+    for at in range(size // strip):
+
+        @pl.when(step == at)
+        def _(at=at):
+            rows = slice(at * strip, (at + 1) * strip)
+            for col in range(at * strip, size, strip):
+                cols = slice(col, col + strip)
+                q = dot(left[rows, :], right[:, cols])
+                block = kernel_values(q, amplitude).astype(bf16)
+                tile[:, cols] = block
+                own[:, cols] += dot(half[:, rows], block)
+                if col > at * strip:
+                    own[:, rows] += dot_nt(half[:, cols], block)
+
+
+def crossing_kernel(
+    place,
+    signal,
+    features_left,
+    features_here,
+    features_sent,
+    inv_scale,
+    dir_left,
+    dir_here,
+    dir_sent,
+    noise,
+    diagonal,
+    tile,
+    row_sums,
+    col_sums,
+    own,
+    over,
+    dir_next,
+    sums,
+    left,
+    right,
+    half_left,
+    half_right,
+    col_part,
+):
+    step = pl.program_id(0)
+    steps = pl.num_programs(0)
+    strip = tile.shape[0]
+    size = tile.shape[1]
+    amplitude = signal[0]
+    shrink = 1.0 / (taper_radius * taper_radius * features_left.shape[0])
+    live = place[1] > 0
+    last = place[2] > 0
+
+    @pl.when(step == 0)
+    def _():
+        dir_next[...] = jnp.where(last, dir_sent[...], dir_here[...])
+        own[...] = jnp.zeros_like(own)
+        over[...] = jnp.zeros_like(over)
+        row_sums[...] = jnp.zeros_like(row_sums)
+        col_part[...] = jnp.zeros_like(col_part)
+
+        @pl.when(live)
+        def _():
+            scale = inv_scale[...]
+            left[...] = left_parts(features_left[...] * scale, shrink)
+            there = jnp.where(last, features_sent[...], features_here[...])
+            right[...] = right_parts(there * scale, shrink)
+            half_left[...] = dir_left[...].astype(bf16)
+            half_right[...] = dir_next[...].astype(bf16)
+
+    @pl.when(live)
+    def _():
+        rows = pl.ds(pl.multiple_of(step * strip, strip), strip)
+        left_rows = left[rows, :]
+        half_rows = half_left[:, rows]
+        toward = jnp.zeros((dir_left.shape[0], strip), f32)
+        row_part = jnp.zeros((strip, 128), f32)
+        for col in range(0, size, strip):
+            cols = slice(col, col + strip)
+            values = kernel_values(dot(left_rows, right[:, cols]), amplitude)
+            block = values.astype(bf16)
+            tile[:, cols] = block
+            toward = toward + dot_nt(half_right[:, cols], block)
+            over[:, cols] += dot(half_rows, block)
+            for lane in range(0, strip, 128):
+                row_part = row_part + values[:, lane : lane + 128]
+            col_part[:, cols] += jnp.sum(values.reshape(strip // 8, 8, strip), axis=0)
+        own[:, rows] = toward
+        row_sums[:, rows] = lax.dot_general(
+            jnp.ones((8, 128), f32),
+            row_part,
+            NT,
+            precision=lax.Precision.HIGHEST,
+            preferred_element_type=f32,
+        )
+
+    @pl.when(step == steps - 1)
+    def _():
+        here = dir_left[...]
+        ahead = dir_next[...]
+        columns = jnp.sum(col_part[...], axis=0, keepdims=True)
+        col_sums[...] = columns
+        mine = own[...] + diagonal[...] + (noise[...] + row_sums[0:1, :]) * here
+        theirs = over[...] + columns * ahead
+        own[...] = mine
+        over[...] = theirs
+        curvature = row_dot(here, mine) + row_dot(ahead, theirs)
+        sums[...] = lanes_of([row_dot(here, here), curvature], here.shape[0])
+
+
+def second_kernel(
+    place,
+    diagonal,
+    crossing,
+    row_sums,
+    col_sums,
+    dir_here,
+    dir_ahead,
+    image_here,
+    image_part,
+    image_over,
+    noise,
+    totals,
+    own,
+    over,
+    sums,
+    res_here,
+    res_ahead,
+    half_here,
+    half_ahead,
+):
+    step = pl.program_id(0)
+    steps = pl.num_programs(0)
+    strip = diagonal.shape[0]
+    size = diagonal.shape[1]
+    strips = size // strip
+    live = place[1] > 0
+
+    @pl.when(step == 0)
+    def _():
+        alpha = totals[:, 0:1] / totals[:, 1:2]
+        here = dir_here[...] - alpha * image_here[...]
+        ahead = dir_ahead[...] - alpha * (image_part[...] + image_over[...])
+        res_here[...] = here
+        res_ahead[...] = ahead
+        half_here[...] = here.astype(bf16)
+        half_ahead[...] = ahead.astype(bf16)
+        own[...] = jnp.zeros_like(own)
+        over[...] = jnp.zeros_like(over)
+
+    for at in range(strips):
+
+        @pl.when(step == at)
+        def _(at=at):
+            rows = slice(at * strip, (at + 1) * strip)
+            tail = slice(at * strip, size)
+            own[:, tail] += dot(half_here[:, rows], diagonal[:, tail])
+            if at + 1 < strips:
+                rest = slice((at + 1) * strip, size)
+                own[:, rows] += dot_nt(half_here[:, rest], diagonal[:, rest])
+
+    @pl.when((step >= strips) & live)
+    def _():
+        rows = pl.ds(pl.multiple_of((step - strips) * strip, strip), strip)
+        own[:, rows] += dot_nt(half_ahead[...], crossing[...])
+        over[...] += dot(half_here[:, rows], crossing[...])
+
+    @pl.when(step == steps - 1)
+    def _():
+        here = res_here[...]
+        ahead = res_ahead[...]
+        mine = own[...] + (noise[...] + row_sums[0:1, :]) * here
+        theirs = over[...] + col_sums[...] * ahead
+        own[...] = mine
+        over[...] = theirs
+        own_form = row_dot(here, mine) + row_dot(ahead, theirs)
+        cross_form = row_dot(dir_here[...], mine) + row_dot(dir_ahead[...], theirs)
+        other_form = row_dot(here, image_here[...])
+        sums[...] = lanes_of(
+            [row_dot(here, here), own_form, cross_form, other_form], here.shape[0]
+        )
+
+
+def final_kernel(place, right_side, first, second, *rest):
+    pieces = (len(rest) - 2) // 2
+    images, images2 = rest[:pieces], rest[pieces : 2 * pieces]
+    solved, residual = rest[2 * pieces :]
+    step = pl.program_id(0)
+    rho = first[:, 0:1]
+    curvature = first[:, 1:2]
+    alpha = rho / curvature
+    new = second[:, 0:1]
+    beta = new / rho
+    curvature2 = (
+        second[:, 1:2] + beta * (second[:, 2:3] + second[:, 3:4]) + beta * beta * curvature
+    )
+    alpha2 = new / curvature2
+    for at in range(pieces):
+
+        @pl.when(step == at)
+        def _(at=at):
+            begin = right_side[...]
+            image = images[at][...]
+            after = begin - alpha * image
+            direction = after + beta * begin
+            solved[...] = alpha * begin + alpha2 * direction
+            residual[...] = after - alpha2 * (images2[at][...] + beta * image)
+
+
+def params():
+    return pltpu.CompilerParams(vmem_limit_bytes=VMEM_LIMIT)
+
+
+def whole(shape):
+    return pl.BlockSpec(shape, lambda *_: (0,) * len(shape))
+
+
+def at_place(shape, shift=0, top=None):
+    if top is None:
+        return pl.BlockSpec(shape, lambda s, place: (0, place[0] + shift))
+    return pl.BlockSpec(shape, lambda s, place: (0, jnp.minimum(place[0] + shift, top)))
+
+
+def shaped(*shape, dtype=f32):
+    return jax.ShapeDtypeStruct(shape, dtype)
+
+
+SCALARS = pl.BlockSpec(memory_space=pltpu.SMEM)
+
+
+def diagonal_call(place, signal, features, inv_scale, right_side, size):
+    depth = features.shape[0]
+    probes = right_side.shape[0]
+    return pl.pallas_call(
+        diagonal_kernel,
+        grid_spec=pltpu.PrefetchScalarGridSpec(
+            num_scalar_prefetch=1,
+            grid=(size // STRIP,),
+            in_specs=[
+                SCALARS,
+                at_place((depth, size)),
+                whole((depth, 1)),
+                at_place((probes, size)),
+            ],
+            out_specs=[
+                pl.BlockSpec((STRIP, size), lambda s, place: (s, 0)),
+                whole((probes, size)),
+            ],
+            scratch_shapes=[
+                pltpu.VMEM((size, 4 * depth), bf16),
+                pltpu.VMEM((4 * depth, size), bf16),
+                pltpu.VMEM((probes, size), bf16),
+            ],
+        ),
+        out_shape=[shaped(size, size, dtype=bf16), shaped(probes, size)],
+        compiler_params=params(),
+    )(place, signal, features, inv_scale, right_side)
+
+
+def crossing_call(
+    place, signal, features, sent_features, inv_scale, right_side, sent_dir, noise, diagonal, size
+):
+    depth = features.shape[0]
+    probes = right_side.shape[0]
+    top = features.shape[1] // size - 1
+    block = whole((probes, size))
+    return pl.pallas_call(
+        crossing_kernel,
+        grid_spec=pltpu.PrefetchScalarGridSpec(
+            num_scalar_prefetch=1,
+            grid=(size // STRIP,),
+            in_specs=[
+                SCALARS,
+                at_place((depth, size)),
+                at_place((depth, size), 1, top),
+                whole((depth, size)),
+                whole((depth, 1)),
+                at_place((probes, size)),
+                at_place((probes, size), 1, top),
+                block,
+                at_place((1, size)),
+                block,
+            ],
+            out_specs=[
+                pl.BlockSpec((STRIP, size), lambda s, place: (s, 0)),
+                whole((8, size)),
+                whole((1, size)),
+                block,
+                block,
+                block,
+                whole((probes, 128)),
+            ],
+            scratch_shapes=[
+                pltpu.VMEM((size, 4 * depth), bf16),
+                pltpu.VMEM((4 * depth, size), bf16),
+                pltpu.VMEM((probes, size), bf16),
+                pltpu.VMEM((probes, size), bf16),
+                pltpu.VMEM((8, size), f32),
+            ],
+        ),
+        out_shape=[
+            shaped(size, size, dtype=bf16),
+            shaped(8, size),
+            shaped(1, size),
+            shaped(probes, size),
+            shaped(probes, size),
+            shaped(probes, size),
+            shaped(probes, 128),
+        ],
+        compiler_params=params(),
+    )(
+        place,
+        signal,
+        features,
+        features,
+        sent_features,
+        inv_scale,
+        right_side,
+        right_side,
+        sent_dir,
+        noise,
+        diagonal,
+    )
+
+
+def second_call(
+    place,
+    tile_here,
+    tile_over,
+    row_sums,
+    col_sums,
+    right_side,
+    dir_ahead,
+    image_here,
+    image_part,
+    image_over,
+    noise,
+    totals,
+):
+    size = tile_here.shape[0]
+    probes = right_side.shape[0]
+    strips = size // STRIP
+    block = whole((probes, size))
+    return pl.pallas_call(
+        second_kernel,
+        grid_spec=pltpu.PrefetchScalarGridSpec(
+            num_scalar_prefetch=1,
+            grid=(2 * strips,),
+            in_specs=[
+                pl.BlockSpec((STRIP, size), lambda s, place: (jnp.minimum(s, strips - 1), 0)),
+                pl.BlockSpec((STRIP, size), lambda s, place: (jnp.maximum(s - strips, 0), 0)),
+                whole((8, size)),
+                whole((1, size)),
+                at_place((probes, size)),
+                block,
+                block,
+                block,
+                block,
+                at_place((1, size)),
+                whole((probes, 128)),
+            ],
+            out_specs=[block, block, whole((probes, 128))],
+            scratch_shapes=[
+                pltpu.VMEM((probes, size), f32),
+                pltpu.VMEM((probes, size), f32),
+                pltpu.VMEM((probes, size), bf16),
+                pltpu.VMEM((probes, size), bf16),
+            ],
+        ),
+        out_shape=[shaped(probes, size), shaped(probes, size), shaped(probes, 128)],
+        compiler_params=params(),
+    )(
+        place,
+        tile_here,
+        tile_over,
+        row_sums,
+        col_sums,
+        right_side,
+        dir_ahead,
+        image_here,
+        image_part,
+        image_over,
+        noise,
+        totals,
+    )
+
+
+def final_call(place, right_side, first, second, images, images2, size):
+    probes = right_side.shape[0]
+    pieces = len(images)
+    turned = pl.BlockSpec((probes, size), lambda s, place: (0, place[0] ^ s))
+    piece = whole((probes, size))
+    return pl.pallas_call(
+        final_kernel,
+        grid_spec=pltpu.PrefetchScalarGridSpec(
+            num_scalar_prefetch=1,
+            grid=(pieces,),
+            in_specs=[turned, whole((probes, 128)), whole((probes, 128))] + [piece] * (2 * pieces),
+            out_specs=[turned, turned],
+        ),
+        out_shape=[shaped(*right_side.shape), shaped(*right_side.shape)],
+        compiler_params=params(),
+    )(place, right_side, first, second, *images, *images2)
+
+
+def moved(x, distance):
+    count = lax.axis_size(BOTH[0]) * lax.axis_size(BOTH[1])
+    route = [(i, i + distance) for i in range(count) if 0 <= i + distance < count]
+    return lax.ppermute(x, BOTH, route)
+
+
+def exchanged(x, axes, distance):
+    count = math.prod(lax.axis_size(a) for a in axes)
+    return lax.ppermute(x, axes, [(i, i ^ distance) for i in range(count)])
+
+
+def summed_over_all(x):
+    count = lax.axis_size(BOTH[0]) * lax.axis_size(BOTH[1])
+    distance = 1
+    while distance < count:
+        x = x + exchanged(x, BOTH, distance)
+        distance *= 2
+    return x
+
+
+def gathered(x):
+    members = lax.axis_size("pair")
+    pieces = {0: x}
+    distance = members // 2
+    while distance:
+        for at in list(pieces):
+            pieces[at ^ distance] = exchanged(pieces[at], ("pair",), distance)
+        distance //= 2
+    return [pieces[at] for at in range(members)]
+
+
+def sent_from_next_group(x, spread):
+    members = lax.axis_size("pair")
+    route = [
+        ((g + 1) * members + spread % members, g * members + members - 1)
+        for g in range(lax.axis_size("blk") - 1)
+    ]
+    return lax.ppermute(x, BOTH, route)
+
+
+def own_block_body(features, inv_scale, signal, noise_var, right_side, block_pairs):
+    members = lax.axis_size("pair")
+    size = features.shape[1] // members
+    half_depth = features.shape[0] // 2
+    mine = lax.axis_index("pair").astype(jnp.int32)
+    base = lax.axis_index("blk").astype(jnp.int32) * members
+
+    sent_dir = sent_from_next_group(right_side[:, :size], 2)
+    sent_features = jnp.concatenate(
+        [
+            sent_from_next_group(features[:half_depth, :size], 3),
+            sent_from_next_group(features[half_depth:, :size], 1),
+        ],
+        axis=0,
+    )
+    wanted = base + jnp.arange(members, dtype=jnp.int32)
+    listed = jnp.any(
+        (block_pairs[:, 0:1] == wanted[None, :]) & (block_pairs[:, 1:2] == wanted[None, :] + 1),
+        axis=0,
+    )
+    listed = jnp.where(listed, 1.0, 0.0).astype(f32)[None, :]
+    anywhere = sum(
+        lax.ppermute(listed, "pair", [(i, (i + k) % members) for i in range(members)])
+        for k in range(1, members)
+    )
+    anywhere = anywhere + listed
+    live = jnp.sum(jnp.where(jnp.arange(members) == mine, anywhere[0], 0.0)) > 0.0
+
+    scale = inv_scale[:, None]
+    noise = noise_var[None, :]
+    spot = jnp.stack([mine, mine, mine])
+    place = jnp.stack([mine, live.astype(jnp.int32), (mine == members - 1).astype(jnp.int32)])
+
+    tile_here, diagonal = diagonal_call(spot, signal, features, scale, right_side, size)
+    tile_over, row_sums, col_sums, own, over, dir_ahead, sums = crossing_call(
+        place,
+        signal,
+        features,
+        sent_features,
+        scale,
+        right_side,
+        sent_dir,
+        noise,
+        diagonal,
+        size,
+    )
+    image_part = moved(own, -1)
+    image = own + moved(over, 1)
+    first = summed_over_all(sums)
+    own2, over2, sums2 = second_call(
+        place,
+        tile_here,
+        tile_over,
+        row_sums,
+        col_sums,
+        right_side,
+        dir_ahead,
+        image,
+        image_part,
+        over,
+        noise,
+        first,
+    )
+    images = gathered(image)
+    images2 = gathered(own2 + moved(over2, 1))
+    second = summed_over_all(sums2)
+    return tuple(final_call(place, right_side, first, second, images, images2, size))
 
 
 def passed_along(block, axis, distance):
@@ -143,9 +748,18 @@
 
 
 def solution(mesh):
+    members = mesh.shape["pair"]
+    groups = mesh.shape["blk"]
+
+    def chosen(features, *rest):
+        one_block_each = features.shape[1] == members * BS and BS % STRIP == 0
+        powers = members & (members - 1) == 0 and groups & (groups - 1) == 0
+        each = own_block_body if one_block_each and powers else body
+        return each(features, *rest)
+
     placed = (P(None, "blk"), P(), P(), P("blk"), P(None, "blk"), P(("blk", "pair"), None))
     return jax.shard_map(
-        body,
+        chosen,
         mesh=mesh,
         in_specs=placed,
         out_specs=(P(None, "blk"), P(None, "blk")),

time: 447 us -> 137 us (0.31)
  matrix products: 172 us -> 0 us
  waiting for transfers between devices: 101 us -> 24.9 us
  blocking collectives: 67.7 us -> 0 us
  starting transfers between devices: 10.8 us -> 67.7 us
  other arithmetic: 37.6 us -> 0.98 us
  Pallas kernels: 0 us -> 30.1 us
  local copies, waits for them, and re-layouts: 29.1 us -> 10 us
  between operations: 14.9 us -> 2.15 us
  loops' own time: 11 us -> 0 us
    dot_general x48 -> x0, matrix products: 172 us -> none  [the longest x16 153 us: kernel_tile(): lax.dot_general(left_scaled, right_scaled, (((0,), (0,)), ((), ())), prec...]
    psum x2 -> x0, waiting for transfers between devices: 75.8 us -> none  [body(): own_sum, next_sum = lax.psum((own_part, next_part), 'pair')]
    psum x3 -> x0, blocking collectives: 61.6 us -> none  [the longest x1 22.3 us: body(): curvature = lax.psum(jnp.sum(direction * applied, axis=1), 'blk')]
    ppermute x5 -> x25, starting transfers between devices: 10.7 us -> 67.7 us  [the longest x16 55.2 us: exchanged(): return lax.ppermute(x, axes, [(i, i ^ distance) for i in range(count)])]
    pallas_call x0 -> x4, Pallas kernels: none -> 30.1 us  [the longest x1 11.9 us: diagonal_call(): pl.pallas_call(diagonal_kernel, grid_spec=pltpu.PrefetchScalarGridSpec(nu...]
    dynamic_update_slice x8 -> x0, other arithmetic: 14.3 us -> none  [visit(): lax.dynamic_update_slice_in_dim(summed, lax.dynamic_slice_in_dim(summed,...]
    another operation x6 -> x0, loops' own time: 11 us -> none  [the longest x2 10.6 us: body(): lax.fori_loop(0, active, visit, jnp.zeros(reach_dir.shape, jnp.float32))]
    slice x10 -> x2, local copies, waits for them, and re-layouts: 13 us -> 2.12 us  [the longest x1 1.15 us: own_block_body(): features[:half_depth, :size]]
  transfers between devices with their start and end apart: 7 -> 25, of which waited for: 6 -> 11; matrix products, arithmetic and copies ran while one was open for 2% -> 3% of each run, Pallas kernels for 0% -> 9%
where the time goes in v1:
time: 137 us; the launch traced here: 136 us
  starting transfers between devices  67.7 us (49%)
  Pallas kernels  30.1 us (22%)
  waiting for transfers between devices  24.9 us (18%)
  local copies, waits for them, and re-layouts  10 us (7%)
  between operations  2.15 us (2%)
    ppermute x16, starting transfers between devices, exchanged(): return lax.ppermute(x, axes, [(i, i ^ distance) for i in range(count)])  55.2 us
    ppermute x16, waiting for transfers between devices, exchanged(): return lax.ppermute(x, axes, [(i, i ^ distance) for i in range(count)])  24.9 us
    pallas_call x1, Pallas kernels, diagonal_call(): pl.pallas_call(diagonal_kernel, grid_spec=pltpu.PrefetchScalarGridSpec(nu...  11.9 us
    pallas_call x1, Pallas kernels, second_call(): pl.pallas_call(second_kernel, grid_spec=pltpu.PrefetchScalarGridSpec(num_...  10.2 us
    ppermute x3, starting transfers between devices, moved(): return lax.ppermute(x, BOTH, route)  6.44 us
    unnamed x12, local copies, waits for them, and re-layouts  6.38 us
    pallas_call x1, Pallas kernels, crossing_call(): pl.pallas_call(crossing_kernel, grid_spec=pltpu.PrefetchScalarGridSpec(nu...  4.33 us
    ppermute x3, starting transfers between devices, own_block_body(): lax.ppermute(listed, 'pair', [(i, (i + k) % members) for i in range(membe...  3.88 us
  transfers between devices with their start and end apart: 25, of which 11 were waited for; matrix products, arithmetic and copies ran while one was open for 3% of the time, Pallas kernels for 9%

profile of v1, /device:TPU:0, one launch (start us, length us, event | category | flops | bytes accessed | tf_op | source)
XLA Modules:
  0.0 135.9 jit_solution(17305411127485131213)
XLA Ops:
  0.6 0.0 copy-start.2
  0.6 1.2 fusion.1
  1.8 0.7 collective-permute-start.3
  2.5 0.7 collective-permute-start.4
  3.2 0.8 slice_bitcast_fusion.1
  3.9 0.1 and_reduce_fusion
  4.0 3.7 %collective-permute-start.2 = (f32[1,4]{1,0:T(1,128)S(1)}, f32[1,4]{1,0:T(1,128)S(1)}, u32[]{:S(2)}, u32[]{:S(2)}) collective-permute-start(f32[1,4]{1,0:T(1,128)S(1)} %select_bitcast_fusion), channel_id=1, source_target_pairs={{0,3},{1,0},{2,1},{3,2},{4,7},{5,4},{6,5},{7,6},{8,11},{9,8},{10,9... | collective-permute-start | bytes 56 | tf_op jit(solution)/shard_map/ppermute | solution.py:572
  7.7 0.0 collective-permute-start.1
  7.7 0.2 collective-permute-start
  8.6 0.7 copy.11.inv_scale
  9.3 1.0 slice.19
  10.3 0.0 copy-start
  10.3 1.2 copy-done
  11.5 1.6 %copy-done.3 = f32[64,8192]{1,0:T(8,128)S(1)} copy-done((f32[64,8192]{1,0:T(8,128)S(1)}, f32[64,8192]{1,0:T(8,128)}, u32[]{:S(2)}) %copy-start.3) | copy-done | bytes 2097176
  13.1 11.9 %shard_map.77 = (bf16[2048,2048]{1,0:T(8,128)(2,1)}, f32[32,2048]{1,0:T(8,128)S(1)}) custom-call(s32[3]{0:T(128)S(1)} %stack.30.place, f32[1]{0:T(128)S(6)} %copy.12.signal, f32[64,8192]{1,0:T(8,128)S(1)} %copy-done.3, f32[64,1]{1,0:T(8,128)S(1)} %copy.11.inv_scale, f32[32,8192]{1,0:T(8,128)S(1)} %copy-done), custom_call_target="tpu_custom_call" | custom-call | tf_op jit(solution)/shard_map/pallas_call | solution.py:338
  25.0 0.0 collective-permute-done.2
  25.0 0.8 collective-permute-start.5
  25.9 0.0 collective-permute-done.1
  25.9 0.6 fusion
  27.2 0.1 pad_add_fusion.place
  27.3 0.0 collective-permute-done.3
  27.3 0.0 collective-permute-done.4
  27.3 0.0 collective-permute-done.5.dir_sent
  27.3 0.0 copy-start.1
  27.3 1.2 copy-done.1
  28.5 1.6 %copy-done.4 = f32[64,8192]{1,0:T(8,128)S(1)} copy-done((f32[64,8192]{1,0:T(8,128)S(1)}, f32[64,8192]{1,0:T(8,128)}, u32[]{:S(2)}) %copy-start.4) | copy-done | bytes 2097176
  30.1 0.8 copy-done.5
  30.9 4.3 %shard_map.78 = (bf16[2048,2048]{1,0:T(8,128)(2,1)}, f32[8,2048]{1,0:T(8,128)S(1)}, f32[1,2048]{1,0:T(1,128)S(1)}, f32[32,2048]{1,0:T(8,128)S(1)}, f32[32,2048]{...) custom-call(s32[3]{0:T(128)S(1)} %pad_add_fusion.place, f32[1]{0:T(128)S(6)} %copy.12.signal, ...), custom_call_target="tpu_custom_call" | custom-call | tf_op jit(solution)/shard_map/pallas_call | solution.py:371
  35.2 3.8 %collective-permute-start.11 = (f32[32,2048]{1,0:T(8,128)S(1)}, f32[32,2048]{1,0:T(8,128)S(1)}, u32[]{:S(2)}, u32[]{:S(2)}) collective-permute-start(f32[32,2048]{1,0:T(8,128)S(1)} %get-tuple-element.22.image_over), channel_id=1, source_target_pairs={{0,1},{1,2},{2,3},{3,4},{4,5},{5,6},{6,7},{7,8},{8,9},{9,10},{10,1... | collective-permute-start | bytes 786440 | tf_op jit(solution)/shard_map/ppermute | solution.py:513
  39.1 1.3 collective-permute-start.12
  40.4 1.2 collective-permute-start.6
  41.6 1.0 collective-permute-done.6
  42.5 20.1 %collective-permute-start.7 = (f32[32,128]{1,0:T(8,128)S(1)}, f32[32,128]{1,0:T(8,128)S(1)}, u32[]{:S(2)}, u32[]{:S(2)}) collective-permute-start(f32[32,128]{1,0:T(8,128)S(1)} %add.72), channel_id=1, source_target_pairs={{0,2},{1,3},{2,0},{3,1},{4,6},{5,7},{6,4},{7,5},{8,10},{9,11},{10,... | collective-permute-start | bytes 49160 | tf_op jit(solution)/shard_map/ppermute | solution.py:518
  62.7 3.2 %collective-permute-done.7 = f32[32,128]{1,0:T(8,128)S(1)} collective-permute-done((f32[32,128]{1,0:T(8,128)S(1)}, f32[32,128]{1,0:T(8,128)S(1)}, u32[]{:S(2)}, u32[]{:S(2)}) %collective-permute-start.7) | collective-permute-done | bytes 16416 | tf_op jit(solution)/shard_map/ppermute | solution.py:518
  65.9 1.6 %collective-permute-start.8 = (f32[32,128]{1,0:T(8,128)S(1)}, f32[32,128]{1,0:T(8,128)S(1)}, u32[]{:S(2)}, u32[]{:S(2)}) collective-permute-start(f32[32,128]{1,0:T(8,128)S(1)} %add.73), channel_id=1, source_target_pairs={{0,4},{1,5},{2,6},{3,7},{4,0},{5,1},{6,2},{7,3},{8,12},{9,13},{10,... | collective-permute-start | bytes 49160 | tf_op jit(solution)/shard_map/ppermute | solution.py:518
  67.5 2.2 %collective-permute-done.8 = f32[32,128]{1,0:T(8,128)S(1)} collective-permute-done((f32[32,128]{1,0:T(8,128)S(1)}, f32[32,128]{1,0:T(8,128)S(1)}, u32[]{:S(2)}, u32[]{:S(2)}) %collective-permute-start.8) | collective-permute-done | bytes 16416 | tf_op jit(solution)/shard_map/ppermute | solution.py:518
  69.6 4.6 %collective-permute-start.9 = (f32[32,128]{1,0:T(8,128)S(1)}, f32[32,128]{1,0:T(8,128)S(1)}, u32[]{:S(2)}, u32[]{:S(2)}) collective-permute-start(f32[32,128]{1,0:T(8,128)S(1)} %add.74), channel_id=1, source_target_pairs={{0,8},{1,9},{2,10},{3,11},{4,12},{5,13},{6,14},{7,15},{8,0},{9,1},... | collective-permute-start | bytes 49160 | tf_op jit(solution)/shard_map/ppermute | solution.py:518
  74.3 1.7 %collective-permute-done.9 = f32[32,128]{1,0:T(8,128)S(1)} collective-permute-done((f32[32,128]{1,0:T(8,128)S(1)}, f32[32,128]{1,0:T(8,128)S(1)}, u32[]{:S(2)}, u32[]{:S(2)}) %collective-permute-start.9) | collective-permute-done | bytes 16416 | tf_op jit(solution)/shard_map/ppermute | solution.py:518
  76.0 5.1 %collective-permute-start.10 = (f32[32,128]{1,0:T(8,128)S(1)}, f32[32,128]{1,0:T(8,128)S(1)}, u32[]{:S(2)}, u32[]{:S(2)}) collective-permute-start(f32[32,128]{1,0:T(8,128)S(1)} %add.75), channel_id=1, source_target_pairs={{0,16},{1,17},{2,18},{3,19},{4,20},{5,21},{6,22},{7,23},{8,24},{9,... | collective-permute-start | bytes 49160 | tf_op jit(solution)/shard_map/ppermute | solution.py:518
  81.1 1.7 %collective-permute-done.10 = f32[32,128]{1,0:T(8,128)S(1)} collective-permute-done((f32[32,128]{1,0:T(8,128)S(1)}, f32[32,128]{1,0:T(8,128)S(1)}, u32[]{:S(2)}, u32[]{:S(2)}) %collective-permute-start.10) | collective-permute-done | bytes 16416 | tf_op jit(solution)/shard_map/ppermute | solution.py:518
  82.9 0.0 collective-permute-done.12.image_part
  82.9 10.2 %shard_map.79 = (f32[32,2048]{1,0:T(8,128)S(1)}, f32[32,2048]{1,0:T(8,128)S(1)}, f32[32,128]{1,0:T(8,128)S(1)}) custom-call(s32[3]{0:T(128)S(1)} %pad_add_fusion.place, bf16[2048,2048]{1,0:T(8,128)(2,1)} %get-tuple-element.16.diagonal, bf16[2048,2048]{1,0:T(8,128)(2,1)} %get-tuple-element.17.crossing, f32[8,2048]{1,0:T(8,128)S(1)} %get-tuple-element.18.row_sums, ...), custom_call_target="tpu_custom_call" | custom-call | tf_op jit(solution)/shard_map/pallas_call | solution.py:448
  93.1 1.3 collective-permute-start.21
  94.4 3.0 %collective-permute-start.19 = (f32[32,2048]{1,0:T(8,128)S(1)}, f32[32,2048]{1,0:T(8,128)S(1)}, u32[]{:S(2)}, u32[]{:S(2)}) collective-permute-start(f32[32,2048]{1,0:T(8,128)S(1)} %add.77.image_here.rest_0_), channel_id=1, source_target_pairs={{0,2},{1,3},{2,0},{3,1},{4,6},{5,7},{6,4},{7,5},{8,10},{9,11},{10,... | collective-permute-start | bytes 786440 | tf_op jit(solution)/shard_map/ppermute | solution.py:518
  97.5 7.9 %collective-permute-start.23 = (f32[32,2048]{1,0:T(8,128)S(1)}, f32[32,2048]{1,0:T(8,128)S(1)}, u32[]{:S(2)}, u32[]{:S(2)}) collective-permute-start(f32[32,2048]{1,0:T(8,128)S(1)} %add.83.rest_4_), channel_id=1, source_target_pairs={{0,2},{1,3},{2,0},{3,1},{4,6},{5,7},{6,4},{7,5},{8,10},{9,11},{10,... | collective-permute-start | bytes 786440 | tf_op jit(solution)/shard_map/ppermute | solution.py:518
  105.4 0.0 collective-permute-start.18
  105.4 0.5 collective-permute-start.22
  105.9 0.0 collective-permute-done.19.rest_2_
  105.9 0.5 collective-permute-start.20
  106.4 5.5 %collective-permute-done.23.rest_6_ = f32[32,2048]{1,0:T(8,128)S(1)} collective-permute-done((f32[32,2048]{1,0:T(8,128)S(1)}, f32[32,2048]{1,0:T(8,128)S(1)}, u32[]{:S(2)}, u32[]{:S(2)}) %collective-permute-start.23) | collective-permute-done | bytes 262176 | tf_op jit(solution)/shard_map/ppermute | solution.py:518
  111.9 0.5 collective-permute-start.13
  112.4 1.0 collective-permute-done.13
  113.4 2.5 %collective-permute-start.14 = (f32[32,128]{1,0:T(8,128)S(1)}, f32[32,128]{1,0:T(8,128)S(1)}, u32[]{:S(2)}, u32[]{:S(2)}) collective-permute-start(f32[32,128]{1,0:T(8,128)S(1)} %add.78), channel_id=1, source_target_pairs={{0,2},{1,3},{2,0},{3,1},{4,6},{5,7},{6,4},{7,5},{8,10},{9,11},{10,... | collective-permute-start | bytes 49160 | tf_op jit(solution)/shard_map/ppermute | solution.py:518
  115.9 1.7 %collective-permute-done.14 = f32[32,128]{1,0:T(8,128)S(1)} collective-permute-done((f32[32,128]{1,0:T(8,128)S(1)}, f32[32,128]{1,0:T(8,128)S(1)}, u32[]{:S(2)}, u32[]{:S(2)}) %collective-permute-start.14) | collective-permute-done | bytes 16416 | tf_op jit(solution)/shard_map/ppermute | solution.py:518
  117.6 4.1 %collective-permute-start.15 = (f32[32,128]{1,0:T(8,128)S(1)}, f32[32,128]{1,0:T(8,128)S(1)}, u32[]{:S(2)}, u32[]{:S(2)}) collective-permute-start(f32[32,128]{1,0:T(8,128)S(1)} %add.79), channel_id=1, source_target_pairs={{0,4},{1,5},{2,6},{3,7},{4,0},{5,1},{6,2},{7,3},{8,12},{9,13},{10,... | collective-permute-start | bytes 49160 | tf_op jit(solution)/shard_map/ppermute | solution.py:518
  121.7 1.7 %collective-permute-done.15 = f32[32,128]{1,0:T(8,128)S(1)} collective-permute-done((f32[32,128]{1,0:T(8,128)S(1)}, f32[32,128]{1,0:T(8,128)S(1)}, u32[]{:S(2)}, u32[]{:S(2)}) %collective-permute-start.15) | collective-permute-done | bytes 16416 | tf_op jit(solution)/shard_map/ppermute | solution.py:518
  123.4 0.3 collective-permute-start.16
  123.7 3.4 %collective-permute-done.16 = f32[32,128]{1,0:T(8,128)S(1)} collective-permute-done((f32[32,128]{1,0:T(8,128)S(1)}, f32[32,128]{1,0:T(8,128)S(1)}, u32[]{:S(2)}, u32[]{:S(2)}) %collective-permute-start.16) | collective-permute-done | bytes 16416 | tf_op jit(solution)/shard_map/ppermute | solution.py:518
  127.2 3.2 %collective-permute-start.17 = (f32[32,128]{1,0:T(8,128)S(1)}, f32[32,128]{1,0:T(8,128)S(1)}, u32[]{:S(2)}, u32[]{:S(2)}) collective-permute-start(f32[32,128]{1,0:T(8,128)S(1)} %add.81), channel_id=1, source_target_pairs={{0,16},{1,17},{2,18},{3,19},{4,20},{5,21},{6,22},{7,23},{8,24},{9,... | collective-permute-start | bytes 49160 | tf_op jit(solution)/shard_map/ppermute | solution.py:518
  130.4 1.7 %collective-permute-done.17 = f32[32,128]{1,0:T(8,128)S(1)} collective-permute-done((f32[32,128]{1,0:T(8,128)S(1)}, f32[32,128]{1,0:T(8,128)S(1)}, u32[]{:S(2)}, u32[]{:S(2)}) %collective-permute-start.17) | collective-permute-done | bytes 16416 | tf_op jit(solution)/shard_map/ppermute | solution.py:518
  132.1 0.0 collective-permute-done.18.rest_1_
  132.1 0.0 collective-permute-done.20.rest_3_
  132.2 0.0 collective-permute-done.24.rest_7_
  132.2 3.7 %shard_map.80 = (f32[32,8192]{1,0:T(8,128)}, f32[32,8192]{1,0:T(8,128)}) custom-call(s32[3]{0:T(128)S(1)} %pad_add_fusion.place, f32[32,8192]{1,0:T(8,128)S(1)} %copy-done.2, f32[32,128]{1,0:T(8,128)S(1)} %add.76.totals.first, f32[32,128]{1,0:T(8,128)S(1)} %add.82.second, f32[32,2048]{1,0:T(8,128)S(1)} %add.77.image_here.rest_0_, ...), custom_call_target="tpu_custom_call" | custom-call | tf_op jit(solution)/shard_map/pallas_call | solution.py:497
  (25 shorter events, 0.2 us)
Async XLA Ops:
  0.6 82.3 %copy-start.2 = (f32[32,8192]{1,0:T(8,128)S(1)}, f32[32,8192]{1,0:T(8,128)}, u32[]{:S(2)}) copy-start(f32[32,8192]{1,0:T(8,128)} %right_side.1) | copy-start | bytes 3145732
  1.8 25.5 %collective-permute-start.3 = (f32[32,2048]{1,0:T(8,128)S(1)}, f32[32,2048]{1,0:T(8,128)S(1)}, u32[]{:S(2)}, u32[]{:S(2)}) collective-permute-start(f32[32,2048]{1,0:T(8,128)S(1)} %get-tuple-element.26), channel_id=1, source_target_pairs={{7,3},{11,7},{15,11},{19,15},{23,19},{27,23},{31,27}} | collective-permute-start | bytes 786440 | tf_op jit(solution)/shard_map/ppermute | solution.py:547
  2.5 24.8 %collective-permute-start.4 = (f32[32,2048]{1,0:T(8,128)S(1)}, f32[32,2048]{1,0:T(8,128)S(1)}, u32[]{:S(2)}, u32[]{:S(2)}) collective-permute-start(f32[32,2048]{1,0:T(8,128)S(1)} %get-tuple-element.27), channel_id=1, source_target_pairs={{5,3},{9,7},{13,11},{17,15},{21,19},{25,23},{29,27}} | collective-permute-start | bytes 786440 | tf_op jit(solution)/shard_map/ppermute | solution.py:547
  4.0 21.0 %collective-permute-start.2 = (f32[1,4]{1,0:T(1,128)S(1)}, f32[1,4]{1,0:T(1,128)S(1)}, u32[]{:S(2)}, u32[]{:S(2)}) collective-permute-start(f32[1,4]{1,0:T(1,128)S(1)} %select_bitcast_fusion), channel_id=1, source_target_pairs={{0,3},{1,0},{2,1},{3,2},{4,7},{5,4},{6,5},{7,6},{8,11},{9,8},{10,9... | collective-permute-start | bytes 56 | tf_op jit(solution)/shard_map/ppermute | solution.py:572
  7.7 18.1 %collective-permute-start.1 = (f32[1,4]{1,0:T(1,128)S(1)}, f32[1,4]{1,0:T(1,128)S(1)}, u32[]{:S(2)}, u32[]{:S(2)}) collective-permute-start(f32[1,4]{1,0:T(1,128)S(1)} %select_bitcast_fusion), channel_id=1, source_target_pairs={{0,2},{1,3},{2,0},{3,1},{4,6},{5,7},{6,4},{7,5},{8,10},{9,11},{10,... | collective-permute-start | bytes 56 | tf_op jit(solution)/shard_map/ppermute | solution.py:572
  7.7 18.1 %collective-permute-start = (f32[1,4]{1,0:T(1,128)S(1)}, f32[1,4]{1,0:T(1,128)S(1)}, u32[]{:S(2)}, u32[]{:S(2)}) collective-permute-start(f32[1,4]{1,0:T(1,128)S(1)} %select_bitcast_fusion), channel_id=1, source_target_pairs={{0,1},{1,2},{2,3},{3,0},{4,5},{5,6},{6,7},{7,4},{8,9},{9,10},{10,1... | collective-permute-start | bytes 56 | tf_op jit(solution)/shard_map/ppermute | solution.py:572
  10.3 1.2 copy-start
  11.5 1.6 %copy-start.3 = (f32[64,8192]{1,0:T(8,128)S(1)}, f32[64,8192]{1,0:T(8,128)}, u32[]{:S(2)}) copy-start(f32[64,8192]{1,0:T(8,128)} %features_here.1) | copy-start | bytes 6291460
  25.0 2.3 %collective-permute-start.5 = (f32[32,2048]{1,0:T(8,128)S(1)}, f32[32,2048]{1,0:T(8,128)S(1)}, u32[]{:S(2)}, u32[]{:S(2)}) collective-permute-start(f32[32,2048]{1,0:T(8,128)S(1)} %slice.19), channel_id=1, source_target_pairs={{6,3},{10,7},{14,11},{18,15},{22,19},{26,23},{30,27}} | collective-permute-start | bytes 786440 | tf_op jit(solution)/shard_map/ppermute | solution.py:547
  27.3 1.2 copy-start.1
  28.5 1.6 %copy-start.4 = (f32[64,8192]{1,0:T(8,128)S(1)}, f32[64,8192]{1,0:T(8,128)}, u32[]{:S(2)}) copy-start(f32[64,8192]{1,0:T(8,128)} %features_here.1) | copy-start | bytes 6291460
  30.1 0.8 copy-start.5
  35.2 47.6 %collective-permute-start.11 = (f32[32,2048]{1,0:T(8,128)S(1)}, f32[32,2048]{1,0:T(8,128)S(1)}, u32[]{:S(2)}, u32[]{:S(2)}) collective-permute-start(f32[32,2048]{1,0:T(8,128)S(1)} %get-tuple-element.22.image_over), channel_id=1, source_target_pairs={{0,1},{1,2},{2,3},{3,4},{4,5},{5,6},{6,7},{7,8},{8,9},{9,10},{10,1... | collective-permute-start | bytes 786440 | tf_op jit(solution)/shard_map/ppermute | solution.py:513
  39.1 43.8 %collective-permute-start.12 = (f32[32,2048]{1,0:T(8,128)S(1)}, f32[32,2048]{1,0:T(8,128)S(1)}, u32[]{:S(2)}, u32[]{:S(2)}) collective-permute-start(f32[32,2048]{1,0:T(8,128)S(1)} %get-tuple-element.21), channel_id=1, source_target_pairs={{1,0},{2,1},{3,2},{4,3},{5,4},{6,5},{7,6},{8,7},{9,8},{10,9},{11,1... | collective-permute-start | bytes 786440 | tf_op jit(solution)/shard_map/ppermute | solution.py:513
  40.4 2.2 %collective-permute-start.6 = (f32[32,128]{1,0:T(8,128)S(1)}, f32[32,128]{1,0:T(8,128)S(1)}, u32[]{:S(2)}, u32[]{:S(2)}) collective-permute-start(f32[32,128]{1,0:T(8,128)S(1)} %get-tuple-element.15), channel_id=1, source_target_pairs={{0,1},{1,0},{2,3},{3,2},{4,5},{5,4},{6,7},{7,6},{8,9},{9,8},{10,11... | collective-permute-start | bytes 49160 | tf_op jit(solution)/shard_map/ppermute | solution.py:518
  42.5 23.4 %collective-permute-start.7 = (f32[32,128]{1,0:T(8,128)S(1)}, f32[32,128]{1,0:T(8,128)S(1)}, u32[]{:S(2)}, u32[]{:S(2)}) collective-permute-start(f32[32,128]{1,0:T(8,128)S(1)} %add.72), channel_id=1, source_target_pairs={{0,2},{1,3},{2,0},{3,1},{4,6},{5,7},{6,4},{7,5},{8,10},{9,11},{10,... | collective-permute-start | bytes 49160 | tf_op jit(solution)/shard_map/ppermute | solution.py:518
  65.9 3.7 %collective-permute-start.8 = (f32[32,128]{1,0:T(8,128)S(1)}, f32[32,128]{1,0:T(8,128)S(1)}, u32[]{:S(2)}, u32[]{:S(2)}) collective-permute-start(f32[32,128]{1,0:T(8,128)S(1)} %add.73), channel_id=1, source_target_pairs={{0,4},{1,5},{2,6},{3,7},{4,0},{5,1},{6,2},{7,3},{8,12},{9,13},{10,... | collective-permute-start | bytes 49160 | tf_op jit(solution)/shard_map/ppermute | solution.py:518
  69.6 6.3 %collective-permute-start.9 = (f32[32,128]{1,0:T(8,128)S(1)}, f32[32,128]{1,0:T(8,128)S(1)}, u32[]{:S(2)}, u32[]{:S(2)}) collective-permute-start(f32[32,128]{1,0:T(8,128)S(1)} %add.74), channel_id=1, source_target_pairs={{0,8},{1,9},{2,10},{3,11},{4,12},{5,13},{6,14},{7,15},{8,0},{9,1},... | collective-permute-start | bytes 49160 | tf_op jit(solution)/shard_map/ppermute | solution.py:518
  76.0 6.8 %collective-permute-start.10 = (f32[32,128]{1,0:T(8,128)S(1)}, f32[32,128]{1,0:T(8,128)S(1)}, u32[]{:S(2)}, u32[]{:S(2)}) collective-permute-start(f32[32,128]{1,0:T(8,128)S(1)} %add.75), channel_id=1, source_target_pairs={{0,16},{1,17},{2,18},{3,19},{4,20},{5,21},{6,22},{7,23},{8,24},{9,... | collective-permute-start | bytes 49160 | tf_op jit(solution)/shard_map/ppermute | solution.py:518
  93.1 4.4 %collective-permute-start.21 = (f32[32,2048]{1,0:T(8,128)S(1)}, f32[32,2048]{1,0:T(8,128)S(1)}, u32[]{:S(2)}, u32[]{:S(2)}) collective-permute-start(f32[32,2048]{1,0:T(8,128)S(1)} %get-tuple-element.25), channel_id=1, source_target_pairs={{0,1},{1,2},{2,3},{3,4},{4,5},{5,6},{6,7},{7,8},{8,9},{9,10},{10,1... | collective-permute-start | bytes 786440 | tf_op jit(solution)/shard_map/ppermute | solution.py:513
  94.4 11.5 %collective-permute-start.19 = (f32[32,2048]{1,0:T(8,128)S(1)}, f32[32,2048]{1,0:T(8,128)S(1)}, u32[]{:S(2)}, u32[]{:S(2)}) collective-permute-start(f32[32,2048]{1,0:T(8,128)S(1)} %add.77.image_here.rest_0_), channel_id=1, source_target_pairs={{0,2},{1,3},{2,0},{3,1},{4,6},{5,7},{6,4},{7,5},{8,10},{9,11},{10,... | collective-permute-start | bytes 786440 | tf_op jit(solution)/shard_map/ppermute | solution.py:518
  97.5 14.4 %collective-permute-start.23 = (f32[32,2048]{1,0:T(8,128)S(1)}, f32[32,2048]{1,0:T(8,128)S(1)}, u32[]{:S(2)}, u32[]{:S(2)}) collective-permute-start(f32[32,2048]{1,0:T(8,128)S(1)} %add.83.rest_4_), channel_id=1, source_target_pairs={{0,2},{1,3},{2,0},{3,1},{4,6},{5,7},{6,4},{7,5},{8,10},{9,11},{10,... | collective-permute-start | bytes 786440 | tf_op jit(solution)/shard_map/ppermute | solution.py:518
  105.4 26.7 %collective-permute-start.18 = (f32[32,2048]{1,0:T(8,128)S(1)}, f32[32,2048]{1,0:T(8,128)S(1)}, u32[]{:S(2)}, u32[]{:S(2)}) collective-permute-start(f32[32,2048]{1,0:T(8,128)S(1)} %add.77.image_here.rest_0_), channel_id=1, source_target_pairs={{0,1},{1,0},{2,3},{3,2},{4,5},{5,4},{6,7},{7,6},{8,9},{9,8},{10,11... | collective-permute-start | bytes 786440 | tf_op jit(solution)/shard_map/ppermute | solution.py:518
  105.4 26.7 %collective-permute-start.22 = (f32[32,2048]{1,0:T(8,128)S(1)}, f32[32,2048]{1,0:T(8,128)S(1)}, u32[]{:S(2)}, u32[]{:S(2)}) collective-permute-start(f32[32,2048]{1,0:T(8,128)S(1)} %add.83.rest_4_), channel_id=1, source_target_pairs={{0,1},{1,0},{2,3},{3,2},{4,5},{5,4},{6,7},{7,6},{8,9},{9,8},{10,11... | collective-permute-start | bytes 786440 | tf_op jit(solution)/shard_map/ppermute | solution.py:518
  105.9 26.2 %collective-permute-start.20 = (f32[32,2048]{1,0:T(8,128)S(1)}, f32[32,2048]{1,0:T(8,128)S(1)}, u32[]{:S(2)}, u32[]{:S(2)}) collective-permute-start(f32[32,2048]{1,0:T(8,128)S(1)} %collective-permute-done.19.rest_2_), channel_id=1, source_target_pairs={{0,1},{1,0},{2,3},{3,2},{4,5},{5,4},{6,7},{7,6},{8,9},{9,8},{10,11... | collective-permute-start | bytes 786440 | tf_op jit(solution)/shard_map/ppermute | solution.py:518
  111.9 20.3 %collective-permute-start.24 = (f32[32,2048]{1,0:T(8,128)S(1)}, f32[32,2048]{1,0:T(8,128)S(1)}, u32[]{:S(2)}, u32[]{:S(2)}) collective-permute-start(f32[32,2048]{1,0:T(8,128)S(1)} %collective-permute-done.23.rest_6_), channel_id=1, source_target_pairs={{0,1},{1,0},{2,3},{3,2},{4,5},{5,4},{6,7},{7,6},{8,9},{9,8},{10,11... | collective-permute-start | bytes 786440 | tf_op jit(solution)/shard_map/ppermute | solution.py:518
  111.9 1.6 %collective-permute-start.13 = (f32[32,128]{1,0:T(8,128)S(1)}, f32[32,128]{1,0:T(8,128)S(1)}, u32[]{:S(2)}, u32[]{:S(2)}) collective-permute-start(f32[32,128]{1,0:T(8,128)S(1)} %get-tuple-element.23), channel_id=1, source_target_pairs={{0,1},{1,0},{2,3},{3,2},{4,5},{5,4},{6,7},{7,6},{8,9},{9,8},{10,11... | collective-permute-start | bytes 49160 | tf_op jit(solution)/shard_map/ppermute | solution.py:518
  113.4 4.2 %collective-permute-start.14 = (f32[32,128]{1,0:T(8,128)S(1)}, f32[32,128]{1,0:T(8,128)S(1)}, u32[]{:S(2)}, u32[]{:S(2)}) collective-permute-start(f32[32,128]{1,0:T(8,128)S(1)} %add.78), channel_id=1, source_target_pairs={{0,2},{1,3},{2,0},{3,1},{4,6},{5,7},{6,4},{7,5},{8,10},{9,11},{10,... | collective-permute-start | bytes 49160 | tf_op jit(solution)/shard_map/ppermute | solution.py:518
  117.6 5.8 %collective-permute-start.15 = (f32[32,128]{1,0:T(8,128)S(1)}, f32[32,128]{1,0:T(8,128)S(1)}, u32[]{:S(2)}, u32[]{:S(2)}) collective-permute-start(f32[32,128]{1,0:T(8,128)S(1)} %add.79), channel_id=1, source_target_pairs={{0,4},{1,5},{2,6},{3,7},{4,0},{5,1},{6,2},{7,3},{8,12},{9,13},{10,... | collective-permute-start | bytes 49160 | tf_op jit(solution)/shard_map/ppermute | solution.py:518
  123.4 3.7 %collective-permute-start.16 = (f32[32,128]{1,0:T(8,128)S(1)}, f32[32,128]{1,0:T(8,128)S(1)}, u32[]{:S(2)}, u32[]{:S(2)}) collective-permute-start(f32[32,128]{1,0:T(8,128)S(1)} %add.80), channel_id=1, source_target_pairs={{0,8},{1,9},{2,10},{3,11},{4,12},{5,13},{6,14},{7,15},{8,0},{9,1},... | collective-permute-start | bytes 49160 | tf_op jit(solution)/shard_map/ppermute | solution.py:518
  127.2 4.9 %collective-permute-start.17 = (f32[32,128]{1,0:T(8,128)S(1)}, f32[32,128]{1,0:T(8,128)S(1)}, u32[]{:S(2)}, u32[]{:S(2)}) collective-permute-start(f32[32,128]{1,0:T(8,128)S(1)} %add.81), channel_id=1, source_target_pairs={{0,16},{1,17},{2,18},{3,19},{4,20},{5,21},{6,22},{7,23},{8,24},{9,... | collective-permute-start | bytes 49160 | tf_op jit(solution)/shard_map/ppermute | solution.py:518

commit v2 on v0

--- a/solution.py
+++ b/solution.py
@@ -1,14 +1,630 @@
+import functools
+import math
+
 import jax
 import jax.numpy as jnp
 from jax import lax
+from jax.experimental import pallas as pl
+from jax.experimental.pallas import tpu as pltpu
 from jax.sharding import PartitionSpec as P
 
 BS = 2048
 ITERS = 2
 
-
+f32 = jnp.float32
+bf16 = jnp.bfloat16
 root_three = 1.7320508075688772
 taper_radius = 2.0
+BOTH = ("blk", "pair")
+NT = (((1,), (1,)), ((), ()))
+CHUNK = 256
+
+RATE = taper_radius * root_three * math.log2(math.e)
+NEAR = math.log2(math.e)
+FAR = RATE / 4.0
+UNIT = NEAR * FAR * RATE**4
+
+
+def parts_of(x):
+    high = x.astype(bf16)
+    rest = x - high.astype(f32)
+    middle = rest.astype(bf16)
+    low = (rest - middle.astype(f32)).astype(bf16)
+    return high, middle, low
+
+
+def norm_parts(points, axis, first):
+    norms = jnp.sum(points * points, axis=axis, keepdims=True)
+    high, middle, low = (x.astype(f32) for x in parts_of(norms))
+    at = lax.broadcasted_iota(jnp.int32, points.shape, axis)
+    ones = jnp.where(at < 6, 1.0, 0.0)
+    placed = jnp.where(at == first + 2, low, ones)
+    placed = jnp.where(at == first + 1, middle, placed)
+    return jnp.where(at == first, high, placed).astype(bf16)
+
+
+def left_parts(points):
+    turned = points.T
+    high, middle, _ = parts_of(turned)
+    return jnp.concatenate([high, high, middle, norm_parts(turned, 1, 0)], axis=1)
+
+
+def right_parts(points):
+    high, middle, _ = parts_of(-2.0 * points)
+    return jnp.concatenate([high, middle, high, norm_parts(points, 0, 3)], axis=0)
+
+
+def points_of(features, inv_scale):
+    depth = features.shape[0]
+    scale = jnp.broadcast_to(inv_scale, (8, depth)).T[:, 0:1]
+    return features * scale * (RATE / (taper_radius * math.sqrt(depth)))
+
+
+def level_of(signal):
+    return jnp.log2(jnp.full((1, CHUNK), signal * (1.0 / UNIT), f32))
+
+
+def kernel_values(squared, level):
+    squared = jnp.maximum(squared, 1e-30)
+    s = squared * lax.rsqrt(squared)
+    decay = jnp.exp2(level - s)
+    u = jnp.maximum(RATE - s, 0.0)
+    u2 = u * u
+    return ((s + NEAR) * (s + FAR) * decay) * (u2 * u2)
+
+
+def dot(a, b):
+    return jnp.dot(a, b, preferred_element_type=f32)
+
+
+def dot_nt(a, b):
+    return lax.dot_general(a, b, NT, preferred_element_type=f32)
+
+
+def cut(at):
+    return slice(at * CHUNK, (at + 1) * CHUNK)
+
+
+def two_sum(a, b):
+    total = a + b
+    back = total - a
+    return total, (a - (total - back)) + (b - back)
+
+
+def two_product(a, b):
+    def halves(x):
+        big = x * 4097.0
+        high = big - (big - x)
+        return high, x - high
+
+    product = a * b
+    a_high, a_low = halves(a)
+    b_high, b_low = halves(b)
+    error = ((a_high * b_high - product) + a_high * b_low + a_low * b_high) + a_low * b_low
+    return product, error
+
+
+def plus(x, y):
+    total, error = two_sum(x[0], y[0])
+    return two_sum(total, error + (x[1] + y[1]))
+
+
+def times(x, factor):
+    product, error = two_product(x[0], factor)
+    return two_sum(product, error + x[1] * factor)
+
+
+def lane_tiles_sum(x):
+    high = x[:, 0:128]
+    low = jnp.zeros_like(high)
+    for at in range(128, x.shape[1], 128):
+        high, error = two_sum(high, x[:, at : at + 128])
+        low = low + error
+    return high, low
+
+
+def lanes_sum(high, low):
+    shift = 64
+    while shift:
+        high, error = two_sum(high, pltpu.roll(high, shift, 1))
+        low = low + pltpu.roll(low, shift, 1) + error
+        shift //= 2
+    return high, low
+
+
+def diagonal_kernel(
+    signal, features, inv_scale, right_side, tile, own, left, direction, raw, right, half, ahead, sems
+):
+    size = tile.shape[0]
+    mine = lax.axis_index("pair")
+    block = pl.ds(pl.multiple_of(mine * size, size), size)
+    get_features = pltpu.make_async_copy(features.at[:, block], raw, sems.at[0])
+    get_direction = pltpu.make_async_copy(right_side.at[:, block], direction, sems.at[1])
+    get_features.start()
+    get_direction.start()
+    level = level_of(signal[0])
+    get_features.wait()
+    points = points_of(raw[...], inv_scale[...])
+    left[...] = left_parts(points)
+    right[...] = right_parts(points)
+    get_direction.wait()
+    half[...] = direction[...].astype(bf16)
+    own[...] = jnp.zeros_like(own)
+
+    count = size // CHUNK
+    order = [(row, col) for row in range(count) for col in range(row, count)]
+
+    def argument(k):
+        row, col = order[k]
+        ahead[k % 2] = dot(left[cut(row), :], right[:, cut(col)])
+
+    def product(k):
+        row, col = order[k]
+        block = tile[cut(row), cut(col)]
+        own[:, cut(col)] += dot(half[:, cut(row)], block)
+        if col > row:
+            own[:, cut(row)] += dot_nt(half[:, cut(col)], block)
+
+    argument(0)
+    for k, (row, col) in enumerate(order):
+        if k + 1 < len(order):
+            argument(k + 1)
+        if k:
+            product(k - 1)
+        tile[cut(row), cut(col)] = kernel_values(ahead[k % 2], level).astype(bf16)
+    product(len(order) - 1)
+
+
+def crossing_kernel(
+    signal,
+    flags,
+    features,
+    sent_top,
+    sent_bottom,
+    inv_scale,
+    left,
+    right_side,
+    sent_dir,
+    direction,
+    noise,
+    diagonal,
+    tile,
+    row_sums,
+    col_sums,
+    own,
+    over,
+    next_dir,
+    raw,
+    right,
+    half,
+    half_next,
+    ahead,
+    col_part,
+    row_part,
+    sems,
+):
+    size = tile.shape[0]
+    members = lax.axis_size("pair")
+    mine = lax.axis_index("pair")
+    last = mine == members - 1
+    top = raw.shape[0] // 2
+
+    @pl.when(last)
+    def _():
+        copies = [
+            pltpu.make_async_copy(sent_top, raw.at[:top], sems.at[0]),
+            pltpu.make_async_copy(sent_bottom, raw.at[top:], sems.at[1]),
+            pltpu.make_async_copy(sent_dir, next_dir, sems.at[2]),
+        ]
+        for copy in copies:
+            copy.start()
+        for copy in copies:
+            copy.wait()
+
+    @pl.when(jnp.logical_not(last))
+    def _():
+        block = pl.ds(pl.multiple_of((mine + 1) * size, size), size)
+        copies = [
+            pltpu.make_async_copy(features.at[:, block], raw, sems.at[0]),
+            pltpu.make_async_copy(right_side.at[:, block], next_dir, sems.at[1]),
+        ]
+        for copy in copies:
+            copy.start()
+        for copy in copies:
+            copy.wait()
+
+    listed = flags[0, mine]
+    for k in range(1, members):
+        listed = listed + flags[k, mine]
+    live = listed > 0.0
+    own[...] = jnp.zeros_like(own)
+    over[...] = jnp.zeros_like(over)
+    row_sums[...] = jnp.zeros_like(row_sums)
+    col_sums[...] = jnp.zeros_like(col_sums)
+
+    @pl.when(live)
+    def _():
+        level = level_of(signal[0])
+        right[...] = right_parts(points_of(raw[...], inv_scale[...]))
+        half[...] = direction[...].astype(bf16)
+        half_next[...] = next_dir[...].astype(bf16)
+        col_part[...] = jnp.zeros_like(col_part)
+        row_part[...] = jnp.zeros_like(row_part)
+        count = size // CHUNK
+        order = [(row, col) for row in range(count) for col in range(count)]
+
+        def argument(k):
+            row, col = order[k]
+            ahead[k % 2] = dot(left[cut(row), :], right[:, cut(col)])
+
+        def product(k):
+            row, col = order[k]
+            block = tile[cut(row), cut(col)]
+            over[:, cut(col)] += dot(half[:, cut(row)], block)
+            own[:, cut(row)] += dot_nt(half_next[:, cut(col)], block)
+
+        argument(0)
+        for k, (row, col) in enumerate(order):
+            if k + 1 < len(order):
+                argument(k + 1)
+            if k:
+                product(k - 1)
+            values = kernel_values(ahead[k % 2], level)
+            tile[cut(row), cut(col)] = values.astype(bf16)
+            col_part[:, cut(col)] += jnp.sum(values.reshape(CHUNK // 8, 8, CHUNK), axis=0)
+            along = values[:, 0:128]
+            for lane in range(128, CHUNK, 128):
+                along = along + values[:, lane : lane + 128]
+            row_part[cut(row), :] += along
+        product(len(order) - 1)
+        row_sums[...] = lax.dot_general(
+            jnp.ones((8, 128), f32),
+            row_part[...],
+            NT,
+            precision=lax.Precision.HIGHEST,
+            preferred_element_type=f32,
+        )
+        col_sums[...] = jnp.sum(col_part[...], axis=0, keepdims=True)
+
+    own[...] += diagonal[...] + (noise[...] + row_sums[0:1, :]) * direction[...]
+    over[...] += col_sums[...] * next_dir[...]
+
+
+def both_parts(x):
+    high = x.astype(bf16)
+    return jnp.concatenate([high, (x - high.astype(f32)).astype(bf16)], axis=0)
+
+
+def folded(x):
+    half = x.shape[0] // 2
+    return x[:half] + x[half:]
+
+
+def second_crossing_kernel(flags, tile, row_sums, col_sums, image, part, over, own2, over2):
+    members = lax.axis_size("pair")
+    mine = lax.axis_index("pair")
+    listed = flags[0, mine]
+    for k in range(1, members):
+        listed = listed + flags[k, mine]
+    live = listed > 0.0
+
+    @pl.when(live)
+    def _():
+        here = image[...]
+        there = part[...] + over[...]
+        over2[...] = folded(dot(both_parts(here), tile[...])) + col_sums[...] * there
+        own2[...] = folded(dot_nt(both_parts(there), tile[...])) + row_sums[0:1, :] * here
+
+    @pl.when(jnp.logical_not(live))
+    def _():
+        over2[...] = jnp.zeros_like(over2)
+        own2[...] = jnp.zeros_like(own2)
+
+
+def second_diagonal_kernel(tile, noise, direction, next_dir, image, part, over, cross, over2, own2, sums, both):
+    size = tile.shape[0]
+    here = image[...]
+    both[...] = both_parts(here)
+    own2[...] = cross[...] + noise[...] * here
+    wide = CHUNK
+    for at in range(0, size, wide):
+        rows = slice(at, at + wide)
+        tail = slice(at, size)
+        rest = slice(at + wide, size)
+        own2[:, tail] += folded(dot(both[:, rows], tile[rows, tail]))
+        if at + wide < size:
+            own2[:, rows] += folded(dot_nt(both[:, rest], tile[rows, rest]))
+    begin = direction[...]
+    mine = own2[...]
+    theirs = over2[...]
+    there = part[...] + over[...]
+    squares = here * here
+    forms = [
+        begin * begin,
+        begin * here,
+        squares,
+        squares + begin * mine + next_dir[...] * theirs,
+        here * mine + there * theirs,
+    ]
+    pairs = [lane_tiles_sum(x) for x in forms]
+    probes = begin.shape[0]
+    high, low = lanes_sum(
+        jnp.concatenate([x for x, _ in pairs], axis=0), jnp.concatenate([x for _, x in pairs], axis=0)
+    )
+    lane = lax.broadcasted_iota(jnp.int32, (probes, 128), 1)
+    for part_at, values in enumerate((high, low)):
+        out = jnp.zeros((probes, 128), f32)
+        for k in range(len(forms)):
+            out = jnp.where(lane == k, values[k * probes : (k + 1) * probes], out)
+        sums[part_at * probes : (part_at + 1) * probes, :] = out
+
+
+def final_kernel(sums, right_side, *rest):
+    members = lax.axis_size("pair")
+    images, images2 = rest[:members], rest[members : 2 * members]
+    solution_out, residual_out, begins, solved, left_over, get_sems, put_sems = rest[2 * members :]
+    probes, size = images[0].shape
+    mine = lax.axis_index("pair")
+
+    def block(k):
+        return pl.ds(pl.multiple_of((mine ^ k) * size, size), size)
+
+    gets = [
+        pltpu.make_async_copy(right_side.at[:, block(k)], begins.at[k], get_sems.at[k])
+        for k in range(members)
+    ]
+    for get in gets:
+        get.start()
+
+    def total(k):
+        return sums[:probes, k : k + 1], sums[probes:, k : k + 1]
+
+    square, form, image_square, mixed, image_form = (total(k) for k in range(5))
+    alpha = square[0] / form[0]
+    new = plus(plus(square, times(form, -2.0 * alpha)), times(times(image_square, alpha), alpha))[0]
+    beta = new / square[0]
+    less = times(mixed, -alpha)
+    curvature = plus(plus(form, less), times(times(image_form, alpha), alpha))
+    curvature = plus(curvature, times(plus(times(form, 2.0), less), beta))
+    curvature = plus(curvature, times(times(form, beta), beta))
+    alpha2 = new / curvature[0]
+    puts = []
+    for k in range(members):
+        gets[k].wait()
+        begin = begins[k]
+        image = images[k][...]
+        after = begin - alpha * image
+        solved[k] = alpha * begin + alpha2 * (after + beta * begin)
+        left_over[k] = after - alpha2 * ((image - alpha * images2[k][...]) + beta * image)
+        for at, (source, target) in enumerate(((solved, solution_out), (left_over, residual_out))):
+            puts.append(
+                pltpu.make_async_copy(source.at[k], target.at[:, block(k)], put_sems.at[at, k])
+            )
+            puts[-1].start()
+    for put in puts:
+        put.wait()
+
+
+def params(mebibytes):
+    return pltpu.CompilerParams(vmem_limit_bytes=mebibytes << 20)
+
+
+def shaped(*shape):
+    return jax.ShapeDtypeStruct(shape, f32)
+
+
+VMEM = pl.BlockSpec(memory_space=pltpu.VMEM)
+SMEM = pl.BlockSpec(memory_space=pltpu.SMEM)
+HBM = pl.BlockSpec(memory_space=pltpu.HBM)
+ANY = pl.BlockSpec(memory_space=pl.ANY)
+
+
+def diagonal_call(signal, features, inv_scale, right_side, size):
+    depth = features.shape[0]
+    probes = right_side.shape[0]
+    return pl.pallas_call(
+        diagonal_kernel,
+        in_specs=[SMEM, HBM, VMEM, HBM],
+        out_specs=[VMEM] * 4,
+        out_shape=[
+            pltpu.VMEM((size, size), bf16),
+            shaped(probes, size),
+            pltpu.VMEM((size, 4 * depth), bf16),
+            pltpu.VMEM((probes, size), f32),
+        ],
+        scratch_shapes=[
+            pltpu.VMEM((depth, size), f32),
+            pltpu.VMEM((4 * depth, size), bf16),
+            pltpu.VMEM((probes, size), bf16),
+            pltpu.VMEM((2, CHUNK, CHUNK), f32),
+            pltpu.SemaphoreType.DMA((2,)),
+        ],
+        compiler_params=params(16),
+    )(signal, features, inv_scale, right_side)
+
+
+def crossing_call(
+    signal, flags, features, sent, inv_scale, left, right_side, sent_dir, direction, noise, diagonal
+):
+    depth = features.shape[0]
+    probes, size = direction.shape
+    return pl.pallas_call(
+        crossing_kernel,
+        in_specs=[SMEM, SMEM, HBM, ANY, ANY, VMEM, VMEM, HBM, ANY, VMEM, VMEM, VMEM],
+        out_specs=[VMEM] * 5 + [VMEM],
+        out_shape=[
+            pltpu.VMEM((size, size), bf16),
+            shaped(8, size),
+            shaped(1, size),
+            shaped(probes, size),
+            shaped(probes, size),
+            shaped(probes, size),
+        ],
+        scratch_shapes=[
+            pltpu.VMEM((depth, size), f32),
+            pltpu.VMEM((4 * depth, size), bf16),
+            pltpu.VMEM((probes, size), bf16),
+            pltpu.VMEM((probes, size), bf16),
+            pltpu.VMEM((2, CHUNK, CHUNK), f32),
+            pltpu.VMEM((8, size), f32),
+            pltpu.VMEM((size, 128), f32),
+            pltpu.SemaphoreType.DMA((3,)),
+        ],
+        compiler_params=params(16),
+    )(
+        signal,
+        flags,
+        features,
+        *sent,
+        inv_scale,
+        left,
+        right_side,
+        sent_dir,
+        direction,
+        noise,
+        diagonal,
+    )
+
+
+def second_crossing_call(flags, tile, row_sums, col_sums, image, part, over):
+    return pl.pallas_call(
+        second_crossing_kernel,
+        in_specs=[SMEM] + [VMEM] * 6,
+        out_specs=[VMEM] * 2,
+        out_shape=[shaped(*image.shape)] * 2,
+        compiler_params=params(16),
+    )(flags, tile, row_sums, col_sums, image, part, over)
+
+
+def second_diagonal_call(tile, noise, direction, next_dir, image, part, over, cross, over2):
+    probes, size = image.shape
+    return pl.pallas_call(
+        second_diagonal_kernel,
+        in_specs=[VMEM] * 9,
+        out_specs=[VMEM] * 2,
+        out_shape=[shaped(probes, size), shaped(2 * probes, 128)],
+        scratch_shapes=[pltpu.VMEM((2 * probes, size), bf16)],
+        compiler_params=params(16),
+    )(tile, noise, direction, next_dir, image, part, over, cross, over2)
+
+
+def final_call(sums, right_side, images, images2):
+    probes, size = images[0].shape
+    members = len(images)
+    return pl.pallas_call(
+        final_kernel,
+        in_specs=[VMEM, HBM] + [VMEM] * (2 * members),
+        out_specs=[HBM, HBM],
+        out_shape=[shaped(*right_side.shape)] * 2,
+        scratch_shapes=[
+            pltpu.VMEM((members, probes, size), f32),
+            pltpu.VMEM((members, probes, size), f32),
+            pltpu.VMEM((members, probes, size), f32),
+            pltpu.SemaphoreType.DMA((members,)),
+            pltpu.SemaphoreType.DMA((2, members)),
+        ],
+        compiler_params=params(16),
+    )(sums, right_side, *images, *images2)
+
+
+def moved(x, distance):
+    count = lax.axis_size(BOTH[0]) * lax.axis_size(BOTH[1])
+    route = [(i, i + distance) for i in range(count) if 0 <= i + distance < count]
+    return lax.ppermute(x, BOTH, route)
+
+
+def exchanged(x, distance):
+    count = lax.axis_size(BOTH[0]) * lax.axis_size(BOTH[1])
+    return lax.ppermute(x, BOTH, [(i, i ^ distance) for i in range(count)])
+
+
+def joined(x, distance):
+    other = exchanged(x, distance)
+    half = x.shape[0] // 2
+    high, error = two_sum(x[:half], other[:half])
+    return jnp.concatenate([high, (x[half:] + other[half:]) + error], axis=0)
+
+
+def sent_from_next_group(x, spread):
+    members = lax.axis_size("pair")
+    route = [
+        ((g + 1) * members + spread % members, g * members + members - 1)
+        for g in range(lax.axis_size("blk") - 1)
+    ]
+    return lax.ppermute(x, BOTH, route)
+
+
+def own_block_body(features, inv_scale, signal, noise_var, right_side, block_pairs):
+    members = lax.axis_size("pair")
+    groups = lax.axis_size("blk")
+    size = features.shape[1] // members
+    half_depth = features.shape[0] // 2
+    mine = lax.axis_index("pair").astype(jnp.int32)
+    base = lax.axis_index("blk").astype(jnp.int32) * members
+
+    sent = (
+        sent_from_next_group(features[:half_depth, :size], 3),
+        sent_from_next_group(features[half_depth:, :size], 1),
+    )
+    sent_dir = sent_from_next_group(right_side[:, :size], 2)
+    wanted = (base + jnp.arange(members, dtype=jnp.int32))[None, :]
+    found = (block_pairs[:, 0:1] == wanted) & (block_pairs[:, 1:2] == wanted + 1)
+    found = jnp.sum(jnp.where(found, 1.0, 0.0).astype(f32), axis=0, keepdims=True)
+    flags = jnp.concatenate(
+        [found]
+        + [
+            lax.ppermute(found, "pair", [(i, (i + k) % members) for i in range(members)])
+            for k in range(1, members)
+        ],
+        axis=0,
+    )
+    scale = inv_scale[None, :]
+    noise = lax.dynamic_slice_in_dim(noise_var, mine * size, size, 0)[None, :]
+
+    tile, diagonal, left, direction = diagonal_call(signal, features, scale, right_side, size)
+    cross_tile, row_sums, col_sums, own, over, next_dir = crossing_call(
+        signal,
+        flags,
+        features,
+        sent,
+        scale,
+        left,
+        right_side,
+        sent_dir,
+        direction,
+        noise,
+        diagonal,
+    )
+    part = moved(own, -1)
+    image = own + moved(over, 1)
+    images = {0: image}
+    distance = members // 2
+    if distance:
+        images[distance] = exchanged(image, distance)
+    cross, over2 = second_crossing_call(flags, cross_tile, row_sums, col_sums, image, part, over)
+    own2, sums = second_diagonal_call(
+        tile, noise, direction, next_dir, image, part, over, cross, over2
+    )
+    step = members
+    while step < members * groups:
+        sums = joined(sums, step)
+        step *= 2
+    images2 = {0: own2 + moved(over2, 1)}
+    while distance:
+        sums = joined(sums, distance)
+        for held in (images, images2):
+            for at in list(held):
+                if at ^ distance not in held:
+                    held[at ^ distance] = exchanged(held[at], distance)
+        distance //= 2
+    return tuple(
+        final_call(
+            sums,
+            right_side,
+            [images[k] for k in range(members)],
+            [images2[k] for k in range(members)],
+        )
+    )
 
 
 def passed_along(block, axis, distance):
@@ -143,9 +759,18 @@
 
 
 def solution(mesh):
+    members = mesh.shape["pair"]
+    groups = mesh.shape["blk"]
+
+    def chosen(features, *rest):
+        one_block_each = features.shape[1] == members * BS and BS % CHUNK == 0
+        powers = members & (members - 1) == 0 and groups & (groups - 1) == 0
+        each = own_block_body if one_block_each and powers else body
+        return each(features, *rest)
+
     placed = (P(None, "blk"), P(), P(), P("blk"), P(None, "blk"), P(("blk", "pair"), None))
     return jax.shard_map(
-        body,
+        chosen,
         mesh=mesh,
         in_specs=placed,
         out_specs=(P(None, "blk"), P(None, "blk")),

time: 447 us -> 92.5 us (0.21)
  matrix products: 172 us -> 0 us
  waiting for transfers between devices: 101 us -> 17.8 us
  blocking collectives: 67.7 us -> 0 us
  other arithmetic: 37.6 us -> 0.27 us
  Pallas kernels: 0 us -> 29.4 us
  starting transfers between devices: 10.8 us -> 34.8 us
  local copies, waits for them, and re-layouts: 29.1 us -> 6.97 us
  between operations: 14.9 us -> 1.69 us
  loops' own time: 11 us -> 0 us
    dot_general x48 -> x0, matrix products: 172 us -> none  [the longest x16 153 us: kernel_tile(): lax.dot_general(left_scaled, right_scaled, (((0,), (0,)), ((), ())), prec...]
    psum x2 -> x0, waiting for transfers between devices: 75.8 us -> none  [body(): own_sum, next_sum = lax.psum((own_part, next_part), 'pair')]
    psum x3 -> x0, blocking collectives: 61.6 us -> none  [the longest x1 22.3 us: body(): curvature = lax.psum(jnp.sum(direction * applied, axis=1), 'blk')]
    pallas_call x0 -> x5, Pallas kernels: none -> 29.4 us  [the longest x1 12.6 us: crossing_call(): pl.pallas_call(crossing_kernel, in_specs=[SMEM, SMEM, HBM, ANY, ANY, VMEM...]
    ppermute x5 -> x20, starting transfers between devices: 10.7 us -> 34.8 us  [the longest x11 23.9 us: exchanged(): return lax.ppermute(x, BOTH, [(i, i ^ distance) for i in range(count)])]
    dynamic_update_slice x8 -> x0, other arithmetic: 14.3 us -> none  [visit(): lax.dynamic_update_slice_in_dim(summed, lax.dynamic_slice_in_dim(summed,...]
    another operation x6 -> x0, loops' own time: 11 us -> none  [the longest x2 10.6 us: body(): lax.fori_loop(0, active, visit, jnp.zeros(reach_dir.shape, jnp.float32))]
    slice x10 -> x2, local copies, waits for them, and re-layouts: 13 us -> 2.04 us  [the longest x1 1.07 us: own_block_body(): features[half_depth:, :size]]
  transfers between devices with their start and end apart: 7 -> 20, of which waited for: 6 -> 8; matrix products, arithmetic and copies ran while one was open for 2% -> 3% of each run, Pallas kernels for 0% -> 7%
where the time goes in v2:
time: 92.5 us; the launch traced here: 90.9 us
  starting transfers between devices  34.8 us (38%)
  Pallas kernels  29.4 us (32%)
  waiting for transfers between devices  17.8 us (19%)
  local copies, waits for them, and re-layouts  6.97 us (8%)
  between operations  1.69 us (2%)
    ppermute x11, starting transfers between devices, exchanged(): return lax.ppermute(x, BOTH, [(i, i ^ distance) for i in range(count)])  23.9 us
    pallas_call x1, Pallas kernels, crossing_call(): pl.pallas_call(crossing_kernel, in_specs=[SMEM, SMEM, HBM, ANY, ANY, VMEM...  12.6 us
    ppermute x11, waiting for transfers between devices, exchanged(): return lax.ppermute(x, BOTH, [(i, i ^ distance) for i in range(count)])  11.2 us
    pallas_call x1, Pallas kernels, diagonal_call(): pl.pallas_call(diagonal_kernel, in_specs=[SMEM, HBM, VMEM, HBM], out_spec...  6.79 us
    pallas_call x1, Pallas kernels, second_crossing_call(): pl.pallas_call(second_crossing_kernel, in_specs=[SMEM] + [VMEM] * 6, out_...  4.89 us
    ppermute x3, starting transfers between devices, own_block_body(): lax.ppermute(found, 'pair', [(i, (i + k) % members) for i in range(member...  4.53 us
    ppermute x3, starting transfers between devices, moved(): return lax.ppermute(x, BOTH, route)  4.4 us
    ppermute x3, waiting for transfers between devices, moved(): return lax.ppermute(x, BOTH, route)  3.82 us
  transfers between devices with their start and end apart: 20, of which 8 were waited for; matrix products, arithmetic and copies ran while one was open for 3% of the time, Pallas kernels for 7%

profile of v2, /device:TPU:0, one launch (start us, length us, event | category | flops | bytes accessed | tf_op | source)
XLA Modules:
  0.0 90.9 jit_solution(11154287566827987405)
XLA Ops:
  0.6 1.0 %slice.55 = f32[32,2048]{1,0:T(8,128)S(1)} slice(f32[32,8192]{1,0:T(8,128)} %right_side.5), slice={[0:32], [0:2048]} | slice | bytes 524288 | tf_op jit(solution)/shard_map/slice | solution.py:569
  1.6 0.7 collective-permute-start.5
  2.3 1.1 %fusion.5 = (f32[32,2048]{1,0:T(8,128)S(1)}, f32[32,2048]{1,0:T(8,128)S(1)}) fusion(f32[64,8192]{1,0:T(8,128)} %features.3), kind=kLoop, calls=%fused_computation.26 | loop fusion | bytes 1048576 | tf_op jit(solution)/shard_map/slice | solution.py:567
  3.4 0.7 collective-permute-start.4
  4.0 0.7 collective-permute-start.3
  4.7 0.8 slice_bitcast_fusion.1
  5.5 0.1 select_reduce_fusion
  5.6 4.3 %collective-permute-start.2 = (f32[1,4]{1,0:T(1,128)S(1)}, f32[1,4]{1,0:T(1,128)S(1)}, u32[]{:S(2)}, u32[]{:S(2)}) collective-permute-start(f32[1,4]{1,0:T(1,128)S(1)} %bitcast.11), channel_id=1, source_target_pairs={{0,3},{1,0},{2,1},{3,2},{4,7},{5,4},{6,5},{7,6},{8,11},{9,8},{10,9... | collective-permute-start | bytes 56 | tf_op jit(solution)/shard_map/ppermute | solution.py:576
  9.9 0.0 collective-permute-start.1
  10.5 0.7 dynamic_slice.3
  11.2 0.0 copy-start
  11.2 1.2 %copy-done = f32[32,8192]{1,0:T(8,128)S(1)} copy-done((f32[32,8192]{1,0:T(8,128)S(1)}, f32[32,8192]{1,0:T(8,128)}, u32[]{:S(2)}) %copy-start) | copy-done | bytes 1048600
  12.5 0.0 copy-start.2
  12.5 1.6 %copy-done.2 = f32[64,8192]{1,0:T(8,128)S(1)} copy-done((f32[64,8192]{1,0:T(8,128)S(1)}, f32[64,8192]{1,0:T(8,128)}, u32[]{:S(2)}) %copy-start.2) | copy-done | bytes 2097176
  14.1 0.0 copy-start.3
  14.1 0.7 copy-done.3
  14.7 6.8 %shard_map.77 = (bf16[2048,2048]{1,0:T(8,128)(2,1)S(1)}, f32[32,2048]{1,0:T(8,128)S(1)}, bf16[2048,256]{1,0:T(8,128)(2,1)S(1)}, f32[32,2048]{1,0:T(8,128)S(1)}) custom-call(f32[1]{0:T(128)S(6)} %copy.8.signal, f32[64,8192]{1,0:T(8,128)S(1)} %copy-done.2, f32[1,64]{1,0:T(1,128)S(1)} %bitcast.9, f32[32,8192]{1,0:T(8,128)S(1)} %copy-done), custom_call_target="tpu_custom_call" | custom-call | tf_op jit(solution)/shard_map/pallas_call | solution.py:425
  21.5 0.0 collective-permute-done.2
  21.5 0.2 collective-permute-start
  21.8 0.0 collective-permute-done.1
  21.8 2.8 %collective-permute-done = f32[1,4]{1,0:T(1,128)S(1)} collective-permute-done((f32[1,4]{1,0:T(1,128)S(1)}, f32[1,4]{1,0:T(1,128)S(1)}, u32[]{:S(2)}, u32[]{:S(2)}) %collective-permute-start) | collective-permute-done | bytes 48 | tf_op jit(solution)/shard_map/ppermute | solution.py:576
  24.6 0.0 collective-permute-done.5.sent_dir
  24.6 0.0 collective-permute-done.4.sent_bottom
  24.6 0.0 collective-permute-done.3.sent_top
  24.6 12.6 %shard_map.78 = (bf16[2048,2048]{1,0:T(8,128)(2,1)S(1)}, f32[8,2048]{1,0:T(8,128)S(1)}, f32[1,2048]{1,0:T(1,128)S(1)}, f32[32,2048]{1,0:T(8,128)S(1)}, f32[32,2048]{1,0:T(8,128)S(1)}, /*index=5*/f32[32,2048]{1,0:T(8,128)S(1)}) custom-call(f32[1]{0:T(128)S(6)} %copy.8.signal, f32[4,4]{1,0:T(4,128)S(1)} %pad_maximum_fusion.5.flags, f32[64,8192]{1,0:T(8,128)S(1)} %copy-done.2, ...), custom_call_target="tpu_custom_call" | custom-call | tf_op jit(solution)/shard_map/pallas_call | solution.py:451
  37.1 1.8 %collective-permute-start.6 = (f32[32,2048]{1,0:T(8,128)S(1)}, f32[32,2048]{1,0:T(8,128)S(1)}, u32[]{:S(2)}, u32[]{:S(2)}) collective-permute-start(f32[32,2048]{1,0:T(8,128)S(1)} %get-tuple-element.22.over), channel_id=1, source_target_pairs={{0,1},{1,2},{2,3},{3,4},{4,5},{5,6},{6,7},{7,8},{8,9},{9,10},{10,1... | collective-permute-start | bytes 786440 | tf_op jit(solution)/shard_map/ppermute | solution.py:533
  39.0 1.3 %collective-permute-start.7 = (f32[32,2048]{1,0:T(8,128)S(1)}, f32[32,2048]{1,0:T(8,128)S(1)}, u32[]{:S(2)}, u32[]{:S(2)}) collective-permute-start(f32[32,2048]{1,0:T(8,128)S(1)} %get-tuple-element.21), channel_id=1, source_target_pairs={{1,0},{2,1},{3,2},{4,3},{5,4},{6,5},{7,6},{8,7},{9,8},{10,9},{11,1... | collective-permute-start | bytes 786440 | tf_op jit(solution)/shard_map/ppermute | solution.py:533
  40.3 0.0 collective-permute-done.6
  40.3 3.8 %collective-permute-done.7.part = f32[32,2048]{1,0:T(8,128)S(1)} collective-permute-done((f32[32,2048]{1,0:T(8,128)S(1)}, f32[32,2048]{1,0:T(8,128)S(1)}, u32[]{:S(2)}, u32[]{:S(2)}) %collective-permute-start.7) | collective-permute-done | bytes 262176 | tf_op jit(solution)/shard_map/ppermute | solution.py:533
  44.1 0.0 copy-start.1
  44.1 4.9 %shard_map.79 = (f32[32,2048]{1,0:T(8,128)S(1)}, f32[32,2048]{1,0:T(8,128)S(1)}) custom-call(f32[4,4]{1,0:T(4,128)S(1)} %pad_maximum_fusion.5.flags, bf16[2048,2048]{1,0:T(8,128)(2,1)S(1)} %get-tuple-element.23.tile, f32[8,2048]{1,0:T(8,128)S(1)} %get-tuple-element.24.row_sums, f32[1,2048]{1,0:T(1,128)S(1)} %get-tuple-element.25.col_sums, ...), custom_call_target="tpu_custom_call" | custom-call | tf_op jit(solution)/shard_map/pallas_call | solution.py:490
  49.0 2.7 %shard_map.80 = (f32[32,2048]{1,0:T(8,128)S(1)}, f32[64,128]{1,0:T(8,128)S(1)}) custom-call(bf16[2048,2048]{1,0:T(8,128)(2,1)S(1)} %get-tuple-element.16.tile, f32[1,2048]{1,0:T(1,128)S(1)} %bitcast.8, f32[32,2048]{1,0:T(8,128)S(1)} %get-tuple-element.17.direction, f32[32,2048]{1,0:T(8,128)S(1)} %get-tuple-element.20.next_dir, ...), custom_call_target="tpu_custom_call" | custom-call | tf_op jit(solution)/shard_map/pallas_call | solution.py:501
  51.8 6.6 %collective-permute-start.8 = (f32[64,128]{1,0:T(8,128)S(1)}, f32[64,128]{1,0:T(8,128)S(1)}, u32[]{:S(2)}, u32[]{:S(2)}) collective-permute-start(f32[64,128]{1,0:T(8,128)S(1)} %get-tuple-element.28), channel_id=1, source_target_pairs={{0,4},{1,5},{2,6},{3,7},{4,0},{5,1},{6,2},{7,3},{8,12},{9,13},{10,... | collective-permute-start | bytes 98312 | tf_op jit(solution)/shard_map/ppermute | solution.py:538
  58.4 1.9 %collective-permute-done.8 = f32[64,128]{1,0:T(8,128)S(1)} collective-permute-done((f32[64,128]{1,0:T(8,128)S(1)}, f32[64,128]{1,0:T(8,128)S(1)}, u32[]{:S(2)}, u32[]{:S(2)}) %collective-permute-start.8) | collective-permute-done | bytes 32800 | tf_op jit(solution)/shard_map/ppermute | solution.py:538
  60.3 4.2 %collective-permute-start.9 = (f32[64,128]{1,0:T(8,128)S(1)}, f32[64,128]{1,0:T(8,128)S(1)}, u32[]{:S(2)}, u32[]{:S(2)}) collective-permute-start(f32[64,128]{1,0:T(8,128)S(1)} %pad_maximum_fusion), channel_id=1, source_target_pairs={{0,8},{1,9},{2,10},{3,11},{4,12},{5,13},{6,14},{7,15},{8,0},{9,1},... | collective-permute-start | bytes 98312 | tf_op jit(solution)/shard_map/ppermute | solution.py:538
  64.5 1.9 %collective-permute-done.9 = f32[64,128]{1,0:T(8,128)S(1)} collective-permute-done((f32[64,128]{1,0:T(8,128)S(1)}, f32[64,128]{1,0:T(8,128)S(1)}, u32[]{:S(2)}, u32[]{:S(2)}) %collective-permute-start.9) | collective-permute-done | bytes 32800 | tf_op jit(solution)/shard_map/ppermute | solution.py:538
  66.4 3.1 %collective-permute-start.10 = (f32[64,128]{1,0:T(8,128)S(1)}, f32[64,128]{1,0:T(8,128)S(1)}, u32[]{:S(2)}, u32[]{:S(2)}) collective-permute-start(f32[64,128]{1,0:T(8,128)S(1)} %pad_maximum_fusion.1), channel_id=1, source_target_pairs={{0,16},{1,17},{2,18},{3,19},{4,20},{5,21},{6,22},{7,23},{8,24},{9,... | collective-permute-start | bytes 98312 | tf_op jit(solution)/shard_map/ppermute | solution.py:538
  69.5 1.3 %collective-permute-start.16 = (f32[32,2048]{1,0:T(8,128)S(1)}, f32[32,2048]{1,0:T(8,128)S(1)}, u32[]{:S(2)}, u32[]{:S(2)}) collective-permute-start(f32[32,2048]{1,0:T(8,128)S(1)} %get-tuple-element.27.over2), channel_id=1, source_target_pairs={{0,1},{1,2},{2,3},{3,4},{4,5},{5,6},{6,7},{7,8},{8,9},{9,10},{10,1... | collective-permute-start | bytes 786440 | tf_op jit(solution)/shard_map/ppermute | solution.py:533
  70.8 0.6 collective-permute-done.10
  71.4 0.5 collective-permute-start.11
  71.9 1.6 %collective-permute-start.14 = (f32[32,2048]{1,0:T(8,128)S(1)}, f32[32,2048]{1,0:T(8,128)S(1)}, u32[]{:S(2)}, u32[]{:S(2)}) collective-permute-start(f32[32,2048]{1,0:T(8,128)S(1)} %add.94.image.rest_0_), channel_id=1, source_target_pairs={{0,2},{1,3},{2,0},{3,1},{4,6},{5,7},{6,4},{7,5},{8,10},{9,11},{10,... | collective-permute-start | bytes 786440 | tf_op jit(solution)/shard_map/ppermute | solution.py:538
  73.5 0.0 collective-permute-done.16
  73.6 5.2 %collective-permute-start.18 = (f32[32,2048]{1,0:T(8,128)S(1)}, f32[32,2048]{1,0:T(8,128)S(1)}, u32[]{:S(2)}, u32[]{:S(2)}) collective-permute-start(f32[32,2048]{1,0:T(8,128)S(1)} %add.115.rest_4_), channel_id=1, source_target_pairs={{0,2},{1,3},{2,0},{3,1},{4,6},{5,7},{6,4},{7,5},{8,10},{9,11},{10,... | collective-permute-start | bytes 786440 | tf_op jit(solution)/shard_map/ppermute | solution.py:538
  78.8 0.0 collective-permute-done.11
  78.8 0.1 collective-permute-start.12
  78.9 0.5 collective-permute-start.13
  79.4 0.1 collective-permute-start.17
  79.5 1.6 %collective-permute-done.14.rest_2_ = f32[32,2048]{1,0:T(8,128)S(1)} collective-permute-done((f32[32,2048]{1,0:T(8,128)S(1)}, f32[32,2048]{1,0:T(8,128)S(1)}, u32[]{:S(2)}, u32[]{:S(2)}) %collective-permute-start.14) | collective-permute-done | bytes 262176 | tf_op jit(solution)/shard_map/ppermute | solution.py:538
  81.1 1.5 %collective-permute-start.15 = (f32[32,2048]{1,0:T(8,128)S(1)}, f32[32,2048]{1,0:T(8,128)S(1)}, u32[]{:S(2)}, u32[]{:S(2)}) collective-permute-start(f32[32,2048]{1,0:T(8,128)S(1)} %collective-permute-done.14.rest_2_), channel_id=1, source_target_pairs={{0,1},{1,0},{2,3},{3,2},{4,5},{5,4},{6,7},{7,6},{8,9},{9,8},{10,11... | collective-permute-start | bytes 786440 | tf_op jit(solution)/shard_map/ppermute | solution.py:538
  82.6 4.0 %collective-permute-done.18.rest_6_ = f32[32,2048]{1,0:T(8,128)S(1)} collective-permute-done((f32[32,2048]{1,0:T(8,128)S(1)}, f32[32,2048]{1,0:T(8,128)S(1)}, u32[]{:S(2)}, u32[]{:S(2)}) %collective-permute-start.18) | collective-permute-done | bytes 262176 | tf_op jit(solution)/shard_map/ppermute | solution.py:538
  86.7 0.5 collective-permute-start.19
  87.1 0.0 collective-permute-done.12
  87.2 0.0 collective-permute-done.13.rest_1_
  87.2 0.0 collective-permute-done.17.rest_5_
  87.2 0.0 collective-permute-done.15.rest_3_
  87.2 1.1 %collective-permute-done.19.rest_7_ = f32[32,2048]{1,0:T(8,128)S(1)} collective-permute-done((f32[32,2048]{1,0:T(8,128)S(1)}, f32[32,2048]{1,0:T(8,128)S(1)}, u32[]{:S(2)}, u32[]{:S(2)}) %collective-permute-start.19) | collective-permute-done | bytes 262176 | tf_op jit(solution)/shard_map/ppermute | solution.py:538
  88.3 0.0 copy-done.1
  88.3 2.4 %shard_map.81 = (f32[32,8192]{1,0:T(8,128)}, f32[32,8192]{1,0:T(8,128)}) custom-call(f32[64,128]{1,0:T(8,128)S(1)} %pad_maximum_fusion.4.sums, f32[32,8192]{1,0:T(8,128)S(1)} %copy-done.1, f32[32,2048]{1,0:T(8,128)S(1)} %add.94.image.rest_0_, f32[32,2048]{1,0:T(8,128)S(1)} %collective-permute-done.13.rest_1_, ...), custom_call_target="tpu_custom_call" | custom-call | tf_op jit(solution)/shard_map/pallas_call | solution.py:514
  (14 shorter events, 0.2 us)
Async XLA Ops:
  1.6 23.0 %collective-permute-start.5 = (f32[32,2048]{1,0:T(8,128)S(1)}, f32[32,2048]{1,0:T(8,128)S(1)}, u32[]{:S(2)}, u32[]{:S(2)}) collective-permute-start(f32[32,2048]{1,0:T(8,128)S(1)} %slice.55), channel_id=1, source_target_pairs={{6,3},{10,7},{14,11},{18,15},{22,19},{26,23},{30,27}} | collective-permute-start | bytes 786440 | tf_op jit(solution)/shard_map/ppermute | solution.py:554
  3.4 21.2 %collective-permute-start.4 = (f32[32,2048]{1,0:T(8,128)S(1)}, f32[32,2048]{1,0:T(8,128)S(1)}, u32[]{:S(2)}, u32[]{:S(2)}) collective-permute-start(f32[32,2048]{1,0:T(8,128)S(1)} %get-tuple-element.38), channel_id=1, source_target_pairs={{5,3},{9,7},{13,11},{17,15},{21,19},{25,23},{29,27}} | collective-permute-start | bytes 786440 | tf_op jit(solution)/shard_map/ppermute | solution.py:554
  4.0 20.5 %collective-permute-start.3 = (f32[32,2048]{1,0:T(8,128)S(1)}, f32[32,2048]{1,0:T(8,128)S(1)}, u32[]{:S(2)}, u32[]{:S(2)}) collective-permute-start(f32[32,2048]{1,0:T(8,128)S(1)} %get-tuple-element.39), channel_id=1, source_target_pairs={{7,3},{11,7},{15,11},{19,15},{23,19},{27,23},{31,27}} | collective-permute-start | bytes 786440 | tf_op jit(solution)/shard_map/ppermute | solution.py:554
  5.6 15.9 %collective-permute-start.2 = (f32[1,4]{1,0:T(1,128)S(1)}, f32[1,4]{1,0:T(1,128)S(1)}, u32[]{:S(2)}, u32[]{:S(2)}) collective-permute-start(f32[1,4]{1,0:T(1,128)S(1)} %bitcast.11), channel_id=1, source_target_pairs={{0,3},{1,0},{2,1},{3,2},{4,7},{5,4},{6,5},{7,6},{8,11},{9,8},{10,9... | collective-permute-start | bytes 56 | tf_op jit(solution)/shard_map/ppermute | solution.py:576
  9.9 11.9 %collective-permute-start.1 = (f32[1,4]{1,0:T(1,128)S(1)}, f32[1,4]{1,0:T(1,128)S(1)}, u32[]{:S(2)}, u32[]{:S(2)}) collective-permute-start(f32[1,4]{1,0:T(1,128)S(1)} %bitcast.12), channel_id=1, source_target_pairs={{0,2},{1,3},{2,0},{3,1},{4,6},{5,7},{6,4},{7,5},{8,10},{9,11},{10,... | collective-permute-start | bytes 56 | tf_op jit(solution)/shard_map/ppermute | solution.py:576
  11.2 1.2 %copy-start = (f32[32,8192]{1,0:T(8,128)S(1)}, f32[32,8192]{1,0:T(8,128)}, u32[]{:S(2)}) copy-start(f32[32,8192]{1,0:T(8,128)} %right_side.5) | copy-start | bytes 3145732
  12.5 1.6 %copy-start.2 = (f32[64,8192]{1,0:T(8,128)S(1)}, f32[64,8192]{1,0:T(8,128)}, u32[]{:S(2)}) copy-start(f32[64,8192]{1,0:T(8,128)} %features.3) | copy-start | bytes 6291460
  14.1 0.7 copy-start.3
  21.5 3.0 %collective-permute-start = (f32[1,4]{1,0:T(1,128)S(1)}, f32[1,4]{1,0:T(1,128)S(1)}, u32[]{:S(2)}, u32[]{:S(2)}) collective-permute-start(f32[1,4]{1,0:T(1,128)S(1)} %bitcast.13), channel_id=1, source_target_pairs={{0,1},{1,2},{2,3},{3,0},{4,5},{5,6},{6,7},{7,4},{8,9},{9,10},{10,1... | collective-permute-start | bytes 56 | tf_op jit(solution)/shard_map/ppermute | solution.py:576
  37.1 3.1 %collective-permute-start.6 = (f32[32,2048]{1,0:T(8,128)S(1)}, f32[32,2048]{1,0:T(8,128)S(1)}, u32[]{:S(2)}, u32[]{:S(2)}) collective-permute-start(f32[32,2048]{1,0:T(8,128)S(1)} %get-tuple-element.22.over), channel_id=1, source_target_pairs={{0,1},{1,2},{2,3},{3,4},{4,5},{5,6},{6,7},{7,8},{8,9},{9,10},{10,1... | collective-permute-start | bytes 786440 | tf_op jit(solution)/shard_map/ppermute | solution.py:533
  39.0 5.2 %collective-permute-start.7 = (f32[32,2048]{1,0:T(8,128)S(1)}, f32[32,2048]{1,0:T(8,128)S(1)}, u32[]{:S(2)}, u32[]{:S(2)}) collective-permute-start(f32[32,2048]{1,0:T(8,128)S(1)} %get-tuple-element.21), channel_id=1, source_target_pairs={{1,0},{2,1},{3,2},{4,3},{5,4},{6,5},{7,6},{8,7},{9,8},{10,9},{11,1... | collective-permute-start | bytes 786440 | tf_op jit(solution)/shard_map/ppermute | solution.py:533
  44.1 44.2 %copy-start.1 = (f32[32,8192]{1,0:T(8,128)S(1)}, f32[32,8192]{1,0:T(8,128)}, u32[]{:S(2)}) copy-start(f32[32,8192]{1,0:T(8,128)} %right_side.5) | copy-start | bytes 3145732
  51.8 8.5 %collective-permute-start.8 = (f32[64,128]{1,0:T(8,128)S(1)}, f32[64,128]{1,0:T(8,128)S(1)}, u32[]{:S(2)}, u32[]{:S(2)}) collective-permute-start(f32[64,128]{1,0:T(8,128)S(1)} %get-tuple-element.28), channel_id=1, source_target_pairs={{0,4},{1,5},{2,6},{3,7},{4,0},{5,1},{6,2},{7,3},{8,12},{9,13},{10,... | collective-permute-start | bytes 98312 | tf_op jit(solution)/shard_map/ppermute | solution.py:538
  60.3 6.1 %collective-permute-start.9 = (f32[64,128]{1,0:T(8,128)S(1)}, f32[64,128]{1,0:T(8,128)S(1)}, u32[]{:S(2)}, u32[]{:S(2)}) collective-permute-start(f32[64,128]{1,0:T(8,128)S(1)} %pad_maximum_fusion), channel_id=1, source_target_pairs={{0,8},{1,9},{2,10},{3,11},{4,12},{5,13},{6,14},{7,15},{8,0},{9,1},... | collective-permute-start | bytes 98312 | tf_op jit(solution)/shard_map/ppermute | solution.py:538
  66.4 5.0 %collective-permute-start.10 = (f32[64,128]{1,0:T(8,128)S(1)}, f32[64,128]{1,0:T(8,128)S(1)}, u32[]{:S(2)}, u32[]{:S(2)}) collective-permute-start(f32[64,128]{1,0:T(8,128)S(1)} %pad_maximum_fusion.1), channel_id=1, source_target_pairs={{0,16},{1,17},{2,18},{3,19},{4,20},{5,21},{6,22},{7,23},{8,24},{9,... | collective-permute-start | bytes 98312 | tf_op jit(solution)/shard_map/ppermute | solution.py:538
  69.5 4.0 %collective-permute-start.16 = (f32[32,2048]{1,0:T(8,128)S(1)}, f32[32,2048]{1,0:T(8,128)S(1)}, u32[]{:S(2)}, u32[]{:S(2)}) collective-permute-start(f32[32,2048]{1,0:T(8,128)S(1)} %get-tuple-element.27.over2), channel_id=1, source_target_pairs={{0,1},{1,2},{2,3},{3,4},{4,5},{5,6},{6,7},{7,8},{8,9},{9,10},{10,1... | collective-permute-start | bytes 786440 | tf_op jit(solution)/shard_map/ppermute | solution.py:533
  71.4 7.3 %collective-permute-start.11 = (f32[64,128]{1,0:T(8,128)S(1)}, f32[64,128]{1,0:T(8,128)S(1)}, u32[]{:S(2)}, u32[]{:S(2)}) collective-permute-start(f32[64,128]{1,0:T(8,128)S(1)} %pad_maximum_fusion.2), channel_id=1, source_target_pairs={{0,2},{1,3},{2,0},{3,1},{4,6},{5,7},{6,4},{7,5},{8,10},{9,11},{10,... | collective-permute-start | bytes 98312 | tf_op jit(solution)/shard_map/ppermute | solution.py:538
  71.9 9.2 %collective-permute-start.14 = (f32[32,2048]{1,0:T(8,128)S(1)}, f32[32,2048]{1,0:T(8,128)S(1)}, u32[]{:S(2)}, u32[]{:S(2)}) collective-permute-start(f32[32,2048]{1,0:T(8,128)S(1)} %add.94.image.rest_0_), channel_id=1, source_target_pairs={{0,2},{1,3},{2,0},{3,1},{4,6},{5,7},{6,4},{7,5},{8,10},{9,11},{10,... | collective-permute-start | bytes 786440 | tf_op jit(solution)/shard_map/ppermute | solution.py:538
  73.6 13.1 %collective-permute-start.18 = (f32[32,2048]{1,0:T(8,128)S(1)}, f32[32,2048]{1,0:T(8,128)S(1)}, u32[]{:S(2)}, u32[]{:S(2)}) collective-permute-start(f32[32,2048]{1,0:T(8,128)S(1)} %add.115.rest_4_), channel_id=1, source_target_pairs={{0,2},{1,3},{2,0},{3,1},{4,6},{5,7},{6,4},{7,5},{8,10},{9,11},{10,... | collective-permute-start | bytes 786440 | tf_op jit(solution)/shard_map/ppermute | solution.py:538
  78.8 8.3 %collective-permute-start.12 = (f32[64,128]{1,0:T(8,128)S(1)}, f32[64,128]{1,0:T(8,128)S(1)}, u32[]{:S(2)}, u32[]{:S(2)}) collective-permute-start(f32[64,128]{1,0:T(8,128)S(1)} %pad_maximum_fusion.3), channel_id=1, source_target_pairs={{0,1},{1,0},{2,3},{3,2},{4,5},{5,4},{6,7},{7,6},{8,9},{9,8},{10,11... | collective-permute-start | bytes 98312 | tf_op jit(solution)/shard_map/ppermute | solution.py:538
  78.9 8.3 %collective-permute-start.13 = (f32[32,2048]{1,0:T(8,128)S(1)}, f32[32,2048]{1,0:T(8,128)S(1)}, u32[]{:S(2)}, u32[]{:S(2)}) collective-permute-start(f32[32,2048]{1,0:T(8,128)S(1)} %add.94.image.rest_0_), channel_id=1, source_target_pairs={{0,1},{1,0},{2,3},{3,2},{4,5},{5,4},{6,7},{7,6},{8,9},{9,8},{10,11... | collective-permute-start | bytes 786440 | tf_op jit(solution)/shard_map/ppermute | solution.py:538
  79.4 7.8 %collective-permute-start.17 = (f32[32,2048]{1,0:T(8,128)S(1)}, f32[32,2048]{1,0:T(8,128)S(1)}, u32[]{:S(2)}, u32[]{:S(2)}) collective-permute-start(f32[32,2048]{1,0:T(8,128)S(1)} %add.115.rest_4_), channel_id=1, source_target_pairs={{0,1},{1,0},{2,3},{3,2},{4,5},{5,4},{6,7},{7,6},{8,9},{9,8},{10,11... | collective-permute-start | bytes 786440 | tf_op jit(solution)/shard_map/ppermute | solution.py:538
  81.1 6.1 %collective-permute-start.15 = (f32[32,2048]{1,0:T(8,128)S(1)}, f32[32,2048]{1,0:T(8,128)S(1)}, u32[]{:S(2)}, u32[]{:S(2)}) collective-permute-start(f32[32,2048]{1,0:T(8,128)S(1)} %collective-permute-done.14.rest_2_), channel_id=1, source_target_pairs={{0,1},{1,0},{2,3},{3,2},{4,5},{5,4},{6,7},{7,6},{8,9},{9,8},{10,11... | collective-permute-start | bytes 786440 | tf_op jit(solution)/shard_map/ppermute | solution.py:538
  86.7 1.7 %collective-permute-start.19 = (f32[32,2048]{1,0:T(8,128)S(1)}, f32[32,2048]{1,0:T(8,128)S(1)}, u32[]{:S(2)}, u32[]{:S(2)}) collective-permute-start(f32[32,2048]{1,0:T(8,128)S(1)} %collective-permute-done.18.rest_6_), channel_id=1, source_target_pairs={{0,1},{1,0},{2,3},{3,2},{4,5},{5,4},{6,7},{7,6},{8,9},{9,8},{10,11... | collective-permute-start | bytes 786440 | tf_op jit(solution)/shard_map/ppermute | solution.py:538

commit v3 on v2

--- a/solution.py
+++ b/solution.py
@@ -81,6 +81,20 @@
     return lax.dot_general(a, b, NT, preferred_element_type=f32)
 
 
+def own_block():
+    members = lax.axis_size("pair")
+    return lax.axis_index("pair") ^ ((members - 1) * (lax.axis_index("blk") & 1))
+
+
+def is_live(listings):
+    first = lax.axis_index("blk") * lax.axis_size("pair") + own_block()
+    found = jnp.zeros(listings[0][0:1, :].shape, f32)
+    for listing in listings:
+        match = (listing[0:1, :] == first) & (listing[1:2, :] == first + 1)
+        found = found + jnp.where(match, 1.0, 0.0)
+    return jnp.max(found) > 0.0
+
+
 def cut(at):
     return slice(at * CHUNK, (at + 1) * CHUNK)
 
@@ -132,22 +146,52 @@
     return high, low
 
 
-def diagonal_kernel(
-    signal, features, inv_scale, right_side, tile, own, left, direction, raw, right, half, ahead, sems
+def loading_kernel(
+    features,
+    right_side,
+    noise_var,
+    inv_scale,
+    send,
+    raw,
+    direction,
+    raw_next,
+    next_dir,
+    noise,
+    scale,
+    sems,
 ):
+    size = raw.shape[1]
+    depth = raw.shape[0]
+    mine = own_block()
+    after = jnp.minimum(mine + 1, lax.axis_size("pair") - 1)
+    here = pl.ds(pl.multiple_of(mine * size, size), size)
+    there = pl.ds(pl.multiple_of(after * size, size), size)
+    moves = [
+        (features.at[:, :size], send.at[:depth]),
+        (right_side.at[:, :size], send.at[depth:]),
+        (features.at[:, here], raw),
+        (right_side.at[:, here], direction),
+        (features.at[:, there], raw_next),
+        (right_side.at[:, there], next_dir),
+        (noise_var.at[:, here], noise),
+        (inv_scale, scale),
+    ]
+    copies = [
+        pltpu.make_async_copy(source, target, sems.at[k])
+        for k, (source, target) in enumerate(moves)
+    ]
+    for copy in copies:
+        copy.start()
+    for copy in copies:
+        copy.wait()
+
+
+def diagonal_kernel(signal, raw, scale, direction, tile, own, left, right, half, ahead):
     size = tile.shape[0]
-    mine = lax.axis_index("pair")
-    block = pl.ds(pl.multiple_of(mine * size, size), size)
-    get_features = pltpu.make_async_copy(features.at[:, block], raw, sems.at[0])
-    get_direction = pltpu.make_async_copy(right_side.at[:, block], direction, sems.at[1])
-    get_features.start()
-    get_direction.start()
     level = level_of(signal[0])
-    get_features.wait()
-    points = points_of(raw[...], inv_scale[...])
+    points = points_of(raw[...], scale[...])
     left[...] = left_parts(points)
     right[...] = right_parts(points)
-    get_direction.wait()
     half[...] = direction[...].astype(bf16)
     own[...] = jnp.zeros_like(own)
 
@@ -176,76 +220,30 @@
 
 
 def crossing_kernel(
+    members,
     signal,
-    flags,
-    features,
-    sent_top,
-    sent_bottom,
-    inv_scale,
-    left,
-    right_side,
-    sent_dir,
-    direction,
-    noise,
-    diagonal,
-    tile,
-    row_sums,
-    col_sums,
-    own,
-    over,
-    next_dir,
-    raw,
-    right,
-    half,
-    half_next,
-    ahead,
-    col_part,
-    row_part,
-    sems,
+    *refs,
 ):
+    listings, refs = refs[:members], refs[members:]
+    (raw_next, dir_next, sent, scale, left, direction, noise, diagonal) = refs[:8]
+    (tile, row_sums, own, over, next_dir, mark) = refs[8:14]
+    (right, half, half_next, ahead, col_part, row_part) = refs[14:]
     size = tile.shape[0]
-    members = lax.axis_size("pair")
-    mine = lax.axis_index("pair")
-    last = mine == members - 1
-    top = raw.shape[0] // 2
-
-    @pl.when(last)
-    def _():
-        copies = [
-            pltpu.make_async_copy(sent_top, raw.at[:top], sems.at[0]),
-            pltpu.make_async_copy(sent_bottom, raw.at[top:], sems.at[1]),
-            pltpu.make_async_copy(sent_dir, next_dir, sems.at[2]),
-        ]
-        for copy in copies:
-            copy.start()
-        for copy in copies:
-            copy.wait()
-
-    @pl.when(jnp.logical_not(last))
-    def _():
-        block = pl.ds(pl.multiple_of((mine + 1) * size, size), size)
-        copies = [
-            pltpu.make_async_copy(features.at[:, block], raw, sems.at[0]),
-            pltpu.make_async_copy(right_side.at[:, block], next_dir, sems.at[1]),
-        ]
-        for copy in copies:
-            copy.start()
-        for copy in copies:
-            copy.wait()
-
-    listed = flags[0, mine]
-    for k in range(1, members):
-        listed = listed + flags[k, mine]
-    live = listed > 0.0
+    probes = own.shape[0]
+    last = own_block() == members - 1
+    depth = raw_next.shape[0]
+    next_dir[...] = jnp.where(last, sent[depth:], dir_next[...])
+    live = is_live(listings)
+    mark[...] = jnp.where(live, jnp.ones(mark.shape, f32), jnp.zeros(mark.shape, f32))
     own[...] = jnp.zeros_like(own)
     over[...] = jnp.zeros_like(over)
     row_sums[...] = jnp.zeros_like(row_sums)
-    col_sums[...] = jnp.zeros_like(col_sums)
 
     @pl.when(live)
     def _():
         level = level_of(signal[0])
-        right[...] = right_parts(points_of(raw[...], inv_scale[...]))
+        raw = jnp.where(last, sent[:depth], raw_next[...])
+        right[...] = right_parts(points_of(raw, scale[...]))
         half[...] = direction[...].astype(bf16)
         half_next[...] = next_dir[...].astype(bf16)
         col_part[...] = jnp.zeros_like(col_part)
@@ -260,7 +258,7 @@
         def product(k):
             row, col = order[k]
             block = tile[cut(row), cut(col)]
-            over[:, cut(col)] += dot(half[:, cut(row)], block)
+            over[:probes, cut(col)] += dot(half[:, cut(row)], block)
             own[:, cut(row)] += dot_nt(half_next[:, cut(col)], block)
 
         argument(0)
@@ -284,10 +282,11 @@
             precision=lax.Precision.HIGHEST,
             preferred_element_type=f32,
         )
-        col_sums[...] = jnp.sum(col_part[...], axis=0, keepdims=True)
+        columns = jnp.sum(col_part[...], axis=0, keepdims=True)
+        over[:probes] += columns * next_dir[...]
+        over[probes : probes + 1] = columns
 
     own[...] += diagonal[...] + (noise[...] + row_sums[0:1, :]) * direction[...]
-    over[...] += col_sums[...] * next_dir[...]
 
 
 def both_parts(x):
@@ -300,44 +299,56 @@
     return x[:half] + x[half:]
 
 
-def second_crossing_kernel(flags, tile, row_sums, col_sums, image, part, over, own2, over2):
-    members = lax.axis_size("pair")
-    mine = lax.axis_index("pair")
-    listed = flags[0, mine]
-    for k in range(1, members):
-        listed = listed + flags[k, mine]
-    live = listed > 0.0
+def over_kernel(mark, tile, image, over2):
+    live = jnp.max(mark[...]) > 0.0
 
     @pl.when(live)
     def _():
-        here = image[...]
-        there = part[...] + over[...]
-        over2[...] = folded(dot(both_parts(here), tile[...])) + col_sums[...] * there
-        own2[...] = folded(dot_nt(both_parts(there), tile[...])) + row_sums[0:1, :] * here
+        over2[...] = folded(dot(both_parts(image[...]), tile[...]))
 
     @pl.when(jnp.logical_not(live))
     def _():
         over2[...] = jnp.zeros_like(over2)
-        own2[...] = jnp.zeros_like(own2)
-
-
-def second_diagonal_kernel(tile, noise, direction, next_dir, image, part, over, cross, over2, own2, sums, both):
+
+
+def second_kernel(
+    mark,
+    tile,
+    cross_tile,
+    row_sums,
+    noise,
+    direction,
+    next_dir,
+    image,
+    part,
+    over,
+    got,
+    over2,
+    own2,
+    sums,
+    both,
+):
     size = tile.shape[0]
+    probes = image.shape[0]
     here = image[...]
     both[...] = both_parts(here)
-    own2[...] = cross[...] + noise[...] * here
-    wide = CHUNK
-    for at in range(0, size, wide):
-        rows = slice(at, at + wide)
+    own2[...] = (noise[...] + row_sums[0:1, :] + got[probes : probes + 1, :]) * here
+    for at in range(0, size, CHUNK):
+        rows = slice(at, at + CHUNK)
         tail = slice(at, size)
-        rest = slice(at + wide, size)
+        rest = slice(at + CHUNK, size)
         own2[:, tail] += folded(dot(both[:, rows], tile[rows, tail]))
-        if at + wide < size:
+        if at + CHUNK < size:
             own2[:, rows] += folded(dot_nt(both[:, rest], tile[rows, rest]))
+    there = part[...] + over[:probes]
+
+    @pl.when(jnp.max(mark[...]) > 0.0)
+    def _():
+        own2[...] += folded(dot_nt(both_parts(there), cross_tile[...]))
+
     begin = direction[...]
     mine = own2[...]
     theirs = over2[...]
-    there = part[...] + over[...]
     squares = here * here
     forms = [
         begin * begin,
@@ -347,16 +358,18 @@
         here * mine + there * theirs,
     ]
     pairs = [lane_tiles_sum(x) for x in forms]
-    probes = begin.shape[0]
     high, low = lanes_sum(
         jnp.concatenate([x for x, _ in pairs], axis=0), jnp.concatenate([x for _, x in pairs], axis=0)
     )
+    rows = [(high, 0), (low, 0), (high, 1), (low, 1), (high, 2), (low, 2), (high, 3), (high, 4)]
     lane = lax.broadcasted_iota(jnp.int32, (probes, 128), 1)
-    for part_at, values in enumerate((high, low)):
-        out = jnp.zeros((probes, 128), f32)
-        for k in range(len(forms)):
-            out = jnp.where(lane == k, values[k * probes : (k + 1) * probes], out)
-        sums[part_at * probes : (part_at + 1) * probes, :] = out
+    out = jnp.zeros((probes, 128), f32)
+    for k, (values, at) in enumerate(rows):
+        out = jnp.where(lane == k, values[at * probes : (at + 1) * probes], out)
+    square = jnp.concatenate([out, jnp.zeros((128 - probes, 128), f32)], axis=0)
+    turned = square.T[: len(rows)]
+    for k in range(sums.shape[0]):
+        sums[k] = turned
 
 
 def final_kernel(sums, right_side, *rest):
@@ -364,7 +377,7 @@
     images, images2 = rest[:members], rest[members : 2 * members]
     solution_out, residual_out, begins, solved, left_over, get_sems, put_sems = rest[2 * members :]
     probes, size = images[0].shape
-    mine = lax.axis_index("pair")
+    mine = own_block()
 
     def block(k):
         return pl.ds(pl.multiple_of((mine ^ k) * size, size), size)
@@ -376,10 +389,18 @@
     for get in gets:
         get.start()
 
-    def total(k):
-        return sums[:probes, k : k + 1], sums[probes:, k : k + 1]
-
-    square, form, image_square, mixed, image_form = (total(k) for k in range(5))
+    total = sums[0]
+    error = jnp.zeros_like(total)
+    for k in range(1, sums.shape[0]):
+        total, missed = two_sum(total, sums[k])
+        error = error + missed
+    empty = jnp.zeros((128 - total.shape[0], 128), f32)
+    total = jnp.concatenate([total, empty], axis=0).T[:probes]
+    error = jnp.concatenate([error, empty], axis=0).T[:probes]
+    square, form, image_square = (
+        (total[:, k : k + 1], total[:, k + 1 : k + 2] + error[:, k : k + 1]) for k in (0, 2, 4)
+    )
+    mixed, image_form = ((total[:, k : k + 1], error[:, k : k + 1]) for k in (6, 7))
     alpha = square[0] / form[0]
     new = plus(plus(square, times(form, -2.0 * alpha)), times(times(image_square, alpha), alpha))[0]
     beta = new / square[0]
@@ -419,93 +440,97 @@
 ANY = pl.BlockSpec(memory_space=pl.ANY)
 
 
-def diagonal_call(signal, features, inv_scale, right_side, size):
+def loading_call(features, right_side, noise_var, inv_scale, size):
     depth = features.shape[0]
     probes = right_side.shape[0]
+    shapes = [
+        (depth + probes, size),
+        (depth, size),
+        (probes, size),
+        (depth, size),
+        (probes, size),
+        (1, size),
+        (1, depth),
+    ]
+    return pl.pallas_call(
+        loading_kernel,
+        in_specs=[HBM] * 4,
+        out_specs=[VMEM] * len(shapes),
+        out_shape=[pltpu.VMEM(shape, f32) for shape in shapes],
+        scratch_shapes=[pltpu.SemaphoreType.DMA((len(shapes) + 1,))],
+        compiler_params=params(16),
+    )(features, right_side, noise_var, inv_scale)
+
+
+def diagonal_call(signal, raw, scale, direction):
+    depth, size = raw.shape
+    probes = direction.shape[0]
     return pl.pallas_call(
         diagonal_kernel,
-        in_specs=[SMEM, HBM, VMEM, HBM],
-        out_specs=[VMEM] * 4,
+        in_specs=[SMEM, VMEM, VMEM, VMEM],
+        out_specs=[VMEM] * 3,
         out_shape=[
             pltpu.VMEM((size, size), bf16),
-            shaped(probes, size),
+            pltpu.VMEM((probes, size), f32),
             pltpu.VMEM((size, 4 * depth), bf16),
-            pltpu.VMEM((probes, size), f32),
         ],
         scratch_shapes=[
-            pltpu.VMEM((depth, size), f32),
             pltpu.VMEM((4 * depth, size), bf16),
             pltpu.VMEM((probes, size), bf16),
             pltpu.VMEM((2, CHUNK, CHUNK), f32),
-            pltpu.SemaphoreType.DMA((2,)),
         ],
         compiler_params=params(16),
-    )(signal, features, inv_scale, right_side)
-
-
-def crossing_call(
-    signal, flags, features, sent, inv_scale, left, right_side, sent_dir, direction, noise, diagonal
-):
-    depth = features.shape[0]
-    probes, size = direction.shape
+    )(signal, raw, scale, direction)
+
+
+def crossing_call(signal, listings, *arrays):
+    raw_next, direction = arrays[0], arrays[5]
+    depth, size = raw_next.shape
+    probes = direction.shape[0]
     return pl.pallas_call(
-        crossing_kernel,
-        in_specs=[SMEM, SMEM, HBM, ANY, ANY, VMEM, VMEM, HBM, ANY, VMEM, VMEM, VMEM],
-        out_specs=[VMEM] * 5 + [VMEM],
+        functools.partial(crossing_kernel, len(listings)),
+        in_specs=[SMEM] + [VMEM] * (len(listings) + len(arrays)),
+        out_specs=[VMEM] * 6,
         out_shape=[
             pltpu.VMEM((size, size), bf16),
-            shaped(8, size),
-            shaped(1, size),
-            shaped(probes, size),
-            shaped(probes, size),
-            shaped(probes, size),
+            pltpu.VMEM((8, size), f32),
+            pltpu.VMEM((probes, size), f32),
+            pltpu.VMEM((probes + 8, size), f32),
+            pltpu.VMEM((probes, size), f32),
+            pltpu.VMEM((8, 128), f32),
         ],
         scratch_shapes=[
-            pltpu.VMEM((depth, size), f32),
             pltpu.VMEM((4 * depth, size), bf16),
             pltpu.VMEM((probes, size), bf16),
             pltpu.VMEM((probes, size), bf16),
             pltpu.VMEM((2, CHUNK, CHUNK), f32),
             pltpu.VMEM((8, size), f32),
             pltpu.VMEM((size, 128), f32),
-            pltpu.SemaphoreType.DMA((3,)),
         ],
         compiler_params=params(16),
-    )(
-        signal,
-        flags,
-        features,
-        *sent,
-        inv_scale,
-        left,
-        right_side,
-        sent_dir,
-        direction,
-        noise,
-        diagonal,
-    )
-
-
-def second_crossing_call(flags, tile, row_sums, col_sums, image, part, over):
+    )(signal, *listings, *arrays)
+
+
+def over_call(mark, tile, image):
     return pl.pallas_call(
-        second_crossing_kernel,
-        in_specs=[SMEM] + [VMEM] * 6,
+        over_kernel,
+        in_specs=[VMEM] * 3,
+        out_specs=VMEM,
+        out_shape=pltpu.VMEM(image.shape, f32),
+        compiler_params=params(16),
+    )(mark, tile, image)
+
+
+def second_call(devices, *arrays):
+    probes, size = arrays[5].shape
+    return pl.pallas_call(
+        second_kernel,
+        in_specs=[VMEM] * len(arrays),
         out_specs=[VMEM] * 2,
-        out_shape=[shaped(*image.shape)] * 2,
-        compiler_params=params(16),
-    )(flags, tile, row_sums, col_sums, image, part, over)
-
-
-def second_diagonal_call(tile, noise, direction, next_dir, image, part, over, cross, over2):
-    probes, size = image.shape
-    return pl.pallas_call(
-        second_diagonal_kernel,
-        in_specs=[VMEM] * 9,
-        out_specs=[VMEM] * 2,
-        out_shape=[shaped(probes, size), shaped(2 * probes, 128)],
+        out_shape=[pltpu.VMEM((probes, size), f32), pltpu.VMEM((devices, 8, 128), f32)],
         scratch_shapes=[pltpu.VMEM((2 * probes, size), bf16)],
         compiler_params=params(16),
-    )(tile, noise, direction, next_dir, image, part, over, cross, over2)
+    )(*arrays)
 
 
 def final_call(sums, right_side, images, images2):
@@ -527,9 +552,17 @@
     )(sums, right_side, *images, *images2)
 
 
+def device_of(block):
+    members = lax.axis_size("pair")
+    group, at = divmod(block, members)
+    return group * members + (at ^ ((members - 1) * (group & 1)))
+
+
 def moved(x, distance):
     count = lax.axis_size(BOTH[0]) * lax.axis_size(BOTH[1])
-    route = [(i, i + distance) for i in range(count) if 0 <= i + distance < count]
+    route = [
+        (device_of(i), device_of(i + distance)) for i in range(count) if 0 <= i + distance < count
+    ]
     return lax.ppermute(x, BOTH, route)
 
 
@@ -538,85 +571,70 @@
     return lax.ppermute(x, BOTH, [(i, i ^ distance) for i in range(count)])
 
 
-def joined(x, distance):
-    other = exchanged(x, distance)
-    half = x.shape[0] // 2
-    high, error = two_sum(x[:half], other[:half])
-    return jnp.concatenate([high, (x[half:] + other[half:]) + error], axis=0)
-
-
-def sent_from_next_group(x, spread):
+def sent_from_next_group(x):
     members = lax.axis_size("pair")
-    route = [
-        ((g + 1) * members + spread % members, g * members + members - 1)
-        for g in range(lax.axis_size("blk") - 1)
-    ]
+    route = []
+    for g in range(lax.axis_size("blk") - 1):
+        target = device_of(g * members + members - 1)
+        route.append((target + members, target))
     return lax.ppermute(x, BOTH, route)
 
 
 def own_block_body(features, inv_scale, signal, noise_var, right_side, block_pairs):
     members = lax.axis_size("pair")
-    groups = lax.axis_size("blk")
+    devices = members * lax.axis_size("blk")
     size = features.shape[1] // members
-    half_depth = features.shape[0] // 2
-    mine = lax.axis_index("pair").astype(jnp.int32)
-    base = lax.axis_index("blk").astype(jnp.int32) * members
-
-    sent = (
-        sent_from_next_group(features[:half_depth, :size], 3),
-        sent_from_next_group(features[half_depth:, :size], 1),
-    )
-    sent_dir = sent_from_next_group(right_side[:, :size], 2)
-    wanted = (base + jnp.arange(members, dtype=jnp.int32))[None, :]
-    found = (block_pairs[:, 0:1] == wanted) & (block_pairs[:, 1:2] == wanted + 1)
-    found = jnp.sum(jnp.where(found, 1.0, 0.0).astype(f32), axis=0, keepdims=True)
-    flags = jnp.concatenate(
-        [found]
-        + [
-            lax.ppermute(found, "pair", [(i, (i + k) % members) for i in range(members)])
-            for k in range(1, members)
-        ],
-        axis=0,
-    )
-    scale = inv_scale[None, :]
-    noise = lax.dynamic_slice_in_dim(noise_var, mine * size, size, 0)[None, :]
-
-    tile, diagonal, left, direction = diagonal_call(signal, features, scale, right_side, size)
-    cross_tile, row_sums, col_sums, own, over, next_dir = crossing_call(
-        signal,
-        flags,
-        features,
-        sent,
-        scale,
-        left,
-        right_side,
-        sent_dir,
+    probes = right_side.shape[0]
+
+    features, right_side, scale, noise = (
+        pltpu.with_memory_space_constraint(x, pltpu.HBM)
+        for x in (features, right_side, inv_scale[None, :], noise_var[None, :])
+    )
+    send, raw, direction, raw_next, dir_next, noise, scale = loading_call(
+        features, right_side, noise, scale, size
+    )
+    sent = sent_from_next_group(send)
+    listing = block_pairs.T
+    listings = [listing] + [exchanged(listing, k) for k in range(1, members)]
+
+    tile, diagonal, left = diagonal_call(signal, raw, scale, direction)
+    cross_tile, row_sums, own, over, next_dir, mark = crossing_call(
+        signal, listings, raw_next, dir_next, sent, scale, left, direction, noise, diagonal
+    )
+    got = moved(over, 1)
+    part = moved(own, -1)
+    image = own + got[:probes]
+    images = {0: image, 1: exchanged(image, 1)}
+    spans = [1 << k for k in range(1, members.bit_length() - 1)]
+    for span in spans:
+        images[span] = exchanged(image, span)
+    over2 = over_call(mark, cross_tile, image)
+    own2, sums = second_call(
+        devices,
+        mark,
+        tile,
+        cross_tile,
+        row_sums,
+        noise,
         direction,
-        noise,
-        diagonal,
-    )
-    part = moved(own, -1)
-    image = own + moved(over, 1)
-    images = {0: image}
-    distance = members // 2
-    if distance:
-        images[distance] = exchanged(image, distance)
-    cross, over2 = second_crossing_call(flags, cross_tile, row_sums, col_sums, image, part, over)
-    own2, sums = second_diagonal_call(
-        tile, noise, direction, next_dir, image, part, over, cross, over2
-    )
-    step = members
-    while step < members * groups:
-        sums = joined(sums, step)
-        step *= 2
-    images2 = {0: own2 + moved(over2, 1)}
-    while distance:
-        sums = joined(sums, distance)
-        for held in (images, images2):
-            for at in list(held):
-                if at ^ distance not in held:
-                    held[at ^ distance] = exchanged(held[at], distance)
-        distance //= 2
+        next_dir,
+        image,
+        part,
+        over,
+        got,
+        over2,
+    )
+    image2 = own2 + moved(over2, 1)
+    images2 = {0: image2, 1: exchanged(image2, 1)}
+    for span in spans:
+        images2[span] = exchanged(image2, span)
+    image2, images, sums = lax.optimization_barrier((image2, images, sums))
+    sums = lax.all_to_all(sums, BOTH, 0, 0)
+    images2, images, sums = lax.optimization_barrier((images2, images, sums))
+    for held in (images, images2):
+        for span in spans:
+            for at in range(1, span):
+                held[at + span] = exchanged(held[span], at)
     return tuple(
         final_call(
             sums,
@@ -764,7 +782,7 @@
 
     def chosen(features, *rest):
         one_block_each = features.shape[1] == members * BS and BS % CHUNK == 0
-        powers = members & (members - 1) == 0 and groups & (groups - 1) == 0
+        powers = members > 1 and members & (members - 1) == 0 and groups & (groups - 1) == 0
         each = own_block_body if one_block_each and powers else body
         return each(features, *rest)
 

time: 92.5 us -> 70.2 us (0.76)
  waiting for transfers between devices: 17.8 us -> 1.43 us
  starting transfers between devices: 34.8 us -> 18.6 us
  blocking collectives: 0 us -> 16 us
  local copies, waits for them, and re-layouts: 6.97 us -> 0.67 us
  Pallas kernels: 29.4 us -> 31.1 us
    all_to_all x0 -> x1, blocking collectives: none -> 16 us  [own_block_body(): sums = lax.all_to_all(sums, BOTH, 0, 0)]
    ppermute x11 -> x9, starting transfers between devices: 23.9 us -> 9.67 us  [exchanged(): return lax.ppermute(x, BOTH, [(i, i ^ distance) for i in range(count)])]
    ppermute x11 -> x9, waiting for transfers between devices: 11.2 us -> 1.42 us  [exchanged(): return lax.ppermute(x, BOTH, [(i, i ^ distance) for i in range(count)])]
    ppermute x3 -> x0, starting transfers between devices: 4.53 us -> none  [own_block_body(): lax.ppermute(found, 'pair', [(i, (i + k) % members) for i in range(member...]
    ppermute x3, waiting for transfers between devices: 3.82 us -> 0.01 us  [moved(): return lax.ppermute(x, BOTH, route)]
    ppermute x3, starting transfers between devices: 4.4 us -> 8.19 us  [moved(): return lax.ppermute(x, BOTH, route)]
    unnamed x8 -> x2, local copies, waits for them, and re-layouts: 3.47 us -> 0.67 us
    ppermute x3 -> x0, waiting for transfers between devices: 2.78 us -> none  [own_block_body(): lax.ppermute(found, 'pair', [(i, (i + k) % members) for i in range(member...]
  transfers between devices with their start and end apart: 20 -> 13, of which waited for: 8 -> 2; matrix products, arithmetic and copies ran while one was open for 3% -> 0% of each run, Pallas kernels for 7% -> 20%
where the time goes in v3:
time: 70.2 us; the launch traced here: 69.4 us
  Pallas kernels  31.1 us (44%)
  starting transfers between devices  18.6 us (26%)
  blocking collectives  16 us (23%)
  between operations  1.6 us (2%)
  waiting for transfers between devices  1.43 us (2%)
    all_to_all x1, blocking collectives, own_block_body(): sums = lax.all_to_all(sums, BOTH, 0, 0)  16 us
    pallas_call x1, Pallas kernels, crossing_call(): pl.pallas_call(functools.partial(crossing_kernel, len(listings)), in_spec...  12 us
    ppermute x9, starting transfers between devices, exchanged(): return lax.ppermute(x, BOTH, [(i, i ^ distance) for i in range(count)])  9.67 us
    ppermute x3, starting transfers between devices, moved(): return lax.ppermute(x, BOTH, route)  8.19 us
    pallas_call x1, Pallas kernels, diagonal_call(): pl.pallas_call(diagonal_kernel, in_specs=[SMEM, VMEM, VMEM, VMEM], out_sp...  6.46 us
    pallas_call x1, Pallas kernels, second_call(): pl.pallas_call(second_kernel, in_specs=[VMEM] * len(arrays), out_specs=[V...  5.58 us
    pallas_call x1, Pallas kernels, final_call(): pl.pallas_call(final_kernel, in_specs=[VMEM, HBM] + [VMEM] * (2 * members...  3.46 us
    pallas_call x1, Pallas kernels, over_call(): pl.pallas_call(over_kernel, in_specs=[VMEM] * 3, out_specs=VMEM, out_shap...  1.89 us
  transfers between devices with their start and end apart: 13, of which 2 were waited for; matrix products, arithmetic and copies ran while one was open for 0% of the time, Pallas kernels for 20%

profile of v3, /device:TPU:0, one launch (start us, length us, event | category | flops | bytes accessed | tf_op | source)
XLA Modules:
  0.0 69.4 jit_solution(4529635779438387333)
XLA Ops:
  0.6 1.7 %shard_map.77 = (f32[96,2048]{1,0:T(8,128)S(1)}, f32[64,2048]{1,0:T(8,128)S(1)}, f32[32,2048]{1,0:T(8,128)S(1)}, f32[64,2048]{1,0:T(8,128)S(1)}, f32[32,2048]{1,...) custom-call(f32[64,8192]{1,0:T(8,128)} %features.1, f32[32,8192]{1,0:T(8,128)} %right_side.3, ...), custom_call_target="tpu_custom_call" | custom-call | tf_op jit(solution)/shard_map/pallas_call | solution.py:455
  2.3 0.7 %collective-permute-start.3 = (f32[96,2048]{1,0:T(8,128)S(1)}, f32[96,2048]{1,0:T(8,128)S(1)}, u32[]{:S(2)}, u32[]{:S(2)}) collective-permute-start(f32[96,2048]{1,0:T(8,128)S(1)} %get-tuple-element.33), channel_id=1, source_target_pairs={{7,3},{8,4},{15,11},{16,12},{23,19},{24,20},{31,27}} | collective-permute-start | bytes 2359304 | tf_op jit(solution)/shard_map/ppermute | solution.py:580
  3.0 3.1 %collective-permute-start.2 = (s32[2,4]{1,0:T(2,128)}, s32[2,4]{1,0:T(2,128)S(1)}, u32[]{:S(2)}, u32[]{:S(2)}) collective-permute-start(s32[2,4]{1,0:T(2,128)} %bitcast.3), channel_id=1, source_target_pairs={{0,3},{1,2},{2,1},{3,0},{4,7},{5,6},{6,5},{7,4},{8,11},{9,10},{10,... | collective-permute-start | bytes 104 | tf_op jit(solution)/shard_map/ppermute | solution.py:571
  6.1 0.0 collective-permute-start.1
  6.1 0.1 collective-permute-start
  6.9 6.5 %shard_map.78 = (bf16[2048,2048]{1,0:T(8,128)(2,1)S(1)}, f32[32,2048]{1,0:T(8,128)S(1)}, bf16[2048,256]{1,0:T(8,128)(2,1)S(1)}) custom-call(f32[1]{0:T(128)S(6)} %copy.8.signal, f32[64,2048]{1,0:T(8,128)S(1)} %get-tuple-element.35.raw, f32[1,64]{1,0:T(1,128)S(1)} %get-tuple-element.34.scale.refs_7_, f32[32,2048]{1,0:T(8,128)S(1)} %get-tuple-element.36.direction.refs_9_), custom_call_target="tpu_custom_call" | custom-call | tf_op jit(solution)/shard_map/pallas_call | solution.py:468
  13.4 0.0 collective-permute-done.2.refs_3_
  13.4 0.0 collective-permute-done.1.refs_2_
  13.4 0.0 collective-permute-done.refs_1_
  13.4 0.0 collective-permute-done.3.refs_6_
  13.4 0.0 copy-start
  13.4 0.7 copy-done
  14.1 12.0 %shard_map.79 = (bf16[2048,2048]{1,0:T(8,128)(2,1)S(1)}, f32[8,2048]{1,0:T(8,128)S(1)}, f32[32,2048]{1,0:T(8,128)S(1)}, f32[40,2048]{1,0:T(8,128)S(1)}, f32[32,2048]{1,0:T(8,128)S(1)}, /*index=5*/f32[8,128]{1,0:T(8,128)S(1)}) custom-call(f32[1]{0:T(128)S(6)} %copy.8.signal, s32[2,4]{1,0:T(2,128)S(1)} %bitcast.6, s32[2,4]{1,0:T(2,128)S(1)} %collective-permute-done.refs_1_, ...), custom_call_target="tpu_custom_call" | custom-call | tf_op jit(solution)/shard_map/pallas_call | solution.py:490
  26.1 2.3 %collective-permute-start.4 = (f32[40,2048]{1,0:T(8,128)S(1)}, f32[40,2048]{1,0:T(8,128)S(1)}, u32[]{:S(2)}, u32[]{:S(2)}) collective-permute-start(f32[40,2048]{1,0:T(8,128)S(1)} %get-tuple-element.46.over), channel_id=1, source_target_pairs={{0,1},{1,2},{2,3},{3,7},{7,6},{6,5},{5,4},{4,8},{8,9},{9,10},{10,1... | collective-permute-start | bytes 983048 | tf_op jit(solution)/shard_map/ppermute | solution.py:566
  28.4 1.3 %collective-permute-start.5 = (f32[32,2048]{1,0:T(8,128)S(1)}, f32[32,2048]{1,0:T(8,128)S(1)}, u32[]{:S(2)}, u32[]{:S(2)}) collective-permute-start(f32[32,2048]{1,0:T(8,128)S(1)} %get-tuple-element.45), channel_id=1, source_target_pairs={{1,0},{2,1},{3,2},{7,3},{6,7},{5,6},{4,5},{8,4},{9,8},{10,9},{11,1... | collective-permute-start | bytes 786440 | tf_op jit(solution)/shard_map/ppermute | solution.py:566
  29.7 0.0 collective-permute-done.4.got
  29.8 1.9 %shard_map.80.over2 = f32[32,2048]{1,0:T(8,128)S(1)} custom-call(f32[8,128]{1,0:T(8,128)S(1)} %get-tuple-element.40.mark, bf16[2048,2048]{1,0:T(8,128)(2,1)S(1)} %get-tuple-element.42.tile.cross_tile, f32[32,2048]{1,0:T(8,128)S(1)} %slice_add_fusion.image.rest_0_), custom_call_target="tpu_custom_call" | custom-call | tf_op jit(solution)/shard_map/pallas_call | solution.py:515
  31.6 4.6 %collective-permute-start.6 = (f32[32,2048]{1,0:T(8,128)S(1)}, f32[32,2048]{1,0:T(8,128)S(1)}, u32[]{:S(2)}, u32[]{:S(2)}) collective-permute-start(f32[32,2048]{1,0:T(8,128)S(1)} %shard_map.80.over2), channel_id=1, source_target_pairs={{0,1},{1,2},{2,3},{3,7},{7,6},{6,5},{5,4},{4,8},{8,9},{9,10},{10,1... | collective-permute-start | bytes 786440 | tf_op jit(solution)/shard_map/ppermute | solution.py:566
  36.3 2.6 %collective-permute-start.10 = (f32[32,2048]{1,0:T(8,128)S(1)}, f32[32,2048]{1,0:T(8,128)S(1)}, u32[]{:S(2)}, u32[]{:S(2)}) collective-permute-start(f32[32,2048]{1,0:T(8,128)S(1)} %slice_add_fusion.image.rest_0_), channel_id=1, source_target_pairs={{0,2},{1,3},{2,0},{3,1},{4,6},{5,7},{6,4},{7,5},{8,10},{9,11},{10,... | collective-permute-start | bytes 786440 | tf_op jit(solution)/shard_map/ppermute | solution.py:571
  38.9 3.2 %collective-permute-start.9 = (f32[32,2048]{1,0:T(8,128)S(1)}, f32[32,2048]{1,0:T(8,128)S(1)}, u32[]{:S(2)}, u32[]{:S(2)}) collective-permute-start(f32[32,2048]{1,0:T(8,128)S(1)} %slice_add_fusion.image.rest_0_), channel_id=1, source_target_pairs={{0,1},{1,0},{2,3},{3,2},{4,5},{5,4},{6,7},{7,6},{8,9},{9,8},{10,11... | collective-permute-start | bytes 786440 | tf_op jit(solution)/shard_map/ppermute | solution.py:571
  42.0 0.0 collective-permute-done.5.part
  42.0 5.6 %shard_map.81 = (f32[32,2048]{1,0:T(8,128)S(1)}, f32[32,8,128]{2,1,0:T(8,128)S(1)}) custom-call(f32[8,128]{1,0:T(8,128)S(1)} %get-tuple-element.40.mark, bf16[2048,2048]{1,0:T(8,128)(2,1)S(1)} %get-tuple-element.41.tile, bf16[2048,2048]{1,0:T(8,128)(2,1)S(1)} %get-tuple-element.42.tile.cross_tile, f32[8,2048]{1,0:T(8,128)S(1)} %get-tuple-element.43.row_sums, ...), custom_call_target="tpu_custom_call" | custom-call | tf_op jit(solution)/shard_map/pallas_call | solution.py:526
  47.6 0.0 collective-permute-done.6
  47.7 0.1 collective-permute-start.8
  47.7 0.1 collective-permute-start.7
  47.8 0.0 collective-permute-done.10.rest_2_
  47.8 0.0 collective-permute-done.9.rest_1_
  47.8 16.0 %all_to_all.5.sums = f32[32,8,128]{2,1,0:T(8,128)S(1)} all-to-all(f32[32,8,128]{2,1,0:T(8,128)S(1)} %get-tuple-element.52), channel_id=1, replica_groups=mesh['blk'=8,'pair'=4] {'blk','pair'}, dimensions={0} | all-to-all | bytes 262144 | tf_op jit(solution)/shard_map/all_to_all | solution.py:632
  63.9 0.0 collective-permute-done.8.rest_6_
  63.9 0.0 collective-permute-done.7.rest_5_
  63.9 0.2 collective-permute-start.11
  64.1 0.3 collective-permute-start.12
  64.4 1.0 %collective-permute-done.11.rest_3_ = f32[32,2048]{1,0:T(8,128)S(1)} collective-permute-done((f32[32,2048]{1,0:T(8,128)S(1)}, f32[32,2048]{1,0:T(8,128)S(1)}, u32[]{:S(2)}, u32[]{:S(2)}) %collective-permute-start.11) | collective-permute-done | bytes 262176 | tf_op jit(solution)/shard_map/ppermute | solution.py:571
  65.4 0.4 collective-permute-done.12.rest_7_
  65.8 3.5 %shard_map.82 = (f32[32,8192]{1,0:T(8,128)}, f32[32,8192]{1,0:T(8,128)}) custom-call(f32[32,8,128]{2,1,0:T(8,128)S(1)} %all_to_all.5.sums, f32[32,8192]{1,0:T(8,128)} %right_side.3, f32[32,2048]{1,0:T(8,128)S(1)} %slice_add_fusion.image.rest_0_, f32[32,2048]{1,0:T(8,128)S(1)} %collective-permute-done.9.rest_1_, ...), custom_call_target="tpu_custom_call" | custom-call | tf_op jit(solution)/shard_map/pallas_call | solution.py:539
  (2 shorter events, 0.1 us)
Async XLA Ops:
  2.3 11.1 %collective-permute-start.3 = (f32[96,2048]{1,0:T(8,128)S(1)}, f32[96,2048]{1,0:T(8,128)S(1)}, u32[]{:S(2)}, u32[]{:S(2)}) collective-permute-start(f32[96,2048]{1,0:T(8,128)S(1)} %get-tuple-element.33), channel_id=1, source_target_pairs={{7,3},{8,4},{15,11},{16,12},{23,19},{24,20},{31,27}} | collective-permute-start | bytes 2359304 | tf_op jit(solution)/shard_map/ppermute | solution.py:580
  3.0 10.4 %collective-permute-start.2 = (s32[2,4]{1,0:T(2,128)}, s32[2,4]{1,0:T(2,128)S(1)}, u32[]{:S(2)}, u32[]{:S(2)}) collective-permute-start(s32[2,4]{1,0:T(2,128)} %bitcast.3), channel_id=1, source_target_pairs={{0,3},{1,2},{2,1},{3,0},{4,7},{5,6},{6,5},{7,4},{8,11},{9,10},{10,... | collective-permute-start | bytes 104 | tf_op jit(solution)/shard_map/ppermute | solution.py:571
  6.1 7.3 %collective-permute-start.1 = (s32[2,4]{1,0:T(2,128)}, s32[2,4]{1,0:T(2,128)S(1)}, u32[]{:S(2)}, u32[]{:S(2)}) collective-permute-start(s32[2,4]{1,0:T(2,128)} %bitcast.4), channel_id=1, source_target_pairs={{0,2},{1,3},{2,0},{3,1},{4,6},{5,7},{6,4},{7,5},{8,10},{9,11},{10,... | collective-permute-start | bytes 104 | tf_op jit(solution)/shard_map/ppermute | solution.py:571
  6.1 7.3 %collective-permute-start = (s32[2,4]{1,0:T(2,128)}, s32[2,4]{1,0:T(2,128)S(1)}, u32[]{:S(2)}, u32[]{:S(2)}) collective-permute-start(s32[2,4]{1,0:T(2,128)} %bitcast.5), channel_id=1, source_target_pairs={{0,1},{1,0},{2,3},{3,2},{4,5},{5,4},{6,7},{7,6},{8,9},{9,8},{10,11... | collective-permute-start | bytes 104 | tf_op jit(solution)/shard_map/ppermute | solution.py:571
  13.4 0.7 copy-start
  26.1 3.6 %collective-permute-start.4 = (f32[40,2048]{1,0:T(8,128)S(1)}, f32[40,2048]{1,0:T(8,128)S(1)}, u32[]{:S(2)}, u32[]{:S(2)}) collective-permute-start(f32[40,2048]{1,0:T(8,128)S(1)} %get-tuple-element.46.over), channel_id=1, source_target_pairs={{0,1},{1,2},{2,3},{3,7},{7,6},{6,5},{5,4},{4,8},{8,9},{9,10},{10,1... | collective-permute-start | bytes 983048 | tf_op jit(solution)/shard_map/ppermute | solution.py:566
  28.4 13.6 %collective-permute-start.5 = (f32[32,2048]{1,0:T(8,128)S(1)}, f32[32,2048]{1,0:T(8,128)S(1)}, u32[]{:S(2)}, u32[]{:S(2)}) collective-permute-start(f32[32,2048]{1,0:T(8,128)S(1)} %get-tuple-element.45), channel_id=1, source_target_pairs={{1,0},{2,1},{3,2},{7,3},{6,7},{5,6},{4,5},{8,4},{9,8},{10,9},{11,1... | collective-permute-start | bytes 786440 | tf_op jit(solution)/shard_map/ppermute | solution.py:566
  31.6 16.0 %collective-permute-start.6 = (f32[32,2048]{1,0:T(8,128)S(1)}, f32[32,2048]{1,0:T(8,128)S(1)}, u32[]{:S(2)}, u32[]{:S(2)}) collective-permute-start(f32[32,2048]{1,0:T(8,128)S(1)} %shard_map.80.over2), channel_id=1, source_target_pairs={{0,1},{1,2},{2,3},{3,7},{7,6},{6,5},{5,4},{4,8},{8,9},{9,10},{10,1... | collective-permute-start | bytes 786440 | tf_op jit(solution)/shard_map/ppermute | solution.py:566
  36.3 11.6 %collective-permute-start.10 = (f32[32,2048]{1,0:T(8,128)S(1)}, f32[32,2048]{1,0:T(8,128)S(1)}, u32[]{:S(2)}, u32[]{:S(2)}) collective-permute-start(f32[32,2048]{1,0:T(8,128)S(1)} %slice_add_fusion.image.rest_0_), channel_id=1, source_target_pairs={{0,2},{1,3},{2,0},{3,1},{4,6},{5,7},{6,4},{7,5},{8,10},{9,11},{10,... | collective-permute-start | bytes 786440 | tf_op jit(solution)/shard_map/ppermute | solution.py:571
  38.9 9.0 %collective-permute-start.9 = (f32[32,2048]{1,0:T(8,128)S(1)}, f32[32,2048]{1,0:T(8,128)S(1)}, u32[]{:S(2)}, u32[]{:S(2)}) collective-permute-start(f32[32,2048]{1,0:T(8,128)S(1)} %slice_add_fusion.image.rest_0_), channel_id=1, source_target_pairs={{0,1},{1,0},{2,3},{3,2},{4,5},{5,4},{6,7},{7,6},{8,9},{9,8},{10,11... | collective-permute-start | bytes 786440 | tf_op jit(solution)/shard_map/ppermute | solution.py:571
  47.7 16.2 %collective-permute-start.8 = (f32[32,2048]{1,0:T(8,128)S(1)}, f32[32,2048]{1,0:T(8,128)S(1)}, u32[]{:S(2)}, u32[]{:S(2)}) collective-permute-start(f32[32,2048]{1,0:T(8,128)S(1)} %add.7.rest_4_), channel_id=1, source_target_pairs={{0,2},{1,3},{2,0},{3,1},{4,6},{5,7},{6,4},{7,5},{8,10},{9,11},{10,... | collective-permute-start | bytes 786440 | tf_op jit(solution)/shard_map/ppermute | solution.py:571
  47.7 16.1 %collective-permute-start.7 = (f32[32,2048]{1,0:T(8,128)S(1)}, f32[32,2048]{1,0:T(8,128)S(1)}, u32[]{:S(2)}, u32[]{:S(2)}) collective-permute-start(f32[32,2048]{1,0:T(8,128)S(1)} %add.7.rest_4_), channel_id=1, source_target_pairs={{0,1},{1,0},{2,3},{3,2},{4,5},{5,4},{6,7},{7,6},{8,9},{9,8},{10,11... | collective-permute-start | bytes 786440 | tf_op jit(solution)/shard_map/ppermute | solution.py:571
  63.9 1.5 %collective-permute-start.11 = (f32[32,2048]{1,0:T(8,128)S(1)}, f32[32,2048]{1,0:T(8,128)S(1)}, u32[]{:S(2)}, u32[]{:S(2)}) collective-permute-start(f32[32,2048]{1,0:T(8,128)S(1)} %collective-permute-done.10.rest_2_), channel_id=1, source_target_pairs={{0,1},{1,0},{2,3},{3,2},{4,5},{5,4},{6,7},{7,6},{8,9},{9,8},{10,11... | collective-permute-start | bytes 786440 | tf_op jit(solution)/shard_map/ppermute | solution.py:571
  64.1 1.7 %collective-permute-start.12 = (f32[32,2048]{1,0:T(8,128)S(1)}, f32[32,2048]{1,0:T(8,128)S(1)}, u32[]{:S(2)}, u32[]{:S(2)}) collective-permute-start(f32[32,2048]{1,0:T(8,128)S(1)} %collective-permute-done.8.rest_6_), channel_id=1, source_target_pairs={{0,1},{1,0},{2,3},{3,2},{4,5},{5,4},{6,7},{7,6},{8,9},{9,8},{10,11... | collective-permute-start | bytes 786440 | tf_op jit(solution)/shard_map/ppermute | solution.py:571

commit v4 on v3

--- a/solution.py
+++ b/solution.py
@@ -18,6 +18,7 @@
 BOTH = ("blk", "pair")
 NT = (((1,), (1,)), ((), ()))
 CHUNK = 256
+UPPER_STRIPS = 2
 
 RATE = taper_radius * root_three * math.log2(math.e)
 NEAR = math.log2(math.e)
@@ -86,13 +87,18 @@
     return lax.axis_index("pair") ^ ((members - 1) * (lax.axis_index("blk") & 1))
 
 
-def is_live(listings):
-    first = lax.axis_index("blk") * lax.axis_size("pair") + own_block()
-    found = jnp.zeros(listings[0][0:1, :].shape, f32)
-    for listing in listings:
-        match = (listing[0:1, :] == first) & (listing[1:2, :] == first + 1)
-        found = found + jnp.where(match, 1.0, 0.0)
-    return jnp.max(found) > 0.0
+def found_in(listing, shape):
+    wanted = lax.axis_index("blk") * lax.axis_size("pair") + lax.broadcasted_iota(jnp.int32, shape, 1)
+    found = jnp.zeros(shape, f32)
+    for slot in range(listing.shape[1]):
+        first, second = listing[0:1, slot : slot + 1], listing[1:2, slot : slot + 1]
+        found = jnp.where((first == wanted) & (second == wanted + 1), 1.0, found)
+    return found
+
+
+def is_live(found):
+    lane = lax.broadcasted_iota(jnp.int32, found.shape, 1)
+    return jnp.max(jnp.where(lane == own_block(), found, 0.0)) > 0.0
 
 
 def cut(at):
@@ -151,30 +157,37 @@
     right_side,
     noise_var,
     inv_scale,
+    block_pairs,
     send,
+    send_rest,
     raw,
     direction,
     raw_next,
     next_dir,
     noise,
     scale,
+    found,
+    listing,
     sems,
 ):
     size = raw.shape[1]
     depth = raw.shape[0]
+    cut_at = send.shape[0]
     mine = own_block()
     after = jnp.minimum(mine + 1, lax.axis_size("pair") - 1)
     here = pl.ds(pl.multiple_of(mine * size, size), size)
     there = pl.ds(pl.multiple_of(after * size, size), size)
     moves = [
-        (features.at[:, :size], send.at[:depth]),
-        (right_side.at[:, :size], send.at[depth:]),
+        (features.at[:cut_at, :size], send),
+        (features.at[cut_at:, :size], send_rest.at[: depth - cut_at]),
+        (right_side.at[:, :size], send_rest.at[depth - cut_at :]),
         (features.at[:, here], raw),
         (right_side.at[:, here], direction),
         (features.at[:, there], raw_next),
         (right_side.at[:, there], next_dir),
         (noise_var.at[:, here], noise),
         (inv_scale, scale),
+        (block_pairs, listing),
     ]
     copies = [
         pltpu.make_async_copy(source, target, sems.at[k])
@@ -184,19 +197,16 @@
         copy.start()
     for copy in copies:
         copy.wait()
-
-
-def diagonal_kernel(signal, raw, scale, direction, tile, own, left, right, half, ahead):
-    size = tile.shape[0]
-    level = level_of(signal[0])
-    points = points_of(raw[...], scale[...])
-    left[...] = left_parts(points)
-    right[...] = right_parts(points)
-    half[...] = direction[...].astype(bf16)
-    own[...] = jnp.zeros_like(own)
-
+    found[...] = found_in(listing, found.shape)
+
+
+def diagonal_products(level, first, tile, own, left, right, half, ahead):
+    size = tile.shape[1]
     count = size // CHUNK
-    order = [(row, col) for row in range(count) for col in range(row, count)]
+    begin = first // CHUNK
+    order = [
+        (row, col) for row in range(begin, begin + tile.shape[0] // CHUNK) for col in range(row, count)
+    ]
 
     def argument(k):
         row, col = order[k]
@@ -204,7 +214,7 @@
 
     def product(k):
         row, col = order[k]
-        block = tile[cut(row), cut(col)]
+        block = tile[cut(row - begin), cut(col)]
         own[:, cut(col)] += dot(half[:, cut(row)], block)
         if col > row:
             own[:, cut(row)] += dot_nt(half[:, cut(col)], block)
@@ -215,25 +225,55 @@
             argument(k + 1)
         if k:
             product(k - 1)
-        tile[cut(row), cut(col)] = kernel_values(ahead[k % 2], level).astype(bf16)
+        tile[cut(row - begin), cut(col)] = kernel_values(ahead[k % 2], level).astype(bf16)
     product(len(order) - 1)
 
 
+def diagonal_kernel(signal, raw, scale, direction, tile, own, left, right, half, ahead):
+    points = points_of(raw[...], scale[...])
+    left[...] = left_parts(points)
+    right[...] = right_parts(points)
+    half[...] = direction[...].astype(bf16)
+    own[...] = jnp.zeros_like(own)
+    diagonal_products(level_of(signal[0]), 0, tile, own, left, right, half, ahead)
+
+
+def lower_diagonal_kernel(signal, left, right, half, upper, crossed, tile, own, ahead):
+    own[...] = upper[...] + crossed[...]
+    first = tile.shape[1] - tile.shape[0]
+    diagonal_products(level_of(signal[0]), first, tile, own, left, right, half, ahead)
+
+
 def crossing_kernel(
-    members,
     signal,
-    *refs,
+    found,
+    raw_next,
+    dir_next,
+    sent,
+    sent_rest,
+    scale,
+    left,
+    half,
+    direction,
+    noise,
+    tile,
+    row_sums,
+    own,
+    over,
+    next_dir,
+    mark,
+    right,
+    half_next,
+    ahead,
+    col_part,
+    row_part,
 ):
-    listings, refs = refs[:members], refs[members:]
-    (raw_next, dir_next, sent, scale, left, direction, noise, diagonal) = refs[:8]
-    (tile, row_sums, own, over, next_dir, mark) = refs[8:14]
-    (right, half, half_next, ahead, col_part, row_part) = refs[14:]
     size = tile.shape[0]
     probes = own.shape[0]
-    last = own_block() == members - 1
-    depth = raw_next.shape[0]
-    next_dir[...] = jnp.where(last, sent[depth:], dir_next[...])
-    live = is_live(listings)
+    last = own_block() == lax.axis_size("pair") - 1
+    rest = raw_next.shape[0] - sent.shape[0]
+    next_dir[...] = jnp.where(last, sent_rest[rest:], dir_next[...])
+    live = is_live(found[...])
     mark[...] = jnp.where(live, jnp.ones(mark.shape, f32), jnp.zeros(mark.shape, f32))
     own[...] = jnp.zeros_like(own)
     over[...] = jnp.zeros_like(over)
@@ -242,9 +282,9 @@
     @pl.when(live)
     def _():
         level = level_of(signal[0])
-        raw = jnp.where(last, sent[:depth], raw_next[...])
+        raw = jnp.concatenate([sent[...], sent_rest[:rest]], axis=0)
+        raw = jnp.where(last, raw, raw_next[...])
         right[...] = right_parts(points_of(raw, scale[...]))
-        half[...] = direction[...].astype(bf16)
         half_next[...] = next_dir[...].astype(bf16)
         col_part[...] = jnp.zeros_like(col_part)
         row_part[...] = jnp.zeros_like(row_part)
@@ -286,7 +326,7 @@
         over[:probes] += columns * next_dir[...]
         over[probes : probes + 1] = columns
 
-    own[...] += diagonal[...] + (noise[...] + row_sums[0:1, :]) * direction[...]
+    own[...] += (noise[...] + row_sums[0:1, :]) * direction[...]
 
 
 def both_parts(x):
@@ -311,35 +351,28 @@
         over2[...] = jnp.zeros_like(over2)
 
 
-def second_kernel(
-    mark,
-    tile,
-    cross_tile,
-    row_sums,
-    noise,
-    direction,
-    next_dir,
-    image,
-    part,
-    over,
-    got,
-    over2,
-    own2,
-    sums,
-    both,
-):
-    size = tile.shape[0]
+def second_diagonal_kernel(upper, lower, row_sums, noise, image, got, own2, both):
+    size = upper.shape[1]
     probes = image.shape[0]
     here = image[...]
     both[...] = both_parts(here)
     own2[...] = (noise[...] + row_sums[0:1, :] + got[probes : probes + 1, :]) * here
-    for at in range(0, size, CHUNK):
-        rows = slice(at, at + CHUNK)
-        tail = slice(at, size)
-        rest = slice(at + CHUNK, size)
-        own2[:, tail] += folded(dot(both[:, rows], tile[rows, tail]))
-        if at + CHUNK < size:
-            own2[:, rows] += folded(dot_nt(both[:, rest], tile[rows, rest]))
+    for tile, first in ((upper, 0), (lower, upper.shape[0])):
+        for at in range(first, first + tile.shape[0], CHUNK):
+            rows = slice(at, at + CHUNK)
+            inside = slice(at - first, at - first + CHUNK)
+            rest = slice(at + CHUNK, size)
+            own2[:, at:] += folded(dot(both[:, rows], tile[inside, at:]))
+            if at + CHUNK < size:
+                own2[:, rows] += folded(dot_nt(both[:, rest], tile[inside, rest]))
+
+
+def second_kernel(
+    mark, cross_tile, direction, next_dir, image, part, over, over2, partial, own2, sums
+):
+    probes = image.shape[0]
+    here = image[...]
+    own2[...] = partial[...]
     there = part[...] + over[:probes]
 
     @pl.when(jnp.max(mark[...]) > 0.0)
@@ -375,44 +408,41 @@
 def final_kernel(sums, right_side, *rest):
     members = lax.axis_size("pair")
     images, images2 = rest[:members], rest[members : 2 * members]
-    solution_out, residual_out, begins, solved, left_over, get_sems, put_sems = rest[2 * members :]
-    probes, size = images[0].shape
+    solution_out, residual_out, solved, left_over, put_sems = rest[2 * members :]
+    probes, size = solved.shape[1:]
     mine = own_block()
 
     def block(k):
         return pl.ds(pl.multiple_of((mine ^ k) * size, size), size)
 
-    gets = [
-        pltpu.make_async_copy(right_side.at[:, block(k)], begins.at[k], get_sems.at[k])
-        for k in range(members)
-    ]
-    for get in gets:
-        get.start()
-
-    total = sums[0]
-    error = jnp.zeros_like(total)
-    for k in range(1, sums.shape[0]):
+    runs = [two_sum(sums[k], sums[k + 4]) for k in range(4)]
+    for k in range(8, sums.shape[0]):
+        total, error = runs[k % 4]
         total, missed = two_sum(total, sums[k])
-        error = error + missed
+        runs[k % 4] = (total, error + missed)
+    while len(runs) > 1:
+        joined = []
+        for (a, a_error), (b, b_error) in zip(runs[::2], runs[1::2]):
+            total, missed = two_sum(a, b)
+            joined.append((total, a_error + b_error + missed))
+        runs = joined
+    total, error = runs[0]
     empty = jnp.zeros((128 - total.shape[0], 128), f32)
     total = jnp.concatenate([total, empty], axis=0).T[:probes]
     error = jnp.concatenate([error, empty], axis=0).T[:probes]
     square, form, image_square = (
         (total[:, k : k + 1], total[:, k + 1 : k + 2] + error[:, k : k + 1]) for k in (0, 2, 4)
     )
-    mixed, image_form = ((total[:, k : k + 1], error[:, k : k + 1]) for k in (6, 7))
+    mixed, image_form = (total[:, k : k + 1] for k in (6, 7))
     alpha = square[0] / form[0]
     new = plus(plus(square, times(form, -2.0 * alpha)), times(times(image_square, alpha), alpha))[0]
     beta = new / square[0]
-    less = times(mixed, -alpha)
-    curvature = plus(plus(form, less), times(times(image_form, alpha), alpha))
-    curvature = plus(curvature, times(plus(times(form, 2.0), less), beta))
-    curvature = plus(curvature, times(times(form, beta), beta))
-    alpha2 = new / curvature[0]
+    less = form[0] - alpha * mixed
+    curvature = (less + alpha * alpha * image_form) + beta * ((form[0] + less) + beta * form[0])
+    alpha2 = new / curvature
     puts = []
     for k in range(members):
-        gets[k].wait()
-        begin = begins[k]
+        begin = right_side[:, block(k)]
         image = images[k][...]
         after = begin - alpha * image
         solved[k] = alpha * begin + alpha2 * (after + beta * begin)
@@ -440,56 +470,72 @@
 ANY = pl.BlockSpec(memory_space=pl.ANY)
 
 
-def loading_call(features, right_side, noise_var, inv_scale, size):
+def loading_call(features, right_side, noise_var, inv_scale, block_pairs, size):
     depth = features.shape[0]
     probes = right_side.shape[0]
+    half = min(depth, (depth + probes) // 16 * 8)
     shapes = [
-        (depth + probes, size),
+        (half, size),
+        (depth + probes - half, size),
         (depth, size),
         (probes, size),
         (depth, size),
         (probes, size),
         (1, size),
         (1, depth),
+        (8, 128),
     ]
     return pl.pallas_call(
         loading_kernel,
-        in_specs=[HBM] * 4,
+        in_specs=[HBM] * 5,
         out_specs=[VMEM] * len(shapes),
         out_shape=[pltpu.VMEM(shape, f32) for shape in shapes],
-        scratch_shapes=[pltpu.SemaphoreType.DMA((len(shapes) + 1,))],
+        scratch_shapes=[
+            pltpu.VMEM(block_pairs.shape, jnp.int32),
+            pltpu.SemaphoreType.DMA((len(shapes) + 1,)),
+        ],
         compiler_params=params(16),
-    )(features, right_side, noise_var, inv_scale)
-
-
-def diagonal_call(signal, raw, scale, direction):
+    )(features, right_side, noise_var, inv_scale, block_pairs)
+
+
+def diagonal_call(signal, raw, scale, direction, rows):
     depth, size = raw.shape
     probes = direction.shape[0]
     return pl.pallas_call(
         diagonal_kernel,
         in_specs=[SMEM, VMEM, VMEM, VMEM],
-        out_specs=[VMEM] * 3,
+        out_specs=[VMEM] * 5,
         out_shape=[
-            pltpu.VMEM((size, size), bf16),
+            pltpu.VMEM((rows, size), bf16),
             pltpu.VMEM((probes, size), f32),
             pltpu.VMEM((size, 4 * depth), bf16),
-        ],
-        scratch_shapes=[
             pltpu.VMEM((4 * depth, size), bf16),
             pltpu.VMEM((probes, size), bf16),
-            pltpu.VMEM((2, CHUNK, CHUNK), f32),
         ],
+        scratch_shapes=[pltpu.VMEM((2, CHUNK, CHUNK), f32)],
         compiler_params=params(16),
     )(signal, raw, scale, direction)
 
 
-def crossing_call(signal, listings, *arrays):
-    raw_next, direction = arrays[0], arrays[5]
+def lower_diagonal_call(signal, left, right, half, upper, crossed, rows):
+    probes, size = upper.shape
+    return pl.pallas_call(
+        lower_diagonal_kernel,
+        in_specs=[SMEM] + [VMEM] * 5,
+        out_specs=[VMEM] * 2,
+        out_shape=[pltpu.VMEM((rows, size), bf16), pltpu.VMEM((probes, size), f32)],
+        scratch_shapes=[pltpu.VMEM((2, CHUNK, CHUNK), f32)],
+        compiler_params=params(16),
+    )(signal, left, right, half, upper, crossed)
+
+
+def crossing_call(signal, *arrays):
+    raw_next, direction = arrays[1], arrays[8]
     depth, size = raw_next.shape
     probes = direction.shape[0]
     return pl.pallas_call(
-        functools.partial(crossing_kernel, len(listings)),
-        in_specs=[SMEM] + [VMEM] * (len(listings) + len(arrays)),
+        crossing_kernel,
+        in_specs=[SMEM] + [VMEM] * len(arrays),
         out_specs=[VMEM] * 6,
         out_shape=[
             pltpu.VMEM((size, size), bf16),
@@ -502,13 +548,12 @@
         scratch_shapes=[
             pltpu.VMEM((4 * depth, size), bf16),
             pltpu.VMEM((probes, size), bf16),
-            pltpu.VMEM((probes, size), bf16),
             pltpu.VMEM((2, CHUNK, CHUNK), f32),
             pltpu.VMEM((8, size), f32),
             pltpu.VMEM((size, 128), f32),
         ],
         compiler_params=params(16),
-    )(signal, *listings, *arrays)
+    )(signal, *arrays)
 
 
 def over_call(mark, tile, image):
@@ -521,31 +566,41 @@
     )(mark, tile, image)
 
 
+def second_diagonal_call(upper, lower, row_sums, noise, image, got):
+    probes, size = image.shape
+    return pl.pallas_call(
+        second_diagonal_kernel,
+        in_specs=[VMEM] * 6,
+        out_specs=VMEM,
+        out_shape=pltpu.VMEM((probes, size), f32),
+        scratch_shapes=[pltpu.VMEM((2 * probes, size), bf16)],
+        compiler_params=params(16),
+    )(upper, lower, row_sums, noise, image, got)
+
+
 def second_call(devices, *arrays):
-    probes, size = arrays[5].shape
+    probes, size = arrays[2].shape
     return pl.pallas_call(
         second_kernel,
         in_specs=[VMEM] * len(arrays),
         out_specs=[VMEM] * 2,
         out_shape=[pltpu.VMEM((probes, size), f32), pltpu.VMEM((devices, 8, 128), f32)],
-        scratch_shapes=[pltpu.VMEM((2 * probes, size), bf16)],
         compiler_params=params(16),
     )(*arrays)
 
 
 def final_call(sums, right_side, images, images2):
-    probes, size = images[0].shape
+    probes = right_side.shape[0]
+    size = images[0].shape[1]
     members = len(images)
     return pl.pallas_call(
         final_kernel,
-        in_specs=[VMEM, HBM] + [VMEM] * (2 * members),
+        in_specs=[VMEM] * (2 + 2 * members),
         out_specs=[HBM, HBM],
         out_shape=[shaped(*right_side.shape)] * 2,
         scratch_shapes=[
             pltpu.VMEM((members, probes, size), f32),
             pltpu.VMEM((members, probes, size), f32),
-            pltpu.VMEM((members, probes, size), f32),
-            pltpu.SemaphoreType.DMA((members,)),
             pltpu.SemaphoreType.DMA((2, members)),
         ],
         compiler_params=params(16),
@@ -571,12 +626,12 @@
     return lax.ppermute(x, BOTH, [(i, i ^ distance) for i in range(count)])
 
 
-def sent_from_next_group(x):
+def sent_from_next_group(x, aside):
     members = lax.axis_size("pair")
     route = []
     for g in range(lax.axis_size("blk") - 1):
         target = device_of(g * members + members - 1)
-        route.append((target + members, target))
+        route.append(((target + members) ^ aside, target))
     return lax.ppermute(x, BOTH, route)
 
 
@@ -586,51 +641,44 @@
     size = features.shape[1] // members
     probes = right_side.shape[0]
 
-    features, right_side, scale, noise = (
+    features, begins, scale, noise, listing = (
         pltpu.with_memory_space_constraint(x, pltpu.HBM)
-        for x in (features, right_side, inv_scale[None, :], noise_var[None, :])
-    )
-    send, raw, direction, raw_next, dir_next, noise, scale = loading_call(
-        features, right_side, noise, scale, size
-    )
-    sent = sent_from_next_group(send)
-    listing = block_pairs.T
-    listings = [listing] + [exchanged(listing, k) for k in range(1, members)]
-
-    tile, diagonal, left = diagonal_call(signal, raw, scale, direction)
-    cross_tile, row_sums, own, over, next_dir, mark = crossing_call(
-        signal, listings, raw_next, dir_next, sent, scale, left, direction, noise, diagonal
+        for x in (features, right_side, inv_scale[None, :], noise_var[None, :], block_pairs.T)
+    )
+    send, send_rest, raw, direction, raw_next, dir_next, noise, scale, found = loading_call(
+        features, begins, noise, scale, listing, size
+    )
+    spans = [1 << k for k in range(members.bit_length() - 1)]
+    sent = sent_from_next_group(send, 0)
+    sent_rest = sent_from_next_group(send_rest, members // 2)
+    found = found + exchanged(found, spans[-1])
+    split = UPPER_STRIPS * CHUNK
+    tile, diagonal, left, right, half = diagonal_call(signal, raw, scale, direction, split)
+    for span in reversed(spans[:-1]):
+        found, left = lax.optimization_barrier((found, left))
+        found = found + exchanged(found, span)
+    cross_tile, row_sums, crossed, over, next_dir, mark = crossing_call(
+        signal, found, raw_next, dir_next, sent, sent_rest, scale, left, half, direction, noise
     )
     got = moved(over, 1)
+    lower_tile, own = lower_diagonal_call(signal, left, right, half, diagonal, crossed, size - split)
     part = moved(own, -1)
     image = own + got[:probes]
-    images = {0: image, 1: exchanged(image, 1)}
-    spans = [1 << k for k in range(1, members.bit_length() - 1)]
+    images = {0: image}
     for span in spans:
         images[span] = exchanged(image, span)
     over2 = over_call(mark, cross_tile, image)
+    partial = second_diagonal_call(tile, lower_tile, row_sums, noise, image, got)
     own2, sums = second_call(
-        devices,
-        mark,
-        tile,
-        cross_tile,
-        row_sums,
-        noise,
-        direction,
-        next_dir,
-        image,
-        part,
-        over,
-        got,
-        over2,
+        devices, mark, cross_tile, direction, next_dir, image, part, over, over2, partial
     )
     image2 = own2 + moved(over2, 1)
-    images2 = {0: image2, 1: exchanged(image2, 1)}
+    images2 = {0: image2}
     for span in spans:
         images2[span] = exchanged(image2, span)
     image2, images, sums = lax.optimization_barrier((image2, images, sums))
     sums = lax.all_to_all(sums, BOTH, 0, 0)
-    images2, images, sums = lax.optimization_barrier((images2, images, sums))
+    images, images2, sums = lax.optimization_barrier((images, images2, sums))
     for held in (images, images2):
         for span in spans:
             for at in range(1, span):
@@ -781,7 +829,7 @@
     groups = mesh.shape["blk"]
 
     def chosen(features, *rest):
-        one_block_each = features.shape[1] == members * BS and BS % CHUNK == 0
+        one_block_each = features.shape[1] == members * BS and BS % CHUNK == 0 and BS > UPPER_STRIPS * CHUNK
         powers = members > 1 and members & (members - 1) == 0 and groups & (groups - 1) == 0
         each = own_block_body if one_block_each and powers else body
         return each(features, *rest)

time: 70.2 us -> 69.2 us (0.986); the launches traced: 69.4 us -> 69.2 us
  waiting for transfers between devices: 1.43 us -> 3.36 us
  starting transfers between devices: 18.6 us -> 17.3 us
    pallas_call x3 -> x5, Pallas kernels: 17.1 us -> 22 us  [the longest x1 12 us: crossing_call(): pl.pallas_call(crossing_kernel, in_specs=[SMEM] + [VMEM] * len(arrays), o...]
    ppermute x3, starting transfers between devices: 8.19 us -> 4.34 us  [moved(): return lax.ppermute(x, BOTH, route)]
    pallas_call x1, Pallas kernels: 6.46 us -> 3.53 us  [diagonal_call(): pl.pallas_call(diagonal_kernel, in_specs=[SMEM, VMEM, VMEM, VMEM], out_sp...]
    ppermute x9 -> x8, waiting for transfers between devices: 1.42 us -> 3.35 us  [exchanged(): return lax.ppermute(x, BOTH, [(i, i ^ distance) for i in range(count)])]
    ppermute x9 -> x8, starting transfers between devices: 9.67 us -> 11.6 us  [exchanged(): return lax.ppermute(x, BOTH, [(i, i ^ distance) for i in range(count)])]
    pallas_call x1, Pallas kernels: 5.58 us -> 3.75 us  [second_call(): pl.pallas_call(second_kernel, in_specs=[VMEM] * len(arrays), out_specs=[V...]
  transfers between devices with their start and end apart: 13 -> 13, of which waited for: 2 -> 4; matrix products, arithmetic and copies ran while one was open for 0% -> 0% of each run, Pallas kernels for 20% -> 21%
where the time goes in v4:
time: 69.2 us
  Pallas kernels  31 us (45%)
  starting transfers between devices  17.3 us (25%)
  blocking collectives  15.8 us (23%)
  waiting for transfers between devices  3.36 us (5%)
  between operations  1.61 us (2%)
    all_to_all x1, blocking collectives, own_block_body(): sums = lax.all_to_all(sums, BOTH, 0, 0)  15.8 us
    pallas_call x1, Pallas kernels, crossing_call(): pl.pallas_call(crossing_kernel, in_specs=[SMEM] + [VMEM] * len(arrays), o...  12 us
    ppermute x8, starting transfers between devices, exchanged(): return lax.ppermute(x, BOTH, [(i, i ^ distance) for i in range(count)])  11.6 us
    ppermute x3, starting transfers between devices, moved(): return lax.ppermute(x, BOTH, route)  4.34 us
    pallas_call x1, Pallas kernels, second_call(): pl.pallas_call(second_kernel, in_specs=[VMEM] * len(arrays), out_specs=[V...  3.75 us
    pallas_call x1, Pallas kernels, diagonal_call(): pl.pallas_call(diagonal_kernel, in_specs=[SMEM, VMEM, VMEM, VMEM], out_sp...  3.53 us
    pallas_call x1, Pallas kernels, lower_diagonal_call(): pl.pallas_call(lower_diagonal_kernel, in_specs=[SMEM] + [VMEM] * 5, out_s...  3.46 us
    ppermute x8, waiting for transfers between devices, exchanged(): return lax.ppermute(x, BOTH, [(i, i ^ distance) for i in range(count)])  3.35 us
  transfers between devices with their start and end apart: 13, of which 4 were waited for; matrix products, arithmetic and copies ran while one was open for 0% of the time, Pallas kernels for 21%

profile of v4, /device:TPU:0, one launch (start us, length us, event | category | flops | bytes accessed | tf_op | source)
XLA Modules:
  0.0 69.2 jit_solution(7971348450911523708)
XLA Ops:
  0.6 1.8 %shard_map.77 = (f32[48,2048]{1,0:T(8,128)S(1)}, f32[48,2048]{1,0:T(8,128)S(1)}, f32[64,2048]{1,0:T(8,128)S(1)}, f32[32,2048]{1,0:T(8,128)S(1)}, f32[64,2048]{1,...) custom-call(f32[64,8192]{1,0:T(8,128)} %features.1, ...), custom_call_target="tpu_custom_call" | custom-call | tf_op jit(solution)/shard_map/pallas_call | solution.py:488
  2.4 0.7 collective-permute-start.2
  3.1 0.7 collective-permute-start.3
  3.8 3.0 %collective-permute-start = (f32[8,128]{1,0:T(8,128)S(1)}, f32[8,128]{1,0:T(8,128)S(1)}, u32[]{:S(2)}, u32[]{:S(2)}) collective-permute-start(f32[8,128]{1,0:T(8,128)S(1)} %get-tuple-element.39), channel_id=1, source_target_pairs={{0,2},{1,3},{2,0},{3,1},{4,6},{5,7},{6,4},{7,5},{8,10},{9,11},{10,... | collective-permute-start | bytes 12296 | tf_op jit(solution)/shard_map/ppermute | solution.py:626
  7.5 3.5 %shard_map.78 = (bf16[512,2048]{1,0:T(8,128)(2,1)S(1)}, f32[32,2048]{1,0:T(8,128)S(1)}, bf16[2048,256]{1,0:T(8,128)(2,1)S(1)}, bf16[256,2048]{1,0:T(8,128)(2,1)S(1)}, bf16[32,2048]{1,0:T(8,128)(2,1)S(1)}) custom-call(f32[1]{0:T(128)S(6)} %copy.8.signal, f32[64,2048]{1,0:T(8,128)S(1)} %get-tuple-element.40.raw, f32[1,64]{1,0:T(1,128)S(1)} %get-tuple-element.41.scale, ...), custom_call_target="tpu_custom_call" | custom-call | tf_op jit(solution)/shard_map/pallas_call | solution.py:504
  11.1 0.0 collective-permute-done
  11.1 0.8 %collective-permute-start.1 = (f32[8,128]{1,0:T(8,128)S(1)}, f32[8,128]{1,0:T(8,128)S(1)}, u32[]{:S(2)}, u32[]{:S(2)}) collective-permute-start(f32[8,128]{1,0:T(8,128)S(1)} %add.12), channel_id=1, source_target_pairs={{0,1},{1,0},{2,3},{3,2},{4,5},{5,4},{6,7},{7,6},{8,9},{9,8},{10,11... | collective-permute-start | bytes 12296 | tf_op jit(solution)/shard_map/ppermute | solution.py:626
  11.9 0.8 %collective-permute-done.1 = f32[8,128]{1,0:T(8,128)S(1)} collective-permute-done((f32[8,128]{1,0:T(8,128)S(1)}, f32[8,128]{1,0:T(8,128)S(1)}, u32[]{:S(2)}, u32[]{:S(2)}) %collective-permute-start.1) | collective-permute-done | bytes 4128 | tf_op jit(solution)/shard_map/ppermute | solution.py:626
  12.8 0.0 collective-permute-done.2.sent
  12.8 0.0 collective-permute-done.3.sent_rest
  12.8 12.0 %shard_map.79 = (bf16[2048,2048]{1,0:T(8,128)(2,1)S(1)}, f32[8,2048]{1,0:T(8,128)S(1)}, f32[32,2048]{1,0:T(8,128)S(1)}, f32[40,2048]{1,0:T(8,128)S(1)}, f32[32,2048]{1,0:T(8,128)S(1)}, /*index=5*/f32[8,128]{1,0:T(8,128)S(1)}) custom-call(f32[1]{0:T(128)S(6)} %copy.8.signal, f32[8,128]{1,0:T(8,128)S(1)} %add.13.found, ...), custom_call_target="tpu_custom_call" | custom-call | tf_op jit(solution)/shard_map/pallas_call | solution.py:536
  24.7 1.5 %collective-permute-start.4 = (f32[40,2048]{1,0:T(8,128)S(1)}, f32[40,2048]{1,0:T(8,128)S(1)}, u32[]{:S(2)}, u32[]{:S(2)}) collective-permute-start(f32[40,2048]{1,0:T(8,128)S(1)} %get-tuple-element.59.over), channel_id=1, source_target_pairs={{0,1},{1,2},{2,3},{3,7},{7,6},{6,5},{5,4},{4,8},{8,9},{9,10},{10,1... | collective-permute-start | bytes 983048 | tf_op jit(solution)/shard_map/ppermute | solution.py:621
  26.3 3.5 %shard_map.80 = (bf16[1536,2048]{1,0:T(8,128)(2,1)S(1)}, f32[32,2048]{1,0:T(8,128)S(1)}) custom-call(f32[1]{0:T(128)S(6)} %copy.8.signal, bf16[2048,256]{1,0:T(8,128)(2,1)S(1)} %get-tuple-element.49.left, bf16[256,2048]{1,0:T(8,128)(2,1)S(1)} %get-tuple-element.55.right, bf16[32,2048]{1,0:T(8,128)(2,1)S(1)} %get-tuple-element.50.half, ...), custom_call_target="tpu_custom_call" | custom-call | tf_op jit(solution)/shard_map/pallas_call | solution.py:522
  29.7 1.3 %collective-permute-start.5 = (f32[32,2048]{1,0:T(8,128)S(1)}, f32[32,2048]{1,0:T(8,128)S(1)}, u32[]{:S(2)}, u32[]{:S(2)}) collective-permute-start(f32[32,2048]{1,0:T(8,128)S(1)} %get-tuple-element.58), channel_id=1, source_target_pairs={{1,0},{2,1},{3,2},{7,3},{6,7},{5,6},{4,5},{8,4},{9,8},{10,9},{11,1... | collective-permute-start | bytes 786440 | tf_op jit(solution)/shard_map/ppermute | solution.py:621
  31.0 0.0 collective-permute-done.4.got
  31.1 1.7 %shard_map.81.over2 = f32[32,2048]{1,0:T(8,128)S(1)} custom-call(f32[8,128]{1,0:T(8,128)S(1)} %get-tuple-element.52.mark, bf16[2048,2048]{1,0:T(8,128)(2,1)S(1)} %get-tuple-element.53.tile.cross_tile, f32[32,2048]{1,0:T(8,128)S(1)} %slice_add_fusion.image.rest_0_), custom_call_target="tpu_custom_call" | custom-call | tf_op jit(solution)/shard_map/pallas_call | solution.py:560
  32.8 1.5 %collective-permute-start.6 = (f32[32,2048]{1,0:T(8,128)S(1)}, f32[32,2048]{1,0:T(8,128)S(1)}, u32[]{:S(2)}, u32[]{:S(2)}) collective-permute-start(f32[32,2048]{1,0:T(8,128)S(1)} %shard_map.81.over2), channel_id=1, source_target_pairs={{0,1},{1,2},{2,3},{3,7},{7,6},{6,5},{5,4},{4,8},{8,9},{9,10},{10,1... | collective-permute-start | bytes 786440 | tf_op jit(solution)/shard_map/ppermute | solution.py:621
  34.3 0.1 collective-permute-start.7
  34.4 7.0 %collective-permute-start.8 = (f32[32,2048]{1,0:T(8,128)S(1)}, f32[32,2048]{1,0:T(8,128)S(1)}, u32[]{:S(2)}, u32[]{:S(2)}) collective-permute-start(f32[32,2048]{1,0:T(8,128)S(1)} %slice_add_fusion.image.rest_0_), channel_id=1, source_target_pairs={{0,2},{1,3},{2,0},{3,1},{4,6},{5,7},{6,4},{7,5},{8,10},{9,11},{10,... | collective-permute-start | bytes 786440 | tf_op jit(solution)/shard_map/ppermute | solution.py:626
  41.3 2.0 %shard_map.82.partial = f32[32,2048]{1,0:T(8,128)S(1)} custom-call(bf16[512,2048]{1,0:T(8,128)(2,1)S(1)} %get-tuple-element.60.upper, bf16[1536,2048]{1,0:T(8,128)(2,1)S(1)} %get-tuple-element.61.lower, f32[8,2048]{1,0:T(8,128)S(1)} %get-tuple-element.62.row_sums, f32[1,2048]{1,0:T(1,128)S(1)} %get-tuple-element.51.noise, ...), custom_call_target="tpu_custom_call" | custom-call | tf_op jit(solution)/shard_map/pallas_call | solution.py:571
  43.3 0.0 copy-start
  43.3 0.0 collective-permute-done.5.part
  43.4 3.7 %shard_map.83 = (f32[32,2048]{1,0:T(8,128)S(1)}, f32[32,8,128]{2,1,0:T(8,128)S(1)}) custom-call(f32[8,128]{1,0:T(8,128)S(1)} %get-tuple-element.52.mark, bf16[2048,2048]{1,0:T(8,128)(2,1)S(1)} %get-tuple-element.53.tile.cross_tile, f32[32,2048]{1,0:T(8,128)S(1)} %get-tuple-element.42.direction, f32[32,2048]{1,0:T(8,128)S(1)} %get-tuple-element.54.next_dir, ...), custom_call_target="tpu_custom_call" | custom-call | tf_op jit(solution)/shard_map/pallas_call | solution.py:583
  47.1 0.0 collective-permute-done.6
  47.2 0.1 collective-permute-start.10
  47.2 0.1 collective-permute-start.9
  47.3 0.0 collective-permute-done.7.rest_1_
  47.3 1.1 %collective-permute-done.8.rest_2_ = f32[32,2048]{1,0:T(8,128)S(1)} collective-permute-done((f32[32,2048]{1,0:T(8,128)S(1)}, f32[32,2048]{1,0:T(8,128)S(1)}, u32[]{:S(2)}, u32[]{:S(2)}) %collective-permute-start.8) | collective-permute-done | bytes 262176 | tf_op jit(solution)/shard_map/ppermute | solution.py:626
  48.4 15.8 %all_to_all.5.sums = f32[32,8,128]{2,1,0:T(8,128)S(1)} all-to-all(f32[32,8,128]{2,1,0:T(8,128)S(1)} %get-tuple-element.68), channel_id=1, replica_groups=mesh['blk'=8,'pair'=4] {'blk','pair'}, dimensions={0} | all-to-all | bytes 262144 | tf_op jit(solution)/shard_map/all_to_all | solution.py:680
  64.3 0.0 collective-permute-done.10.rest_6_
  64.3 0.0 collective-permute-done.9.rest_5_
  64.3 0.2 collective-permute-start.11
  64.5 0.3 collective-permute-start.12
  64.8 1.0 %collective-permute-done.11.rest_3_ = f32[32,2048]{1,0:T(8,128)S(1)} collective-permute-done((f32[32,2048]{1,0:T(8,128)S(1)}, f32[32,2048]{1,0:T(8,128)S(1)}, u32[]{:S(2)}, u32[]{:S(2)}) %collective-permute-start.11) | collective-permute-done | bytes 262176 | tf_op jit(solution)/shard_map/ppermute | solution.py:626
  65.8 0.4 collective-permute-done.12.rest_7_
  66.2 0.0 copy-done
  66.2 2.8 %shard_map.84 = (f32[32,8192]{1,0:T(8,128)}, f32[32,8192]{1,0:T(8,128)}) custom-call(f32[32,8,128]{2,1,0:T(8,128)S(1)} %all_to_all.5.sums, f32[32,8192]{1,0:T(8,128)S(1)} %copy-done, f32[32,2048]{1,0:T(8,128)S(1)} %slice_add_fusion.image.rest_0_, f32[32,2048]{1,0:T(8,128)S(1)} %collective-permute-done.7.rest_1_, ...), custom_call_target="tpu_custom_call" | custom-call | tf_op jit(solution)/shard_map/pallas_call | solution.py:596
  (4 shorter events, 0.1 us)
Async XLA Ops:
  2.4 10.3 %collective-permute-start.2 = (f32[48,2048]{1,0:T(8,128)S(1)}, f32[48,2048]{1,0:T(8,128)S(1)}, u32[]{:S(2)}, u32[]{:S(2)}) collective-permute-start(f32[48,2048]{1,0:T(8,128)S(1)} %get-tuple-element.47), channel_id=1, source_target_pairs={{7,3},{8,4},{15,11},{16,12},{23,19},{24,20},{31,27}} | collective-permute-start | bytes 1179656 | tf_op jit(solution)/shard_map/ppermute | solution.py:635
  3.1 9.6 %collective-permute-start.3 = (f32[48,2048]{1,0:T(8,128)S(1)}, f32[48,2048]{1,0:T(8,128)S(1)}, u32[]{:S(2)}, u32[]{:S(2)}) collective-permute-start(f32[48,2048]{1,0:T(8,128)S(1)} %get-tuple-element.48), channel_id=1, source_target_pairs={{5,3},{10,4},{13,11},{18,12},{21,19},{26,20},{29,27}} | collective-permute-start | bytes 1179656 | tf_op jit(solution)/shard_map/ppermute | solution.py:635
  3.8 7.2 %collective-permute-start = (f32[8,128]{1,0:T(8,128)S(1)}, f32[8,128]{1,0:T(8,128)S(1)}, u32[]{:S(2)}, u32[]{:S(2)}) collective-permute-start(f32[8,128]{1,0:T(8,128)S(1)} %get-tuple-element.39), channel_id=1, source_target_pairs={{0,2},{1,3},{2,0},{3,1},{4,6},{5,7},{6,4},{7,5},{8,10},{9,11},{10,... | collective-permute-start | bytes 12296 | tf_op jit(solution)/shard_map/ppermute | solution.py:626
  11.1 1.7 %collective-permute-start.1 = (f32[8,128]{1,0:T(8,128)S(1)}, f32[8,128]{1,0:T(8,128)S(1)}, u32[]{:S(2)}, u32[]{:S(2)}) collective-permute-start(f32[8,128]{1,0:T(8,128)S(1)} %add.12), channel_id=1, source_target_pairs={{0,1},{1,0},{2,3},{3,2},{4,5},{5,4},{6,7},{7,6},{8,9},{9,8},{10,11... | collective-permute-start | bytes 12296 | tf_op jit(solution)/shard_map/ppermute | solution.py:626
  24.7 6.3 %collective-permute-start.4 = (f32[40,2048]{1,0:T(8,128)S(1)}, f32[40,2048]{1,0:T(8,128)S(1)}, u32[]{:S(2)}, u32[]{:S(2)}) collective-permute-start(f32[40,2048]{1,0:T(8,128)S(1)} %get-tuple-element.59.over), channel_id=1, source_target_pairs={{0,1},{1,2},{2,3},{3,7},{7,6},{6,5},{5,4},{4,8},{8,9},{9,10},{10,1... | collective-permute-start | bytes 983048 | tf_op jit(solution)/shard_map/ppermute | solution.py:621
  29.7 13.6 %collective-permute-start.5 = (f32[32,2048]{1,0:T(8,128)S(1)}, f32[32,2048]{1,0:T(8,128)S(1)}, u32[]{:S(2)}, u32[]{:S(2)}) collective-permute-start(f32[32,2048]{1,0:T(8,128)S(1)} %get-tuple-element.58), channel_id=1, source_target_pairs={{1,0},{2,1},{3,2},{7,3},{6,7},{5,6},{4,5},{8,4},{9,8},{10,9},{11,1... | collective-permute-start | bytes 786440 | tf_op jit(solution)/shard_map/ppermute | solution.py:621
  32.8 14.4 %collective-permute-start.6 = (f32[32,2048]{1,0:T(8,128)S(1)}, f32[32,2048]{1,0:T(8,128)S(1)}, u32[]{:S(2)}, u32[]{:S(2)}) collective-permute-start(f32[32,2048]{1,0:T(8,128)S(1)} %shard_map.81.over2), channel_id=1, source_target_pairs={{0,1},{1,2},{2,3},{3,7},{7,6},{6,5},{5,4},{4,8},{8,9},{9,10},{10,1... | collective-permute-start | bytes 786440 | tf_op jit(solution)/shard_map/ppermute | solution.py:621
  34.3 13.0 %collective-permute-start.7 = (f32[32,2048]{1,0:T(8,128)S(1)}, f32[32,2048]{1,0:T(8,128)S(1)}, u32[]{:S(2)}, u32[]{:S(2)}) collective-permute-start(f32[32,2048]{1,0:T(8,128)S(1)} %slice_add_fusion.image.rest_0_), channel_id=1, source_target_pairs={{0,1},{1,0},{2,3},{3,2},{4,5},{5,4},{6,7},{7,6},{8,9},{9,8},{10,11... | collective-permute-start | bytes 786440 | tf_op jit(solution)/shard_map/ppermute | solution.py:626
  34.4 14.1 %collective-permute-start.8 = (f32[32,2048]{1,0:T(8,128)S(1)}, f32[32,2048]{1,0:T(8,128)S(1)}, u32[]{:S(2)}, u32[]{:S(2)}) collective-permute-start(f32[32,2048]{1,0:T(8,128)S(1)} %slice_add_fusion.image.rest_0_), channel_id=1, source_target_pairs={{0,2},{1,3},{2,0},{3,1},{4,6},{5,7},{6,4},{7,5},{8,10},{9,11},{10,... | collective-permute-start | bytes 786440 | tf_op jit(solution)/shard_map/ppermute | solution.py:626
  43.3 22.9 %copy-start = (f32[32,8192]{1,0:T(8,128)S(1)}, f32[32,8192]{1,0:T(8,128)}, u32[]{:S(2)}) copy-start(f32[32,8192]{1,0:T(8,128)} %right_side.3) | copy-start | bytes 3145732
  47.2 17.1 %collective-permute-start.10 = (f32[32,2048]{1,0:T(8,128)S(1)}, f32[32,2048]{1,0:T(8,128)S(1)}, u32[]{:S(2)}, u32[]{:S(2)}) collective-permute-start(f32[32,2048]{1,0:T(8,128)S(1)} %add.15.rest_4_), channel_id=1, source_target_pairs={{0,2},{1,3},{2,0},{3,1},{4,6},{5,7},{6,4},{7,5},{8,10},{9,11},{10,... | collective-permute-start | bytes 786440 | tf_op jit(solution)/shard_map/ppermute | solution.py:626
  47.2 17.1 %collective-permute-start.9 = (f32[32,2048]{1,0:T(8,128)S(1)}, f32[32,2048]{1,0:T(8,128)S(1)}, u32[]{:S(2)}, u32[]{:S(2)}) collective-permute-start(f32[32,2048]{1,0:T(8,128)S(1)} %add.15.rest_4_), channel_id=1, source_target_pairs={{0,1},{1,0},{2,3},{3,2},{4,5},{5,4},{6,7},{7,6},{8,9},{9,8},{10,11... | collective-permute-start | bytes 786440 | tf_op jit(solution)/shard_map/ppermute | solution.py:626
  64.3 1.5 %collective-permute-start.11 = (f32[32,2048]{1,0:T(8,128)S(1)}, f32[32,2048]{1,0:T(8,128)S(1)}, u32[]{:S(2)}, u32[]{:S(2)}) collective-permute-start(f32[32,2048]{1,0:T(8,128)S(1)} %collective-permute-done.8.rest_2_), channel_id=1, source_target_pairs={{0,1},{1,0},{2,3},{3,2},{4,5},{5,4},{6,7},{7,6},{8,9},{9,8},{10,11... | collective-permute-start | bytes 786440 | tf_op jit(solution)/shard_map/ppermute | solution.py:626
  64.5 1.7 %collective-permute-start.12 = (f32[32,2048]{1,0:T(8,128)S(1)}, f32[32,2048]{1,0:T(8,128)S(1)}, u32[]{:S(2)}, u32[]{:S(2)}) collective-permute-start(f32[32,2048]{1,0:T(8,128)S(1)} %collective-permute-done.10.rest_6_), channel_id=1, source_target_pairs={{0,1},{1,0},{2,3},{3,2},{4,5},{5,4},{6,7},{7,6},{8,9},{9,8},{10,11... | collective-permute-start | bytes 786440 | tf_op jit(solution)/shard_map/ppermute | solution.py:626

commit v5 on v4

--- a/solution.py
+++ b/solution.py
@@ -460,6 +460,12 @@
     return pltpu.CompilerParams(vmem_limit_bytes=mebibytes << 20)
 
 
+def taking(microseconds):
+    return pl.CostEstimate(
+        flops=int(microseconds * 1.0e9), transcendentals=0, bytes_accessed=int(microseconds * 3.0e6)
+    )
+
+
 def shaped(*shape):
     return jax.ShapeDtypeStruct(shape, f32)
 
@@ -494,6 +500,7 @@
             pltpu.VMEM(block_pairs.shape, jnp.int32),
             pltpu.SemaphoreType.DMA((len(shapes) + 1,)),
         ],
+        cost_estimate=taking(2),
         compiler_params=params(16),
     )(features, right_side, noise_var, inv_scale, block_pairs)
 
@@ -513,6 +520,7 @@
             pltpu.VMEM((probes, size), bf16),
         ],
         scratch_shapes=[pltpu.VMEM((2, CHUNK, CHUNK), f32)],
+        cost_estimate=taking(4),
         compiler_params=params(16),
     )(signal, raw, scale, direction)
 
@@ -525,6 +533,7 @@
         out_specs=[VMEM] * 2,
         out_shape=[pltpu.VMEM((rows, size), bf16), pltpu.VMEM((probes, size), f32)],
         scratch_shapes=[pltpu.VMEM((2, CHUNK, CHUNK), f32)],
+        cost_estimate=taking(4),
         compiler_params=params(16),
     )(signal, left, right, half, upper, crossed)
 
@@ -552,6 +561,7 @@
             pltpu.VMEM((8, size), f32),
             pltpu.VMEM((size, 128), f32),
         ],
+        cost_estimate=taking(12),
         compiler_params=params(16),
     )(signal, *arrays)
 
@@ -562,6 +572,7 @@
         in_specs=[VMEM] * 3,
         out_specs=VMEM,
         out_shape=pltpu.VMEM(image.shape, f32),
+        cost_estimate=taking(2),
         compiler_params=params(16),
     )(mark, tile, image)
 
@@ -574,6 +585,7 @@
         out_specs=VMEM,
         out_shape=pltpu.VMEM((probes, size), f32),
         scratch_shapes=[pltpu.VMEM((2 * probes, size), bf16)],
+        cost_estimate=taking(2),
         compiler_params=params(16),
     )(upper, lower, row_sums, noise, image, got)
 
@@ -585,6 +597,7 @@
         in_specs=[VMEM] * len(arrays),
         out_specs=[VMEM] * 2,
         out_shape=[pltpu.VMEM((probes, size), f32), pltpu.VMEM((devices, 8, 128), f32)],
+        cost_estimate=taking(4),
         compiler_params=params(16),
     )(*arrays)
 
@@ -603,6 +616,7 @@
             pltpu.VMEM((members, probes, size), f32),
             pltpu.SemaphoreType.DMA((2, members)),
         ],
+        cost_estimate=taking(3),
         compiler_params=params(16),
     )(sums, right_side, *images, *images2)
 

time: 69.2 us -> 67.1 us (0.970); the launches traced: 69.2 us -> 67.8 us
  blocking collectives: 15.8 us -> 13.5 us
  starting transfers between devices: 17.3 us -> 19.4 us
  waiting for transfers between devices: 3.36 us -> 2.26 us
    all_to_all x1, blocking collectives: 15.8 us -> 13.5 us  [own_block_body(): sums = lax.all_to_all(sums, BOTH, 0, 0)]
    ppermute x8, starting transfers between devices: 11.6 us -> 13.9 us  [exchanged(): return lax.ppermute(x, BOTH, [(i, i ^ distance) for i in range(count)])]
    ppermute x8, waiting for transfers between devices: 3.35 us -> 2.24 us  [exchanged(): return lax.ppermute(x, BOTH, [(i, i ^ distance) for i in range(count)])]
  transfers between devices with their start and end apart: 13 -> 13, of which waited for: 4 -> 3; matrix products, arithmetic and copies ran while one was open for 0% -> 0% of each run, Pallas kernels for 21% -> 21%
where the time goes in v5:
time: 67.1 us; the launch traced here: 67.8 us
  Pallas kernels  31 us (46%)
  starting transfers between devices  19.4 us (29%)
  blocking collectives  13.5 us (20%)
  waiting for transfers between devices  2.26 us (3%)
  between operations  1.59 us (2%)
    ppermute x8, starting transfers between devices, exchanged(): return lax.ppermute(x, BOTH, [(i, i ^ distance) for i in range(count)])  13.9 us
    all_to_all x1, blocking collectives, own_block_body(): sums = lax.all_to_all(sums, BOTH, 0, 0)  13.5 us
    pallas_call x1, Pallas kernels, crossing_call(): pl.pallas_call(crossing_kernel, in_specs=[SMEM] + [VMEM] * len(arrays), o...  12 us
    ppermute x3, starting transfers between devices, moved(): return lax.ppermute(x, BOTH, route)  4.14 us
    pallas_call x1, Pallas kernels, second_call(): pl.pallas_call(second_kernel, in_specs=[VMEM] * len(arrays), out_specs=[V...  3.74 us
    pallas_call x1, Pallas kernels, diagonal_call(): pl.pallas_call(diagonal_kernel, in_specs=[SMEM, VMEM, VMEM, VMEM], out_sp...  3.53 us
    pallas_call x1, Pallas kernels, lower_diagonal_call(): pl.pallas_call(lower_diagonal_kernel, in_specs=[SMEM] + [VMEM] * 5, out_s...  3.47 us
    pallas_call x1, Pallas kernels, final_call(): pl.pallas_call(final_kernel, in_specs=[VMEM] * (2 + 2 * members), out_spe...  2.8 us
  transfers between devices with their start and end apart: 13, of which 3 were waited for; matrix products, arithmetic and copies ran while one was open for 0% of the time, Pallas kernels for 21%

profile of v5, /device:TPU:0, one launch (start us, length us, event | category | flops | bytes accessed | tf_op | source)
XLA Modules:
  0.0 67.8 jit_solution(12947661738278424019)
XLA Ops:
  0.6 1.8 %shard_map.77 = (f32[48,2048]{1,0:T(8,128)S(1)}, f32[48,2048]{1,0:T(8,128)S(1)}, f32[64,2048]{1,0:T(8,128)S(1)}, f32[32,2048]{1,0:T(8,128)S(1)}, f32[64,2048]{1,...) custom-call(f32[64,8192]{1,0:T(8,128)} %features.1, ...), custom_call_target="tpu_custom_call" | custom-call | flops 2000000000 | bytes 6000000 | tf_op jit(solution)/shard_map/pallas_call | solution.py:494
  2.4 0.7 %collective-permute-start.2 = (f32[48,2048]{1,0:T(8,128)S(1)}, f32[48,2048]{1,0:T(8,128)S(1)}, u32[]{:S(2)}, u32[]{:S(2)}) collective-permute-start(f32[48,2048]{1,0:T(8,128)S(1)} %get-tuple-element.47), channel_id=1, source_target_pairs={{7,3},{8,4},{15,11},{16,12},{23,19},{24,20},{31,27}} | collective-permute-start | bytes 1179656 | tf_op jit(solution)/shard_map/ppermute | solution.py:649
  3.1 0.7 %collective-permute-start.3 = (f32[48,2048]{1,0:T(8,128)S(1)}, f32[48,2048]{1,0:T(8,128)S(1)}, u32[]{:S(2)}, u32[]{:S(2)}) collective-permute-start(f32[48,2048]{1,0:T(8,128)S(1)} %get-tuple-element.48), channel_id=1, source_target_pairs={{5,3},{10,4},{13,11},{18,12},{21,19},{26,20},{29,27}} | collective-permute-start | bytes 1179656 | tf_op jit(solution)/shard_map/ppermute | solution.py:649
  3.8 3.0 %collective-permute-start = (f32[8,128]{1,0:T(8,128)S(1)}, f32[8,128]{1,0:T(8,128)S(1)}, u32[]{:S(2)}, u32[]{:S(2)}) collective-permute-start(f32[8,128]{1,0:T(8,128)S(1)} %get-tuple-element.39), channel_id=1, source_target_pairs={{0,2},{1,3},{2,0},{3,1},{4,6},{5,7},{6,4},{7,5},{8,10},{9,11},{10,... | collective-permute-start | bytes 12296 | tf_op jit(solution)/shard_map/ppermute | solution.py:640
  7.5 3.5 %shard_map.78 = (bf16[512,2048]{1,0:T(8,128)(2,1)S(1)}, f32[32,2048]{1,0:T(8,128)S(1)}, bf16[2048,256]{1,0:T(8,128)(2,1)S(1)}, bf16[256,2048]{1,0:T(8,128)(2,1)S(1)}, bf16[32,2048]{1,0:T(8,128)(2,1)S(1)}) custom-call(f32[1]{0:T(128)S(6)} %copy.8.signal, f32[64,2048]{1,0:T(8,128)S(1)} %get-tuple-element.40.raw, f32[1,64]{1,0:T(1,128)S(1)} %get-tuple-element.41.scale, ...), custom_call_target="tpu_custom_call" | custom-call | flops 4000000000 | bytes 12000000 | tf_op jit(solution)/shard_map/pallas_call | solution.py:511
  11.1 0.0 collective-permute-done
  11.1 0.8 %collective-permute-start.1 = (f32[8,128]{1,0:T(8,128)S(1)}, f32[8,128]{1,0:T(8,128)S(1)}, u32[]{:S(2)}, u32[]{:S(2)}) collective-permute-start(f32[8,128]{1,0:T(8,128)S(1)} %add.12), channel_id=1, source_target_pairs={{0,1},{1,0},{2,3},{3,2},{4,5},{5,4},{6,7},{7,6},{8,9},{9,8},{10,11... | collective-permute-start | bytes 12296 | tf_op jit(solution)/shard_map/ppermute | solution.py:640
  11.9 0.8 %collective-permute-done.1 = f32[8,128]{1,0:T(8,128)S(1)} collective-permute-done((f32[8,128]{1,0:T(8,128)S(1)}, f32[8,128]{1,0:T(8,128)S(1)}, u32[]{:S(2)}, u32[]{:S(2)}) %collective-permute-start.1) | collective-permute-done | bytes 4128 | tf_op jit(solution)/shard_map/ppermute | solution.py:640
  12.8 0.0 collective-permute-done.2.sent
  12.8 0.0 collective-permute-done.3.sent_rest
  12.8 12.0 %shard_map.79 = (bf16[2048,2048]{1,0:T(8,128)(2,1)S(1)}, f32[8,2048]{1,0:T(8,128)S(1)}, f32[32,2048]{1,0:T(8,128)S(1)}, f32[40,2048]{1,0:T(8,128)S(1)}, f32[32,2048]{1,0:T(8,128)S(1)}, /*index=5*/f32[8,128]{1,0:T(8,128)S(1)}) custom-call(f32[1]{0:T(128)S(6)} %copy.8.signal, f32[8,128]{1,0:T(8,128)S(1)} %add.13.found, ...), custom_call_target="tpu_custom_call" | custom-call | flops 12000000000 | bytes 36000000 | tf_op jit(solution)/shard_map/pallas_call | solution.py:545
  24.7 1.5 %collective-permute-start.4 = (f32[40,2048]{1,0:T(8,128)S(1)}, f32[40,2048]{1,0:T(8,128)S(1)}, u32[]{:S(2)}, u32[]{:S(2)}) collective-permute-start(f32[40,2048]{1,0:T(8,128)S(1)} %get-tuple-element.59.over), channel_id=1, source_target_pairs={{0,1},{1,2},{2,3},{3,7},{7,6},{6,5},{5,4},{4,8},{8,9},{9,10},{10,1... | collective-permute-start | bytes 983048 | tf_op jit(solution)/shard_map/ppermute | solution.py:635
  26.3 3.5 %shard_map.80 = (bf16[1536,2048]{1,0:T(8,128)(2,1)S(1)}, f32[32,2048]{1,0:T(8,128)S(1)}) custom-call(f32[1]{0:T(128)S(6)} %copy.8.signal, bf16[2048,256]{1,0:T(8,128)(2,1)S(1)} %get-tuple-element.49.left, bf16[256,2048]{1,0:T(8,128)(2,1)S(1)} %get-tuple-element.55.right, bf16[32,2048]{1,0:T(8,128)(2,1)S(1)} %get-tuple-element.50.half, ...), custom_call_target="tpu_custom_call" | custom-call | flops 4000000000 | bytes 12000000 | tf_op jit(solution)/shard_map/pallas_call | solution.py:530
  29.7 1.3 %collective-permute-start.5 = (f32[32,2048]{1,0:T(8,128)S(1)}, f32[32,2048]{1,0:T(8,128)S(1)}, u32[]{:S(2)}, u32[]{:S(2)}) collective-permute-start(f32[32,2048]{1,0:T(8,128)S(1)} %get-tuple-element.58), channel_id=1, source_target_pairs={{1,0},{2,1},{3,2},{7,3},{6,7},{5,6},{4,5},{8,4},{9,8},{10,9},{11,1... | collective-permute-start | bytes 786440 | tf_op jit(solution)/shard_map/ppermute | solution.py:635
  31.0 0.0 collective-permute-done.4.got
  31.1 1.7 %collective-permute-start.7 = (f32[32,2048]{1,0:T(8,128)S(1)}, f32[32,2048]{1,0:T(8,128)S(1)}, u32[]{:S(2)}, u32[]{:S(2)}) collective-permute-start(f32[32,2048]{1,0:T(8,128)S(1)} %slice_add_fusion.image.rest_0_), channel_id=1, source_target_pairs={{0,1},{1,0},{2,3},{3,2},{4,5},{5,4},{6,7},{7,6},{8,9},{9,8},{10,11... | collective-permute-start | bytes 786440 | tf_op jit(solution)/shard_map/ppermute | solution.py:640
  32.8 3.5 %collective-permute-start.8 = (f32[32,2048]{1,0:T(8,128)S(1)}, f32[32,2048]{1,0:T(8,128)S(1)}, u32[]{:S(2)}, u32[]{:S(2)}) collective-permute-start(f32[32,2048]{1,0:T(8,128)S(1)} %slice_add_fusion.image.rest_0_), channel_id=1, source_target_pairs={{0,2},{1,3},{2,0},{3,1},{4,6},{5,7},{6,4},{7,5},{8,10},{9,11},{10,... | collective-permute-start | bytes 786440 | tf_op jit(solution)/shard_map/ppermute | solution.py:640
  36.3 1.7 %shard_map.81.over2 = f32[32,2048]{1,0:T(8,128)S(1)} custom-call(f32[8,128]{1,0:T(8,128)S(1)} %get-tuple-element.52.mark, bf16[2048,2048]{1,0:T(8,128)(2,1)S(1)} %get-tuple-element.53.tile.cross_tile, f32[32,2048]{1,0:T(8,128)S(1)} %slice_add_fusion.image.rest_0_), custom_call_target="tpu_custom_call" | custom-call | flops 2000000000 | bytes 6000000 | tf_op jit(solution)/shard_map/pallas_call | solution.py:570
  38.0 1.3 %collective-permute-start.6 = (f32[32,2048]{1,0:T(8,128)S(1)}, f32[32,2048]{1,0:T(8,128)S(1)}, u32[]{:S(2)}, u32[]{:S(2)}) collective-permute-start(f32[32,2048]{1,0:T(8,128)S(1)} %shard_map.81.over2), channel_id=1, source_target_pairs={{0,1},{1,2},{2,3},{3,7},{7,6},{6,5},{5,4},{4,8},{8,9},{9,10},{10,1... | collective-permute-start | bytes 786440 | tf_op jit(solution)/shard_map/ppermute | solution.py:635
  39.3 2.0 %shard_map.82.partial = f32[32,2048]{1,0:T(8,128)S(1)} custom-call(bf16[512,2048]{1,0:T(8,128)(2,1)S(1)} %get-tuple-element.60.upper, bf16[1536,2048]{1,0:T(8,128)(2,1)S(1)} %get-tuple-element.61.lower, f32[8,2048]{1,0:T(8,128)S(1)} %get-tuple-element.62.row_sums, f32[1,2048]{1,0:T(1,128)S(1)} %get-tuple-element.51.noise, ...), custom_call_target="tpu_custom_call" | custom-call | flops 2000000000 | bytes 6000000 | tf_op jit(solution)/shard_map/pallas_call | solution.py:582
  41.3 0.0 collective-permute-done.5.part
  41.3 0.0 copy-start
  41.3 3.7 %shard_map.83 = (f32[32,2048]{1,0:T(8,128)S(1)}, f32[32,8,128]{2,1,0:T(8,128)S(1)}) custom-call(f32[8,128]{1,0:T(8,128)S(1)} %get-tuple-element.52.mark, bf16[2048,2048]{1,0:T(8,128)(2,1)S(1)} %get-tuple-element.53.tile.cross_tile, f32[32,2048]{1,0:T(8,128)S(1)} %get-tuple-element.42.direction, f32[32,2048]{1,0:T(8,128)S(1)} %get-tuple-element.54.next_dir, ...), custom_call_target="tpu_custom_call" | custom-call | flops 4000000000 | bytes 12000000 | tf_op jit(solution)/shard_map/pallas_call | solution.py:595
  45.1 0.0 collective-permute-done.6
  45.1 2.4 %collective-permute-start.10 = (f32[32,2048]{1,0:T(8,128)S(1)}, f32[32,2048]{1,0:T(8,128)S(1)}, u32[]{:S(2)}, u32[]{:S(2)}) collective-permute-start(f32[32,2048]{1,0:T(8,128)S(1)} %add.15.rest_4_), channel_id=1, source_target_pairs={{0,2},{1,3},{2,0},{3,1},{4,6},{5,7},{6,4},{7,5},{8,10},{9,11},{10,... | collective-permute-start | bytes 786440 | tf_op jit(solution)/shard_map/ppermute | solution.py:640
  47.5 2.0 %collective-permute-start.9 = (f32[32,2048]{1,0:T(8,128)S(1)}, f32[32,2048]{1,0:T(8,128)S(1)}, u32[]{:S(2)}, u32[]{:S(2)}) collective-permute-start(f32[32,2048]{1,0:T(8,128)S(1)} %add.15.rest_4_), channel_id=1, source_target_pairs={{0,1},{1,0},{2,3},{3,2},{4,5},{5,4},{6,7},{7,6},{8,9},{9,8},{10,11... | collective-permute-start | bytes 786440 | tf_op jit(solution)/shard_map/ppermute | solution.py:640
  49.5 0.0 collective-permute-done.7.rest_1_
  49.5 0.0 collective-permute-done.8.rest_2_
  49.5 13.5 %all_to_all.5.sums = f32[32,8,128]{2,1,0:T(8,128)S(1)} all-to-all(f32[32,8,128]{2,1,0:T(8,128)S(1)} %get-tuple-element.68), channel_id=1, replica_groups=mesh['blk'=8,'pair'=4] {'blk','pair'}, dimensions={0} | all-to-all | bytes 262144 | tf_op jit(solution)/shard_map/all_to_all | solution.py:694
  62.9 0.0 collective-permute-done.10.rest_6_
  62.9 0.0 collective-permute-done.9.rest_5_
  62.9 0.2 collective-permute-start.11
  63.1 0.3 collective-permute-start.12
  63.4 1.0 %collective-permute-done.11.rest_3_ = f32[32,2048]{1,0:T(8,128)S(1)} collective-permute-done((f32[32,2048]{1,0:T(8,128)S(1)}, f32[32,2048]{1,0:T(8,128)S(1)}, u32[]{:S(2)}, u32[]{:S(2)}) %collective-permute-start.11) | collective-permute-done | bytes 262176 | tf_op jit(solution)/shard_map/ppermute | solution.py:640
  64.5 0.4 collective-permute-done.12.rest_7_
  64.8 0.0 copy-done
  64.8 2.8 %shard_map.84 = (f32[32,8192]{1,0:T(8,128)}, f32[32,8192]{1,0:T(8,128)}) custom-call(f32[32,8,128]{2,1,0:T(8,128)S(1)} %all_to_all.5.sums, f32[32,8192]{1,0:T(8,128)S(1)} %copy-done, f32[32,2048]{1,0:T(8,128)S(1)} %slice_add_fusion.image.rest_0_, f32[32,2048]{1,0:T(8,128)S(1)} %collective-permute-done.7.rest_1_, ...), custom_call_target="tpu_custom_call" | custom-call | flops 3000000000 | bytes 9000000 | tf_op jit(solution)/shard_map/pallas_call | solution.py:609
  (4 shorter events, 0.1 us)
Async XLA Ops:
  2.4 10.3 %collective-permute-start.2 = (f32[48,2048]{1,0:T(8,128)S(1)}, f32[48,2048]{1,0:T(8,128)S(1)}, u32[]{:S(2)}, u32[]{:S(2)}) collective-permute-start(f32[48,2048]{1,0:T(8,128)S(1)} %get-tuple-element.47), channel_id=1, source_target_pairs={{7,3},{8,4},{15,11},{16,12},{23,19},{24,20},{31,27}} | collective-permute-start | bytes 1179656 | tf_op jit(solution)/shard_map/ppermute | solution.py:649
  3.1 9.6 %collective-permute-start.3 = (f32[48,2048]{1,0:T(8,128)S(1)}, f32[48,2048]{1,0:T(8,128)S(1)}, u32[]{:S(2)}, u32[]{:S(2)}) collective-permute-start(f32[48,2048]{1,0:T(8,128)S(1)} %get-tuple-element.48), channel_id=1, source_target_pairs={{5,3},{10,4},{13,11},{18,12},{21,19},{26,20},{29,27}} | collective-permute-start | bytes 1179656 | tf_op jit(solution)/shard_map/ppermute | solution.py:649
  3.8 7.2 %collective-permute-start = (f32[8,128]{1,0:T(8,128)S(1)}, f32[8,128]{1,0:T(8,128)S(1)}, u32[]{:S(2)}, u32[]{:S(2)}) collective-permute-start(f32[8,128]{1,0:T(8,128)S(1)} %get-tuple-element.39), channel_id=1, source_target_pairs={{0,2},{1,3},{2,0},{3,1},{4,6},{5,7},{6,4},{7,5},{8,10},{9,11},{10,... | collective-permute-start | bytes 12296 | tf_op jit(solution)/shard_map/ppermute | solution.py:640
  11.1 1.7 %collective-permute-start.1 = (f32[8,128]{1,0:T(8,128)S(1)}, f32[8,128]{1,0:T(8,128)S(1)}, u32[]{:S(2)}, u32[]{:S(2)}) collective-permute-start(f32[8,128]{1,0:T(8,128)S(1)} %add.12), channel_id=1, source_target_pairs={{0,1},{1,0},{2,3},{3,2},{4,5},{5,4},{6,7},{7,6},{8,9},{9,8},{10,11... | collective-permute-start | bytes 12296 | tf_op jit(solution)/shard_map/ppermute | solution.py:640
  24.7 6.3 %collective-permute-start.4 = (f32[40,2048]{1,0:T(8,128)S(1)}, f32[40,2048]{1,0:T(8,128)S(1)}, u32[]{:S(2)}, u32[]{:S(2)}) collective-permute-start(f32[40,2048]{1,0:T(8,128)S(1)} %get-tuple-element.59.over), channel_id=1, source_target_pairs={{0,1},{1,2},{2,3},{3,7},{7,6},{6,5},{5,4},{4,8},{8,9},{9,10},{10,1... | collective-permute-start | bytes 983048 | tf_op jit(solution)/shard_map/ppermute | solution.py:635
  29.7 11.5 %collective-permute-start.5 = (f32[32,2048]{1,0:T(8,128)S(1)}, f32[32,2048]{1,0:T(8,128)S(1)}, u32[]{:S(2)}, u32[]{:S(2)}) collective-permute-start(f32[32,2048]{1,0:T(8,128)S(1)} %get-tuple-element.58), channel_id=1, source_target_pairs={{1,0},{2,1},{3,2},{7,3},{6,7},{5,6},{4,5},{8,4},{9,8},{10,9},{11,1... | collective-permute-start | bytes 786440 | tf_op jit(solution)/shard_map/ppermute | solution.py:635
  31.1 18.4 %collective-permute-start.7 = (f32[32,2048]{1,0:T(8,128)S(1)}, f32[32,2048]{1,0:T(8,128)S(1)}, u32[]{:S(2)}, u32[]{:S(2)}) collective-permute-start(f32[32,2048]{1,0:T(8,128)S(1)} %slice_add_fusion.image.rest_0_), channel_id=1, source_target_pairs={{0,1},{1,0},{2,3},{3,2},{4,5},{5,4},{6,7},{7,6},{8,9},{9,8},{10,11... | collective-permute-start | bytes 786440 | tf_op jit(solution)/shard_map/ppermute | solution.py:640
  32.8 16.7 %collective-permute-start.8 = (f32[32,2048]{1,0:T(8,128)S(1)}, f32[32,2048]{1,0:T(8,128)S(1)}, u32[]{:S(2)}, u32[]{:S(2)}) collective-permute-start(f32[32,2048]{1,0:T(8,128)S(1)} %slice_add_fusion.image.rest_0_), channel_id=1, source_target_pairs={{0,2},{1,3},{2,0},{3,1},{4,6},{5,7},{6,4},{7,5},{8,10},{9,11},{10,... | collective-permute-start | bytes 786440 | tf_op jit(solution)/shard_map/ppermute | solution.py:640
  38.0 7.1 %collective-permute-start.6 = (f32[32,2048]{1,0:T(8,128)S(1)}, f32[32,2048]{1,0:T(8,128)S(1)}, u32[]{:S(2)}, u32[]{:S(2)}) collective-permute-start(f32[32,2048]{1,0:T(8,128)S(1)} %shard_map.81.over2), channel_id=1, source_target_pairs={{0,1},{1,2},{2,3},{3,7},{7,6},{6,5},{5,4},{4,8},{8,9},{9,10},{10,1... | collective-permute-start | bytes 786440 | tf_op jit(solution)/shard_map/ppermute | solution.py:635
  41.3 23.5 %copy-start = (f32[32,8192]{1,0:T(8,128)S(1)}, f32[32,8192]{1,0:T(8,128)}, u32[]{:S(2)}) copy-start(f32[32,8192]{1,0:T(8,128)} %right_side.3) | copy-start | bytes 3145732
  45.1 17.8 %collective-permute-start.10 = (f32[32,2048]{1,0:T(8,128)S(1)}, f32[32,2048]{1,0:T(8,128)S(1)}, u32[]{:S(2)}, u32[]{:S(2)}) collective-permute-start(f32[32,2048]{1,0:T(8,128)S(1)} %add.15.rest_4_), channel_id=1, source_target_pairs={{0,2},{1,3},{2,0},{3,1},{4,6},{5,7},{6,4},{7,5},{8,10},{9,11},{10,... | collective-permute-start | bytes 786440 | tf_op jit(solution)/shard_map/ppermute | solution.py:640
  47.5 15.4 %collective-permute-start.9 = (f32[32,2048]{1,0:T(8,128)S(1)}, f32[32,2048]{1,0:T(8,128)S(1)}, u32[]{:S(2)}, u32[]{:S(2)}) collective-permute-start(f32[32,2048]{1,0:T(8,128)S(1)} %add.15.rest_4_), channel_id=1, source_target_pairs={{0,1},{1,0},{2,3},{3,2},{4,5},{5,4},{6,7},{7,6},{8,9},{9,8},{10,11... | collective-permute-start | bytes 786440 | tf_op jit(solution)/shard_map/ppermute | solution.py:640
  62.9 1.5 %collective-permute-start.11 = (f32[32,2048]{1,0:T(8,128)S(1)}, f32[32,2048]{1,0:T(8,128)S(1)}, u32[]{:S(2)}, u32[]{:S(2)}) collective-permute-start(f32[32,2048]{1,0:T(8,128)S(1)} %collective-permute-done.8.rest_2_), channel_id=1, source_target_pairs={{0,1},{1,0},{2,3},{3,2},{4,5},{5,4},{6,7},{7,6},{8,9},{9,8},{10,11... | collective-permute-start | bytes 786440 | tf_op jit(solution)/shard_map/ppermute | solution.py:640
  63.1 1.7 %collective-permute-start.12 = (f32[32,2048]{1,0:T(8,128)S(1)}, f32[32,2048]{1,0:T(8,128)S(1)}, u32[]{:S(2)}, u32[]{:S(2)}) collective-permute-start(f32[32,2048]{1,0:T(8,128)S(1)} %collective-permute-done.10.rest_6_), channel_id=1, source_target_pairs={{0,1},{1,0},{2,3},{3,2},{4,5},{5,4},{6,7},{7,6},{8,9},{9,8},{10,11... | collective-permute-start | bytes 786440 | tf_op jit(solution)/shard_map/ppermute | solution.py:640

commit v6 on v5

--- a/solution.py
+++ b/solution.py
@@ -143,13 +143,31 @@
     return high, low
 
 
-def lanes_sum(high, low):
-    shift = 64
-    while shift:
-        high, error = two_sum(high, pltpu.roll(high, shift, 1))
-        low = low + pltpu.roll(low, shift, 1) + error
-        shift //= 2
+def rows_sum(high, low):
+    parts = [(high[at : at + 8], low[at : at + 8]) for at in range(0, 128, 8)]
+    while len(parts) > 1:
+        parts = [
+            (total, error + (x[1] + y[1]))
+            for x, y in zip(parts[::2], parts[1::2])
+            for total, error in (two_sum(x[0], y[0]),)
+        ]
+    high, low = parts[0]
+    for shift in (4, 2, 1):
+        high, error = two_sum(high, pltpu.roll(high, shift, 0))
+        low = low + pltpu.roll(low, shift, 0) + error
     return high, low
+
+
+def lane_tiles_plain(x):
+    total = x[:, 0:128]
+    for at in range(128, x.shape[1], 128):
+        total = total + x[:, at : at + 128]
+    return total
+
+
+def padded(pieces):
+    rows = sum(piece.shape[0] for piece in pieces)
+    return jnp.concatenate([*pieces, jnp.zeros((128 - rows, 128), f32)], axis=0)
 
 
 def loading_kernel(
@@ -383,26 +401,17 @@
     mine = own2[...]
     theirs = over2[...]
     squares = here * here
-    forms = [
-        begin * begin,
-        begin * here,
-        squares,
-        squares + begin * mine + next_dir[...] * theirs,
-        here * mine + there * theirs,
+    exact = [lane_tiles_sum(x) for x in (begin * begin, begin * here, squares)]
+    plain = [
+        lane_tiles_plain(x)
+        for x in (squares + begin * mine + next_dir[...] * theirs, here * mine + there * theirs)
     ]
-    pairs = [lane_tiles_sum(x) for x in forms]
-    high, low = lanes_sum(
-        jnp.concatenate([x for x, _ in pairs], axis=0), jnp.concatenate([x for _, x in pairs], axis=0)
-    )
-    rows = [(high, 0), (low, 0), (high, 1), (low, 1), (high, 2), (low, 2), (high, 3), (high, 4)]
-    lane = lax.broadcasted_iota(jnp.int32, (probes, 128), 1)
-    out = jnp.zeros((probes, 128), f32)
-    for k, (values, at) in enumerate(rows):
-        out = jnp.where(lane == k, values[at * probes : (at + 1) * probes], out)
-    square = jnp.concatenate([out, jnp.zeros((128 - probes, 128), f32)], axis=0)
-    turned = square.T[: len(rows)]
+    high, low = rows_sum(padded([x for x, _ in exact]).T, padded([x for _, x in exact]).T)
+    rest = jnp.sum(padded(plain).T, axis=0, keepdims=True)
+    row = lax.broadcasted_iota(jnp.int32, high.shape, 0)
+    tile = jnp.where(row == 0, high, jnp.where(row == 1, low, jnp.where(row == 2, rest, 0.0)))
     for k in range(sums.shape[0]):
-        sums[k] = turned
+        sums[k] = tile
 
 
 def final_kernel(sums, right_side, *rest):
@@ -427,13 +436,12 @@
             joined.append((total, a_error + b_error + missed))
         runs = joined
     total, error = runs[0]
-    empty = jnp.zeros((128 - total.shape[0], 128), f32)
-    total = jnp.concatenate([total, empty], axis=0).T[:probes]
-    error = jnp.concatenate([error, empty], axis=0).T[:probes]
+    total, error = padded([total]).T, padded([error]).T
     square, form, image_square = (
-        (total[:, k : k + 1], total[:, k + 1 : k + 2] + error[:, k : k + 1]) for k in (0, 2, 4)
-    )
-    mixed, image_form = (total[:, k : k + 1] for k in (6, 7))
+        (total[at : at + probes, 0:1], total[at : at + probes, 1:2] + error[at : at + probes, 0:1])
+        for at in (0, probes, 2 * probes)
+    )
+    mixed, image_form = (total[at : at + probes, 2:3] for at in (0, probes))
     alpha = square[0] / form[0]
     new = plus(plus(square, times(form, -2.0 * alpha)), times(times(image_square, alpha), alpha))[0]
     beta = new / square[0]
@@ -664,7 +672,7 @@
     )
     spans = [1 << k for k in range(members.bit_length() - 1)]
     sent = sent_from_next_group(send, 0)
-    sent_rest = sent_from_next_group(send_rest, members // 2)
+    sent_rest = sent_from_next_group(send_rest, members - 1)
     found = found + exchanged(found, spans[-1])
     split = UPPER_STRIPS * CHUNK
     tile, diagonal, left, right, half = diagonal_call(signal, raw, scale, direction, split)
@@ -845,7 +853,8 @@
     def chosen(features, *rest):
         one_block_each = features.shape[1] == members * BS and BS % CHUNK == 0 and BS > UPPER_STRIPS * CHUNK
         powers = members > 1 and members & (members - 1) == 0 and groups & (groups - 1) == 0
-        each = own_block_body if one_block_each and powers else body
+        fitting = 3 * rest[3].shape[0] <= 128 and rest[3].shape[0] % 8 == 0
+        each = own_block_body if one_block_each and powers and fitting else body
         return each(features, *rest)
 
     placed = (P(None, "blk"), P(), P(), P("blk"), P(None, "blk"), P(("blk", "pair"), None))

time: 67.1 us -> 66.8 us (level); the launches traced: 67.8 us -> 66.5 us
  Pallas kernels: 31 us -> 14.2 us
  starting transfers between devices: 19.4 us -> 34.6 us
    ppermute x3, starting transfers between devices: 4.14 us -> 18.6 us  [moved(): return lax.ppermute(x, BOTH, route)]
    pallas_call x1, Pallas kernels: 12 us -> 0.38 us  [crossing_call(): pl.pallas_call(crossing_kernel, in_specs=[SMEM] + [VMEM] * len(arrays), o...]
    pallas_call x1, Pallas kernels: 3.74 us -> 0.62 us  [second_call(): pl.pallas_call(second_kernel, in_specs=[VMEM] * len(arrays), out_specs=[V...]
    pallas_call x1, Pallas kernels: 1.67 us -> 0.14 us  [over_call(): pl.pallas_call(over_kernel, in_specs=[VMEM] * 3, out_specs=VMEM, out_shap...]
    ppermute x8, starting transfers between devices: 13.9 us -> 14.6 us  [exchanged(): return lax.ppermute(x, BOTH, [(i, i ^ distance) for i in range(count)])]
  transfers between devices with their start and end apart: 13 -> 13, of which waited for: 3 -> 3; matrix products, arithmetic and copies ran while one was open for 0% -> 0% of each run, Pallas kernels for 21% -> 15%
where the time goes in v6:
time: 66.8 us; the launch traced here: 66.5 us
  starting transfers between devices  34.6 us (52%)
  Pallas kernels  14.2 us (21%)
  blocking collectives  13.7 us (21%)
  waiting for transfers between devices  2.26 us (3%)
  between operations  1.6 us (2%)
    ppermute x3, starting transfers between devices, moved(): return lax.ppermute(x, BOTH, route)  18.6 us
    ppermute x8, starting transfers between devices, exchanged(): return lax.ppermute(x, BOTH, [(i, i ^ distance) for i in range(count)])  14.6 us
    all_to_all x1, blocking collectives, own_block_body(): sums = lax.all_to_all(sums, BOTH, 0, 0)  13.7 us
    pallas_call x1, Pallas kernels, diagonal_call(): pl.pallas_call(diagonal_kernel, in_specs=[SMEM, VMEM, VMEM, VMEM], out_sp...  3.53 us
    pallas_call x1, Pallas kernels, lower_diagonal_call(): pl.pallas_call(lower_diagonal_kernel, in_specs=[SMEM] + [VMEM] * 5, out_s...  3.47 us
    pallas_call x1, Pallas kernels, final_call(): pl.pallas_call(final_kernel, in_specs=[VMEM] * (2 + 2 * members), out_spe...  2.27 us
    ppermute x8, waiting for transfers between devices, exchanged(): return lax.ppermute(x, BOTH, [(i, i ^ distance) for i in range(count)])  2.24 us
    pallas_call x1, Pallas kernels, second_diagonal_call(): pl.pallas_call(second_diagonal_kernel, in_specs=[VMEM] * 6, out_specs=VME...  1.99 us
  transfers between devices with their start and end apart: 13, of which 3 were waited for; matrix products, arithmetic and copies ran while one was open for 0% of the time, Pallas kernels for 15%

profile of v6, /device:TPU:0, one launch (start us, length us, event | category | flops | bytes accessed | tf_op | source)
XLA Modules:
  0.0 66.5 jit_solution(18030945453055764645)
XLA Ops:
  0.6 1.8 %shard_map.77 = (f32[48,2048]{1,0:T(8,128)S(1)}, f32[48,2048]{1,0:T(8,128)S(1)}, f32[64,2048]{1,0:T(8,128)S(1)}, f32[32,2048]{1,0:T(8,128)S(1)}, f32[64,2048]{1,...) custom-call(f32[64,8192]{1,0:T(8,128)} %features.1, ...), custom_call_target="tpu_custom_call" | custom-call | flops 2000000000 | bytes 6000000 | tf_op jit(solution)/shard_map/pallas_call | solution.py:502
  2.4 0.7 %collective-permute-start.2 = (f32[48,2048]{1,0:T(8,128)S(1)}, f32[48,2048]{1,0:T(8,128)S(1)}, u32[]{:S(2)}, u32[]{:S(2)}) collective-permute-start(f32[48,2048]{1,0:T(8,128)S(1)} %get-tuple-element.47), channel_id=1, source_target_pairs={{7,3},{8,4},{15,11},{16,12},{23,19},{24,20},{31,27}} | collective-permute-start | bytes 1179656 | tf_op jit(solution)/shard_map/ppermute | solution.py:657
  3.1 0.7 %collective-permute-start.3 = (f32[48,2048]{1,0:T(8,128)S(1)}, f32[48,2048]{1,0:T(8,128)S(1)}, u32[]{:S(2)}, u32[]{:S(2)}) collective-permute-start(f32[48,2048]{1,0:T(8,128)S(1)} %get-tuple-element.48), channel_id=1, source_target_pairs={{4,3},{11,4},{12,11},{19,12},{20,19},{27,20},{28,27}} | collective-permute-start | bytes 1179656 | tf_op jit(solution)/shard_map/ppermute | solution.py:657
  3.8 3.0 %collective-permute-start = (f32[8,128]{1,0:T(8,128)S(1)}, f32[8,128]{1,0:T(8,128)S(1)}, u32[]{:S(2)}, u32[]{:S(2)}) collective-permute-start(f32[8,128]{1,0:T(8,128)S(1)} %get-tuple-element.39), channel_id=1, source_target_pairs={{0,2},{1,3},{2,0},{3,1},{4,6},{5,7},{6,4},{7,5},{8,10},{9,11},{10,... | collective-permute-start | bytes 12296 | tf_op jit(solution)/shard_map/ppermute | solution.py:648
  7.5 3.5 %shard_map.78 = (bf16[512,2048]{1,0:T(8,128)(2,1)S(1)}, f32[32,2048]{1,0:T(8,128)S(1)}, bf16[2048,256]{1,0:T(8,128)(2,1)S(1)}, bf16[256,2048]{1,0:T(8,128)(2,1)S(1)}, bf16[32,2048]{1,0:T(8,128)(2,1)S(1)}) custom-call(f32[1]{0:T(128)S(6)} %copy.8.signal, f32[64,2048]{1,0:T(8,128)S(1)} %get-tuple-element.40.raw, f32[1,64]{1,0:T(1,128)S(1)} %get-tuple-element.41.scale, ...), custom_call_target="tpu_custom_call" | custom-call | flops 4000000000 | bytes 12000000 | tf_op jit(solution)/shard_map/pallas_call | solution.py:519
  11.1 0.0 collective-permute-done
  11.1 0.8 %collective-permute-start.1 = (f32[8,128]{1,0:T(8,128)S(1)}, f32[8,128]{1,0:T(8,128)S(1)}, u32[]{:S(2)}, u32[]{:S(2)}) collective-permute-start(f32[8,128]{1,0:T(8,128)S(1)} %add.12), channel_id=1, source_target_pairs={{0,1},{1,0},{2,3},{3,2},{4,5},{5,4},{6,7},{7,6},{8,9},{9,8},{10,11... | collective-permute-start | bytes 12296 | tf_op jit(solution)/shard_map/ppermute | solution.py:648
  11.9 0.8 %collective-permute-done.1 = f32[8,128]{1,0:T(8,128)S(1)} collective-permute-done((f32[8,128]{1,0:T(8,128)S(1)}, f32[8,128]{1,0:T(8,128)S(1)}, u32[]{:S(2)}, u32[]{:S(2)}) %collective-permute-start.1) | collective-permute-done | bytes 4128 | tf_op jit(solution)/shard_map/ppermute | solution.py:648
  12.8 0.0 collective-permute-done.2.sent
  12.8 0.0 collective-permute-done.3.sent_rest
  12.8 0.4 shard_map.79
  13.1 14.1 %collective-permute-start.4 = (f32[40,2048]{1,0:T(8,128)S(1)}, f32[40,2048]{1,0:T(8,128)S(1)}, u32[]{:S(2)}, u32[]{:S(2)}) collective-permute-start(f32[40,2048]{1,0:T(8,128)S(1)} %get-tuple-element.59.over), channel_id=1, source_target_pairs={{0,1},{1,2},{2,3},{3,7},{7,6},{6,5},{5,4},{4,8},{8,9},{9,10},{10,1... | collective-permute-start | bytes 983048 | tf_op jit(solution)/shard_map/ppermute | solution.py:643
  27.2 3.5 %shard_map.80 = (bf16[1536,2048]{1,0:T(8,128)(2,1)S(1)}, f32[32,2048]{1,0:T(8,128)S(1)}) custom-call(f32[1]{0:T(128)S(6)} %copy.8.signal, bf16[2048,256]{1,0:T(8,128)(2,1)S(1)} %get-tuple-element.49.left, bf16[256,2048]{1,0:T(8,128)(2,1)S(1)} %get-tuple-element.55.right, bf16[32,2048]{1,0:T(8,128)(2,1)S(1)} %get-tuple-element.50.half, ...), custom_call_target="tpu_custom_call" | custom-call | flops 4000000000 | bytes 12000000 | tf_op jit(solution)/shard_map/pallas_call | solution.py:538
  30.7 1.3 %collective-permute-start.5 = (f32[32,2048]{1,0:T(8,128)S(1)}, f32[32,2048]{1,0:T(8,128)S(1)}, u32[]{:S(2)}, u32[]{:S(2)}) collective-permute-start(f32[32,2048]{1,0:T(8,128)S(1)} %get-tuple-element.58), channel_id=1, source_target_pairs={{1,0},{2,1},{3,2},{7,3},{6,7},{5,6},{4,5},{8,4},{9,8},{10,9},{11,1... | collective-permute-start | bytes 786440 | tf_op jit(solution)/shard_map/ppermute | solution.py:643
  32.0 0.0 collective-permute-done.4.got
  32.0 1.2 %collective-permute-start.7 = (f32[32,2048]{1,0:T(8,128)S(1)}, f32[32,2048]{1,0:T(8,128)S(1)}, u32[]{:S(2)}, u32[]{:S(2)}) collective-permute-start(f32[32,2048]{1,0:T(8,128)S(1)} %slice_add_fusion.image.rest_0_), channel_id=1, source_target_pairs={{0,1},{1,0},{2,3},{3,2},{4,5},{5,4},{6,7},{7,6},{8,9},{9,8},{10,11... | collective-permute-start | bytes 786440 | tf_op jit(solution)/shard_map/ppermute | solution.py:648
  33.2 3.4 %collective-permute-start.8 = (f32[32,2048]{1,0:T(8,128)S(1)}, f32[32,2048]{1,0:T(8,128)S(1)}, u32[]{:S(2)}, u32[]{:S(2)}) collective-permute-start(f32[32,2048]{1,0:T(8,128)S(1)} %slice_add_fusion.image.rest_0_), channel_id=1, source_target_pairs={{0,2},{1,3},{2,0},{3,1},{4,6},{5,7},{6,4},{7,5},{8,10},{9,11},{10,... | collective-permute-start | bytes 786440 | tf_op jit(solution)/shard_map/ppermute | solution.py:648
  36.7 0.1 shard_map.81.over2
  36.8 3.3 %collective-permute-start.6 = (f32[32,2048]{1,0:T(8,128)S(1)}, f32[32,2048]{1,0:T(8,128)S(1)}, u32[]{:S(2)}, u32[]{:S(2)}) collective-permute-start(f32[32,2048]{1,0:T(8,128)S(1)} %shard_map.81.over2), channel_id=1, source_target_pairs={{0,1},{1,2},{2,3},{3,7},{7,6},{6,5},{5,4},{4,8},{8,9},{9,10},{10,1... | collective-permute-start | bytes 786440 | tf_op jit(solution)/shard_map/ppermute | solution.py:643
  40.1 2.0 %shard_map.82.partial = f32[32,2048]{1,0:T(8,128)S(1)} custom-call(bf16[512,2048]{1,0:T(8,128)(2,1)S(1)} %get-tuple-element.60.upper, bf16[1536,2048]{1,0:T(8,128)(2,1)S(1)} %get-tuple-element.61.lower, f32[8,2048]{1,0:T(8,128)S(1)} %get-tuple-element.62.row_sums, f32[1,2048]{1,0:T(1,128)S(1)} %get-tuple-element.51.noise, ...), custom_call_target="tpu_custom_call" | custom-call | flops 2000000000 | bytes 6000000 | tf_op jit(solution)/shard_map/pallas_call | solution.py:590
  42.1 0.0 collective-permute-done.5.part
  42.1 0.0 copy-start
  42.1 0.6 shard_map.83
  42.7 0.0 collective-permute-done.6
  42.8 5.1 %collective-permute-start.10 = (f32[32,2048]{1,0:T(8,128)S(1)}, f32[32,2048]{1,0:T(8,128)S(1)}, u32[]{:S(2)}, u32[]{:S(2)}) collective-permute-start(f32[32,2048]{1,0:T(8,128)S(1)} %add.15.rest_4_), channel_id=1, source_target_pairs={{0,2},{1,3},{2,0},{3,1},{4,6},{5,7},{6,4},{7,5},{8,10},{9,11},{10,... | collective-permute-start | bytes 786440 | tf_op jit(solution)/shard_map/ppermute | solution.py:648
  47.9 0.6 collective-permute-start.9
  48.4 0.0 collective-permute-done.7.rest_1_
  48.4 0.0 collective-permute-done.8.rest_2_
  48.4 13.7 %all_to_all.5.sums = f32[32,8,128]{2,1,0:T(8,128)S(1)} all-to-all(f32[32,8,128]{2,1,0:T(8,128)S(1)} %get-tuple-element.68), channel_id=1, replica_groups=mesh['blk'=8,'pair'=4] {'blk','pair'}, dimensions={0} | all-to-all | bytes 262144 | tf_op jit(solution)/shard_map/all_to_all | solution.py:702
  62.1 0.0 collective-permute-done.10.rest_6_
  62.1 0.0 collective-permute-done.9.rest_5_
  62.1 0.2 collective-permute-start.11
  62.4 0.3 collective-permute-start.12
  62.6 1.0 %collective-permute-done.11.rest_3_ = f32[32,2048]{1,0:T(8,128)S(1)} collective-permute-done((f32[32,2048]{1,0:T(8,128)S(1)}, f32[32,2048]{1,0:T(8,128)S(1)}, u32[]{:S(2)}, u32[]{:S(2)}) %collective-permute-start.11) | collective-permute-done | bytes 262176 | tf_op jit(solution)/shard_map/ppermute | solution.py:648
  63.7 0.4 collective-permute-done.12.rest_7_
  64.0 0.0 copy-done
  64.0 2.3 %shard_map.84 = (f32[32,8192]{1,0:T(8,128)}, f32[32,8192]{1,0:T(8,128)}) custom-call(f32[32,8,128]{2,1,0:T(8,128)S(1)} %all_to_all.5.sums, f32[32,8192]{1,0:T(8,128)S(1)} %copy-done, f32[32,2048]{1,0:T(8,128)S(1)} %slice_add_fusion.image.rest_0_, f32[32,2048]{1,0:T(8,128)S(1)} %collective-permute-done.7.rest_1_, ...), custom_call_target="tpu_custom_call" | custom-call | flops 3000000000 | bytes 9000000 | tf_op jit(solution)/shard_map/pallas_call | solution.py:617
  (4 shorter events, 0.1 us)
Async XLA Ops:
  2.4 10.3 %collective-permute-start.2 = (f32[48,2048]{1,0:T(8,128)S(1)}, f32[48,2048]{1,0:T(8,128)S(1)}, u32[]{:S(2)}, u32[]{:S(2)}) collective-permute-start(f32[48,2048]{1,0:T(8,128)S(1)} %get-tuple-element.47), channel_id=1, source_target_pairs={{7,3},{8,4},{15,11},{16,12},{23,19},{24,20},{31,27}} | collective-permute-start | bytes 1179656 | tf_op jit(solution)/shard_map/ppermute | solution.py:657
  3.1 9.6 %collective-permute-start.3 = (f32[48,2048]{1,0:T(8,128)S(1)}, f32[48,2048]{1,0:T(8,128)S(1)}, u32[]{:S(2)}, u32[]{:S(2)}) collective-permute-start(f32[48,2048]{1,0:T(8,128)S(1)} %get-tuple-element.48), channel_id=1, source_target_pairs={{4,3},{11,4},{12,11},{19,12},{20,19},{27,20},{28,27}} | collective-permute-start | bytes 1179656 | tf_op jit(solution)/shard_map/ppermute | solution.py:657
  3.8 7.2 %collective-permute-start = (f32[8,128]{1,0:T(8,128)S(1)}, f32[8,128]{1,0:T(8,128)S(1)}, u32[]{:S(2)}, u32[]{:S(2)}) collective-permute-start(f32[8,128]{1,0:T(8,128)S(1)} %get-tuple-element.39), channel_id=1, source_target_pairs={{0,2},{1,3},{2,0},{3,1},{4,6},{5,7},{6,4},{7,5},{8,10},{9,11},{10,... | collective-permute-start | bytes 12296 | tf_op jit(solution)/shard_map/ppermute | solution.py:648
  11.1 1.7 %collective-permute-start.1 = (f32[8,128]{1,0:T(8,128)S(1)}, f32[8,128]{1,0:T(8,128)S(1)}, u32[]{:S(2)}, u32[]{:S(2)}) collective-permute-start(f32[8,128]{1,0:T(8,128)S(1)} %add.12), channel_id=1, source_target_pairs={{0,1},{1,0},{2,3},{3,2},{4,5},{5,4},{6,7},{7,6},{8,9},{9,8},{10,11... | collective-permute-start | bytes 12296 | tf_op jit(solution)/shard_map/ppermute | solution.py:648
  13.1 18.9 %collective-permute-start.4 = (f32[40,2048]{1,0:T(8,128)S(1)}, f32[40,2048]{1,0:T(8,128)S(1)}, u32[]{:S(2)}, u32[]{:S(2)}) collective-permute-start(f32[40,2048]{1,0:T(8,128)S(1)} %get-tuple-element.59.over), channel_id=1, source_target_pairs={{0,1},{1,2},{2,3},{3,7},{7,6},{6,5},{5,4},{4,8},{8,9},{9,10},{10,1... | collective-permute-start | bytes 983048 | tf_op jit(solution)/shard_map/ppermute | solution.py:643
  30.7 11.4 %collective-permute-start.5 = (f32[32,2048]{1,0:T(8,128)S(1)}, f32[32,2048]{1,0:T(8,128)S(1)}, u32[]{:S(2)}, u32[]{:S(2)}) collective-permute-start(f32[32,2048]{1,0:T(8,128)S(1)} %get-tuple-element.58), channel_id=1, source_target_pairs={{1,0},{2,1},{3,2},{7,3},{6,7},{5,6},{4,5},{8,4},{9,8},{10,9},{11,1... | collective-permute-start | bytes 786440 | tf_op jit(solution)/shard_map/ppermute | solution.py:643
  32.0 16.4 %collective-permute-start.7 = (f32[32,2048]{1,0:T(8,128)S(1)}, f32[32,2048]{1,0:T(8,128)S(1)}, u32[]{:S(2)}, u32[]{:S(2)}) collective-permute-start(f32[32,2048]{1,0:T(8,128)S(1)} %slice_add_fusion.image.rest_0_), channel_id=1, source_target_pairs={{0,1},{1,0},{2,3},{3,2},{4,5},{5,4},{6,7},{7,6},{8,9},{9,8},{10,11... | collective-permute-start | bytes 786440 | tf_op jit(solution)/shard_map/ppermute | solution.py:648
  33.2 15.2 %collective-permute-start.8 = (f32[32,2048]{1,0:T(8,128)S(1)}, f32[32,2048]{1,0:T(8,128)S(1)}, u32[]{:S(2)}, u32[]{:S(2)}) collective-permute-start(f32[32,2048]{1,0:T(8,128)S(1)} %slice_add_fusion.image.rest_0_), channel_id=1, source_target_pairs={{0,2},{1,3},{2,0},{3,1},{4,6},{5,7},{6,4},{7,5},{8,10},{9,11},{10,... | collective-permute-start | bytes 786440 | tf_op jit(solution)/shard_map/ppermute | solution.py:648
  36.8 5.9 %collective-permute-start.6 = (f32[32,2048]{1,0:T(8,128)S(1)}, f32[32,2048]{1,0:T(8,128)S(1)}, u32[]{:S(2)}, u32[]{:S(2)}) collective-permute-start(f32[32,2048]{1,0:T(8,128)S(1)} %shard_map.81.over2), channel_id=1, source_target_pairs={{0,1},{1,2},{2,3},{3,7},{7,6},{6,5},{5,4},{4,8},{8,9},{9,10},{10,1... | collective-permute-start | bytes 786440 | tf_op jit(solution)/shard_map/ppermute | solution.py:643
  42.1 22.0 %copy-start = (f32[32,8192]{1,0:T(8,128)S(1)}, f32[32,8192]{1,0:T(8,128)}, u32[]{:S(2)}) copy-start(f32[32,8192]{1,0:T(8,128)} %right_side.3) | copy-start | bytes 3145732
  42.8 19.4 %collective-permute-start.10 = (f32[32,2048]{1,0:T(8,128)S(1)}, f32[32,2048]{1,0:T(8,128)S(1)}, u32[]{:S(2)}, u32[]{:S(2)}) collective-permute-start(f32[32,2048]{1,0:T(8,128)S(1)} %add.15.rest_4_), channel_id=1, source_target_pairs={{0,2},{1,3},{2,0},{3,1},{4,6},{5,7},{6,4},{7,5},{8,10},{9,11},{10,... | collective-permute-start | bytes 786440 | tf_op jit(solution)/shard_map/ppermute | solution.py:648
  47.9 14.3 %collective-permute-start.9 = (f32[32,2048]{1,0:T(8,128)S(1)}, f32[32,2048]{1,0:T(8,128)S(1)}, u32[]{:S(2)}, u32[]{:S(2)}) collective-permute-start(f32[32,2048]{1,0:T(8,128)S(1)} %add.15.rest_4_), channel_id=1, source_target_pairs={{0,1},{1,0},{2,3},{3,2},{4,5},{5,4},{6,7},{7,6},{8,9},{9,8},{10,11... | collective-permute-start | bytes 786440 | tf_op jit(solution)/shard_map/ppermute | solution.py:648
  62.1 1.5 %collective-permute-start.11 = (f32[32,2048]{1,0:T(8,128)S(1)}, f32[32,2048]{1,0:T(8,128)S(1)}, u32[]{:S(2)}, u32[]{:S(2)}) collective-permute-start(f32[32,2048]{1,0:T(8,128)S(1)} %collective-permute-done.8.rest_2_), channel_id=1, source_target_pairs={{0,1},{1,0},{2,3},{3,2},{4,5},{5,4},{6,7},{7,6},{8,9},{9,8},{10,11... | collective-permute-start | bytes 786440 | tf_op jit(solution)/shard_map/ppermute | solution.py:648
  62.4 1.7 %collective-permute-start.12 = (f32[32,2048]{1,0:T(8,128)S(1)}, f32[32,2048]{1,0:T(8,128)S(1)}, u32[]{:S(2)}, u32[]{:S(2)}) collective-permute-start(f32[32,2048]{1,0:T(8,128)S(1)} %collective-permute-done.10.rest_6_), channel_id=1, source_target_pairs={{0,1},{1,0},{2,3},{3,2},{4,5},{5,4},{6,7},{7,6},{8,9},{9,8},{10,11... | collective-permute-start | bytes 786440 | tf_op jit(solution)/shard_map/ppermute | solution.py:648

commit v7 on v6

--- a/solution.py
+++ b/solution.py
@@ -357,24 +357,33 @@
     return x[:half] + x[half:]
 
 
-def over_kernel(mark, tile, image, over2):
+def shift_of(signal):
+    return signal + 1.0
+
+
+def over_kernel(signal, mark, tile, image, direction, over2):
     live = jnp.max(mark[...]) > 0.0
 
     @pl.when(live)
     def _():
-        over2[...] = folded(dot(both_parts(image[...]), tile[...]))
+        shifted = image[...] - shift_of(signal[0]) * direction[...]
+        over2[...] = folded(dot(both_parts(shifted), tile[...]))
 
     @pl.when(jnp.logical_not(live))
     def _():
         over2[...] = jnp.zeros_like(over2)
 
 
-def second_diagonal_kernel(upper, lower, row_sums, noise, image, got, own2, both):
+def second_diagonal_kernel(
+    signal, upper, lower, row_sums, noise, image, got, direction, own2, both
+):
     size = upper.shape[1]
     probes = image.shape[0]
-    here = image[...]
+    shift = shift_of(signal[0])
+    here = image[...] - shift * direction[...]
     both[...] = both_parts(here)
     own2[...] = (noise[...] + row_sums[0:1, :] + got[probes : probes + 1, :]) * here
+    own2[...] += shift * image[...]
     for tile, first in ((upper, 0), (lower, upper.shape[0])):
         for at in range(first, first + tile.shape[0], CHUNK):
             rows = slice(at, at + CHUNK)
@@ -386,7 +395,7 @@
 
 
 def second_kernel(
-    mark, cross_tile, direction, next_dir, image, part, over, over2, partial, own2, sums
+    signal, mark, cross_tile, direction, next_dir, image, part, over, over2, partial, own2, sums
 ):
     probes = image.shape[0]
     here = image[...]
@@ -395,7 +404,8 @@
 
     @pl.when(jnp.max(mark[...]) > 0.0)
     def _():
-        own2[...] += folded(dot_nt(both_parts(there), cross_tile[...]))
+        shifted = there - shift_of(signal[0]) * next_dir[...]
+        own2[...] += folded(dot_nt(both_parts(shifted), cross_tile[...]))
 
     begin = direction[...]
     mine = own2[...]
@@ -574,40 +584,40 @@
     )(signal, *arrays)
 
 
-def over_call(mark, tile, image):
+def over_call(signal, mark, tile, image, direction):
     return pl.pallas_call(
         over_kernel,
-        in_specs=[VMEM] * 3,
+        in_specs=[SMEM] + [VMEM] * 4,
         out_specs=VMEM,
         out_shape=pltpu.VMEM(image.shape, f32),
         cost_estimate=taking(2),
         compiler_params=params(16),
-    )(mark, tile, image)
-
-
-def second_diagonal_call(upper, lower, row_sums, noise, image, got):
+    )(signal, mark, tile, image, direction)
+
+
+def second_diagonal_call(signal, upper, lower, row_sums, noise, image, got, direction):
     probes, size = image.shape
     return pl.pallas_call(
         second_diagonal_kernel,
-        in_specs=[VMEM] * 6,
+        in_specs=[SMEM] + [VMEM] * 7,
         out_specs=VMEM,
         out_shape=pltpu.VMEM((probes, size), f32),
         scratch_shapes=[pltpu.VMEM((2 * probes, size), bf16)],
         cost_estimate=taking(2),
         compiler_params=params(16),
-    )(upper, lower, row_sums, noise, image, got)
-
-
-def second_call(devices, *arrays):
+    )(signal, upper, lower, row_sums, noise, image, got, direction)
+
+
+def second_call(devices, signal, *arrays):
     probes, size = arrays[2].shape
     return pl.pallas_call(
         second_kernel,
-        in_specs=[VMEM] * len(arrays),
+        in_specs=[SMEM] + [VMEM] * len(arrays),
         out_specs=[VMEM] * 2,
         out_shape=[pltpu.VMEM((probes, size), f32), pltpu.VMEM((devices, 8, 128), f32)],
         cost_estimate=taking(4),
         compiler_params=params(16),
-    )(*arrays)
+    )(signal, *arrays)
 
 
 def final_call(sums, right_side, images, images2):
@@ -689,10 +699,12 @@
     images = {0: image}
     for span in spans:
         images[span] = exchanged(image, span)
-    over2 = over_call(mark, cross_tile, image)
-    partial = second_diagonal_call(tile, lower_tile, row_sums, noise, image, got)
+    over2 = over_call(signal, mark, cross_tile, image, direction)
+    partial = second_diagonal_call(
+        signal, tile, lower_tile, row_sums, noise, image, got, direction
+    )
     own2, sums = second_call(
-        devices, mark, cross_tile, direction, next_dir, image, part, over, over2, partial
+        devices, signal, mark, cross_tile, direction, next_dir, image, part, over, over2, partial
     )
     image2 = own2 + moved(over2, 1)
     images2 = {0: image2}

time: 66.8 us -> 66.3 us (level)
  starting transfers between devices: 34.6 us -> 18.3 us
  Pallas kernels: 14.2 us -> 30 us
    ppermute x3, starting transfers between devices: 18.6 us -> 5.5 us  [moved(): return lax.ppermute(x, BOTH, route)]
    pallas_call x1, Pallas kernels: 0.38 us -> 12 us  [crossing_call(): pl.pallas_call(crossing_kernel, in_specs=[SMEM] + [VMEM] * len(arrays), o...]
    pallas_call x3, Pallas kernels: 2.75 us -> 6.94 us  [the longest x1 3.28 us: second_call(): pl.pallas_call(second_kernel, in_specs=[SMEM] + [VMEM] * len(arrays), out...]
    ppermute x8, starting transfers between devices: 14.6 us -> 11.4 us  [exchanged(): return lax.ppermute(x, BOTH, [(i, i ^ distance) for i in range(count)])]
  transfers between devices with their start and end apart: 13 -> 13, of which waited for: 3 -> 3; matrix products, arithmetic and copies ran while one was open for 0% -> 0% of each run, Pallas kernels for 15% -> 21%
where the time goes in v7:
time: 66.3 us; the launch traced here: 65.5 us
  Pallas kernels  30 us (45%)
  starting transfers between devices  18.3 us (28%)
  blocking collectives  13.3 us (20%)
  waiting for transfers between devices  2.26 us (3%)
  between operations  1.58 us (2%)
    all_to_all x1, blocking collectives, own_block_body(): sums = lax.all_to_all(sums, BOTH, 0, 0)  13.3 us
    pallas_call x1, Pallas kernels, crossing_call(): pl.pallas_call(crossing_kernel, in_specs=[SMEM] + [VMEM] * len(arrays), o...  12 us
    ppermute x8, starting transfers between devices, exchanged(): return lax.ppermute(x, BOTH, [(i, i ^ distance) for i in range(count)])  11.4 us
    ppermute x3, starting transfers between devices, moved(): return lax.ppermute(x, BOTH, route)  5.5 us
    pallas_call x1, Pallas kernels, diagonal_call(): pl.pallas_call(diagonal_kernel, in_specs=[SMEM, VMEM, VMEM, VMEM], out_sp...  3.53 us
    pallas_call x1, Pallas kernels, lower_diagonal_call(): pl.pallas_call(lower_diagonal_kernel, in_specs=[SMEM] + [VMEM] * 5, out_s...  3.46 us
    pallas_call x1, Pallas kernels, second_call(): pl.pallas_call(second_kernel, in_specs=[SMEM] + [VMEM] * len(arrays), out...  3.28 us
    pallas_call x1, Pallas kernels, final_call(): pl.pallas_call(final_kernel, in_specs=[VMEM] * (2 + 2 * members), out_spe...  2.27 us
  transfers between devices with their start and end apart: 13, of which 3 were waited for; matrix products, arithmetic and copies ran while one was open for 0% of the time, Pallas kernels for 21%

profile of v7, /device:TPU:0, one launch (start us, length us, event | category | flops | bytes accessed | tf_op | source)
XLA Modules:
  0.0 65.5 jit_solution(16425016294482266675)
XLA Ops:
  0.6 1.8 %shard_map.77 = (f32[48,2048]{1,0:T(8,128)S(1)}, f32[48,2048]{1,0:T(8,128)S(1)}, f32[64,2048]{1,0:T(8,128)S(1)}, f32[32,2048]{1,0:T(8,128)S(1)}, f32[64,2048]{1,...) custom-call(f32[64,8192]{1,0:T(8,128)} %features.1, ...), custom_call_target="tpu_custom_call" | custom-call | flops 2000000000 | bytes 6000000 | tf_op jit(solution)/shard_map/pallas_call | solution.py:512
  2.4 0.7 %collective-permute-start.2 = (f32[48,2048]{1,0:T(8,128)S(1)}, f32[48,2048]{1,0:T(8,128)S(1)}, u32[]{:S(2)}, u32[]{:S(2)}) collective-permute-start(f32[48,2048]{1,0:T(8,128)S(1)} %get-tuple-element.47), channel_id=1, source_target_pairs={{7,3},{8,4},{15,11},{16,12},{23,19},{24,20},{31,27}} | collective-permute-start | bytes 1179656 | tf_op jit(solution)/shard_map/ppermute | solution.py:667
  3.1 0.7 %collective-permute-start.3 = (f32[48,2048]{1,0:T(8,128)S(1)}, f32[48,2048]{1,0:T(8,128)S(1)}, u32[]{:S(2)}, u32[]{:S(2)}) collective-permute-start(f32[48,2048]{1,0:T(8,128)S(1)} %get-tuple-element.48), channel_id=1, source_target_pairs={{4,3},{11,4},{12,11},{19,12},{20,19},{27,20},{28,27}} | collective-permute-start | bytes 1179656 | tf_op jit(solution)/shard_map/ppermute | solution.py:667
  3.8 3.0 %collective-permute-start = (f32[8,128]{1,0:T(8,128)S(1)}, f32[8,128]{1,0:T(8,128)S(1)}, u32[]{:S(2)}, u32[]{:S(2)}) collective-permute-start(f32[8,128]{1,0:T(8,128)S(1)} %get-tuple-element.39), channel_id=1, source_target_pairs={{0,2},{1,3},{2,0},{3,1},{4,6},{5,7},{6,4},{7,5},{8,10},{9,11},{10,... | collective-permute-start | bytes 12296 | tf_op jit(solution)/shard_map/ppermute | solution.py:658
  7.5 3.5 %shard_map.78 = (bf16[512,2048]{1,0:T(8,128)(2,1)S(1)}, f32[32,2048]{1,0:T(8,128)S(1)}, bf16[2048,256]{1,0:T(8,128)(2,1)S(1)}, bf16[256,2048]{1,0:T(8,128)(2,1)S(1)}, bf16[32,2048]{1,0:T(8,128)(2,1)S(1)}) custom-call(f32[1]{0:T(128)S(6)} %copy.8.signal, f32[64,2048]{1,0:T(8,128)S(1)} %get-tuple-element.40.raw, f32[1,64]{1,0:T(1,128)S(1)} %get-tuple-element.41.scale, ...), custom_call_target="tpu_custom_call" | custom-call | flops 4000000000 | bytes 12000000 | tf_op jit(solution)/shard_map/pallas_call | solution.py:529
  11.1 0.0 collective-permute-done
  11.1 0.8 %collective-permute-start.1 = (f32[8,128]{1,0:T(8,128)S(1)}, f32[8,128]{1,0:T(8,128)S(1)}, u32[]{:S(2)}, u32[]{:S(2)}) collective-permute-start(f32[8,128]{1,0:T(8,128)S(1)} %add.12), channel_id=1, source_target_pairs={{0,1},{1,0},{2,3},{3,2},{4,5},{5,4},{6,7},{7,6},{8,9},{9,8},{10,11... | collective-permute-start | bytes 12296 | tf_op jit(solution)/shard_map/ppermute | solution.py:658
  11.9 0.8 %collective-permute-done.1 = f32[8,128]{1,0:T(8,128)S(1)} collective-permute-done((f32[8,128]{1,0:T(8,128)S(1)}, f32[8,128]{1,0:T(8,128)S(1)}, u32[]{:S(2)}, u32[]{:S(2)}) %collective-permute-start.1) | collective-permute-done | bytes 4128 | tf_op jit(solution)/shard_map/ppermute | solution.py:658
  12.8 0.0 collective-permute-done.2.sent
  12.8 0.0 collective-permute-done.3.sent_rest
  12.8 12.0 %shard_map.79 = (bf16[2048,2048]{1,0:T(8,128)(2,1)S(1)}, f32[8,2048]{1,0:T(8,128)S(1)}, f32[32,2048]{1,0:T(8,128)S(1)}, f32[40,2048]{1,0:T(8,128)S(1)}, f32[32,2048]{1,0:T(8,128)S(1)}, /*index=5*/f32[8,128]{1,0:T(8,128)S(1)}) custom-call(f32[1]{0:T(128)S(6)} %copy.8.signal, f32[8,128]{1,0:T(8,128)S(1)} %add.13.found, ...), custom_call_target="tpu_custom_call" | custom-call | flops 12000000000 | bytes 36000000 | tf_op jit(solution)/shard_map/pallas_call | solution.py:563
  24.7 2.5 %collective-permute-start.4 = (f32[40,2048]{1,0:T(8,128)S(1)}, f32[40,2048]{1,0:T(8,128)S(1)}, u32[]{:S(2)}, u32[]{:S(2)}) collective-permute-start(f32[40,2048]{1,0:T(8,128)S(1)} %get-tuple-element.59.over), channel_id=1, source_target_pairs={{0,1},{1,2},{2,3},{3,7},{7,6},{6,5},{5,4},{4,8},{8,9},{9,10},{10,1... | collective-permute-start | bytes 983048 | tf_op jit(solution)/shard_map/ppermute | solution.py:653
  27.2 3.5 %shard_map.80 = (bf16[1536,2048]{1,0:T(8,128)(2,1)S(1)}, f32[32,2048]{1,0:T(8,128)S(1)}) custom-call(f32[1]{0:T(128)S(6)} %copy.8.signal, bf16[2048,256]{1,0:T(8,128)(2,1)S(1)} %get-tuple-element.49.left, bf16[256,2048]{1,0:T(8,128)(2,1)S(1)} %get-tuple-element.55.right, bf16[32,2048]{1,0:T(8,128)(2,1)S(1)} %get-tuple-element.50.half, ...), custom_call_target="tpu_custom_call" | custom-call | flops 4000000000 | bytes 12000000 | tf_op jit(solution)/shard_map/pallas_call | solution.py:548
  30.7 1.3 %collective-permute-start.5 = (f32[32,2048]{1,0:T(8,128)S(1)}, f32[32,2048]{1,0:T(8,128)S(1)}, u32[]{:S(2)}, u32[]{:S(2)}) collective-permute-start(f32[32,2048]{1,0:T(8,128)S(1)} %get-tuple-element.58), channel_id=1, source_target_pairs={{1,0},{2,1},{3,2},{7,3},{6,7},{5,6},{4,5},{8,4},{9,8},{10,9},{11,1... | collective-permute-start | bytes 786440 | tf_op jit(solution)/shard_map/ppermute | solution.py:653
  32.0 0.0 collective-permute-done.4.got
  32.1 1.2 %collective-permute-start.7 = (f32[32,2048]{1,0:T(8,128)S(1)}, f32[32,2048]{1,0:T(8,128)S(1)}, u32[]{:S(2)}, u32[]{:S(2)}) collective-permute-start(f32[32,2048]{1,0:T(8,128)S(1)} %slice_add_fusion.image.rest_0_), channel_id=1, source_target_pairs={{0,1},{1,0},{2,3},{3,2},{4,5},{5,4},{6,7},{7,6},{8,9},{9,8},{10,11... | collective-permute-start | bytes 786440 | tf_op jit(solution)/shard_map/ppermute | solution.py:658
  33.2 3.4 %collective-permute-start.8 = (f32[32,2048]{1,0:T(8,128)S(1)}, f32[32,2048]{1,0:T(8,128)S(1)}, u32[]{:S(2)}, u32[]{:S(2)}) collective-permute-start(f32[32,2048]{1,0:T(8,128)S(1)} %slice_add_fusion.image.rest_0_), channel_id=1, source_target_pairs={{0,2},{1,3},{2,0},{3,1},{4,6},{5,7},{6,4},{7,5},{8,10},{9,11},{10,... | collective-permute-start | bytes 786440 | tf_op jit(solution)/shard_map/ppermute | solution.py:658
  36.7 1.7 %shard_map.81.over2 = f32[32,2048]{1,0:T(8,128)S(1)} custom-call(f32[1]{0:T(128)S(6)} %copy.8.signal, f32[8,128]{1,0:T(8,128)S(1)} %get-tuple-element.52.mark, bf16[2048,2048]{1,0:T(8,128)(2,1)S(1)} %get-tuple-element.53.tile.cross_tile, f32[32,2048]{1,0:T(8,128)S(1)} %slice_add_fusion.image.rest_0_, f32[32,2048]{1,0:T(8,128)S(1)} %get-tuple-element.42.direction), custom_call_target="tpu_custom_call" | custom-call | flops 2000000000 | bytes 6000000 | tf_op jit(solution)/shard_map/pallas_call | solution.py:588
  38.3 1.7 %collective-permute-start.6 = (f32[32,2048]{1,0:T(8,128)S(1)}, f32[32,2048]{1,0:T(8,128)S(1)}, u32[]{:S(2)}, u32[]{:S(2)}) collective-permute-start(f32[32,2048]{1,0:T(8,128)S(1)} %shard_map.81.over2), channel_id=1, source_target_pairs={{0,1},{1,2},{2,3},{3,7},{7,6},{6,5},{5,4},{4,8},{8,9},{9,10},{10,1... | collective-permute-start | bytes 786440 | tf_op jit(solution)/shard_map/ppermute | solution.py:653
  40.1 2.0 %shard_map.82.partial = f32[32,2048]{1,0:T(8,128)S(1)} custom-call(f32[1]{0:T(128)S(6)} %copy.8.signal, bf16[512,2048]{1,0:T(8,128)(2,1)S(1)} %get-tuple-element.60.upper, bf16[1536,2048]{1,0:T(8,128)(2,1)S(1)} %get-tuple-element.61.lower, f32[8,2048]{1,0:T(8,128)S(1)} %get-tuple-element.62.row_sums, f32[1,2048]{1,0:T(1,128)S(1)} %get-tuple-element.51.noise, ...), custom_call_target="tpu_custom_call" | custom-call | flops 2000000000 | bytes 6000000 | tf_op jit(solution)/shard_map/pallas_call | solution.py:600
  42.1 0.0 collective-permute-done.5.part
  42.1 0.0 copy-start
  42.1 3.3 %shard_map.83 = (f32[32,2048]{1,0:T(8,128)S(1)}, f32[32,8,128]{2,1,0:T(8,128)S(1)}) custom-call(f32[1]{0:T(128)S(6)} %copy.8.signal, f32[8,128]{1,0:T(8,128)S(1)} %get-tuple-element.52.mark, bf16[2048,2048]{1,0:T(8,128)(2,1)S(1)} %get-tuple-element.53.tile.cross_tile, f32[32,2048]{1,0:T(8,128)S(1)} %get-tuple-element.42.direction, ...), custom_call_target="tpu_custom_call" | custom-call | flops 4000000000 | bytes 12000000 | tf_op jit(solution)/shard_map/pallas_call | solution.py:613
  45.4 0.0 collective-permute-done.6
  45.4 2.4 %collective-permute-start.10 = (f32[32,2048]{1,0:T(8,128)S(1)}, f32[32,2048]{1,0:T(8,128)S(1)}, u32[]{:S(2)}, u32[]{:S(2)}) collective-permute-start(f32[32,2048]{1,0:T(8,128)S(1)} %add.15.rest_4_), channel_id=1, source_target_pairs={{0,2},{1,3},{2,0},{3,1},{4,6},{5,7},{6,4},{7,5},{8,10},{9,11},{10,... | collective-permute-start | bytes 786440 | tf_op jit(solution)/shard_map/ppermute | solution.py:658
  47.9 0.0 collective-permute-start.9
  47.9 0.0 collective-permute-done.7.rest_1_
  47.9 0.0 collective-permute-done.8.rest_2_
  47.9 13.3 %all_to_all.5.sums = f32[32,8,128]{2,1,0:T(8,128)S(1)} all-to-all(f32[32,8,128]{2,1,0:T(8,128)S(1)} %get-tuple-element.68), channel_id=1, replica_groups=mesh['blk'=8,'pair'=4] {'blk','pair'}, dimensions={0} | all-to-all | bytes 262144 | tf_op jit(solution)/shard_map/all_to_all | solution.py:714
  61.1 0.0 collective-permute-done.10.rest_6_
  61.1 0.0 collective-permute-done.9.rest_5_
  61.1 0.2 collective-permute-start.11
  61.4 0.3 collective-permute-start.12
  61.7 1.0 %collective-permute-done.11.rest_3_ = f32[32,2048]{1,0:T(8,128)S(1)} collective-permute-done((f32[32,2048]{1,0:T(8,128)S(1)}, f32[32,2048]{1,0:T(8,128)S(1)}, u32[]{:S(2)}, u32[]{:S(2)}) %collective-permute-start.11) | collective-permute-done | bytes 262176 | tf_op jit(solution)/shard_map/ppermute | solution.py:658
  62.7 0.4 collective-permute-done.12.rest_7_
  63.1 0.0 copy-done
  63.1 2.3 %shard_map.84 = (f32[32,8192]{1,0:T(8,128)}, f32[32,8192]{1,0:T(8,128)}) custom-call(f32[32,8,128]{2,1,0:T(8,128)S(1)} %all_to_all.5.sums, f32[32,8192]{1,0:T(8,128)S(1)} %copy-done, f32[32,2048]{1,0:T(8,128)S(1)} %slice_add_fusion.image.rest_0_, f32[32,2048]{1,0:T(8,128)S(1)} %collective-permute-done.7.rest_1_, ...), custom_call_target="tpu_custom_call" | custom-call | flops 3000000000 | bytes 9000000 | tf_op jit(solution)/shard_map/pallas_call | solution.py:627
  (4 shorter events, 0.1 us)
Async XLA Ops:
  2.4 10.3 %collective-permute-start.2 = (f32[48,2048]{1,0:T(8,128)S(1)}, f32[48,2048]{1,0:T(8,128)S(1)}, u32[]{:S(2)}, u32[]{:S(2)}) collective-permute-start(f32[48,2048]{1,0:T(8,128)S(1)} %get-tuple-element.47), channel_id=1, source_target_pairs={{7,3},{8,4},{15,11},{16,12},{23,19},{24,20},{31,27}} | collective-permute-start | bytes 1179656 | tf_op jit(solution)/shard_map/ppermute | solution.py:667
  3.1 9.6 %collective-permute-start.3 = (f32[48,2048]{1,0:T(8,128)S(1)}, f32[48,2048]{1,0:T(8,128)S(1)}, u32[]{:S(2)}, u32[]{:S(2)}) collective-permute-start(f32[48,2048]{1,0:T(8,128)S(1)} %get-tuple-element.48), channel_id=1, source_target_pairs={{4,3},{11,4},{12,11},{19,12},{20,19},{27,20},{28,27}} | collective-permute-start | bytes 1179656 | tf_op jit(solution)/shard_map/ppermute | solution.py:667
  3.8 7.2 %collective-permute-start = (f32[8,128]{1,0:T(8,128)S(1)}, f32[8,128]{1,0:T(8,128)S(1)}, u32[]{:S(2)}, u32[]{:S(2)}) collective-permute-start(f32[8,128]{1,0:T(8,128)S(1)} %get-tuple-element.39), channel_id=1, source_target_pairs={{0,2},{1,3},{2,0},{3,1},{4,6},{5,7},{6,4},{7,5},{8,10},{9,11},{10,... | collective-permute-start | bytes 12296 | tf_op jit(solution)/shard_map/ppermute | solution.py:658
  11.1 1.7 %collective-permute-start.1 = (f32[8,128]{1,0:T(8,128)S(1)}, f32[8,128]{1,0:T(8,128)S(1)}, u32[]{:S(2)}, u32[]{:S(2)}) collective-permute-start(f32[8,128]{1,0:T(8,128)S(1)} %add.12), channel_id=1, source_target_pairs={{0,1},{1,0},{2,3},{3,2},{4,5},{5,4},{6,7},{7,6},{8,9},{9,8},{10,11... | collective-permute-start | bytes 12296 | tf_op jit(solution)/shard_map/ppermute | solution.py:658
  24.7 7.3 %collective-permute-start.4 = (f32[40,2048]{1,0:T(8,128)S(1)}, f32[40,2048]{1,0:T(8,128)S(1)}, u32[]{:S(2)}, u32[]{:S(2)}) collective-permute-start(f32[40,2048]{1,0:T(8,128)S(1)} %get-tuple-element.59.over), channel_id=1, source_target_pairs={{0,1},{1,2},{2,3},{3,7},{7,6},{6,5},{5,4},{4,8},{8,9},{9,10},{10,1... | collective-permute-start | bytes 983048 | tf_op jit(solution)/shard_map/ppermute | solution.py:653
  30.7 11.4 %collective-permute-start.5 = (f32[32,2048]{1,0:T(8,128)S(1)}, f32[32,2048]{1,0:T(8,128)S(1)}, u32[]{:S(2)}, u32[]{:S(2)}) collective-permute-start(f32[32,2048]{1,0:T(8,128)S(1)} %get-tuple-element.58), channel_id=1, source_target_pairs={{1,0},{2,1},{3,2},{7,3},{6,7},{5,6},{4,5},{8,4},{9,8},{10,9},{11,1... | collective-permute-start | bytes 786440 | tf_op jit(solution)/shard_map/ppermute | solution.py:653
  32.1 15.8 %collective-permute-start.7 = (f32[32,2048]{1,0:T(8,128)S(1)}, f32[32,2048]{1,0:T(8,128)S(1)}, u32[]{:S(2)}, u32[]{:S(2)}) collective-permute-start(f32[32,2048]{1,0:T(8,128)S(1)} %slice_add_fusion.image.rest_0_), channel_id=1, source_target_pairs={{0,1},{1,0},{2,3},{3,2},{4,5},{5,4},{6,7},{7,6},{8,9},{9,8},{10,11... | collective-permute-start | bytes 786440 | tf_op jit(solution)/shard_map/ppermute | solution.py:658
  33.2 14.6 %collective-permute-start.8 = (f32[32,2048]{1,0:T(8,128)S(1)}, f32[32,2048]{1,0:T(8,128)S(1)}, u32[]{:S(2)}, u32[]{:S(2)}) collective-permute-start(f32[32,2048]{1,0:T(8,128)S(1)} %slice_add_fusion.image.rest_0_), channel_id=1, source_target_pairs={{0,2},{1,3},{2,0},{3,1},{4,6},{5,7},{6,4},{7,5},{8,10},{9,11},{10,... | collective-permute-start | bytes 786440 | tf_op jit(solution)/shard_map/ppermute | solution.py:658
  38.3 7.1 %collective-permute-start.6 = (f32[32,2048]{1,0:T(8,128)S(1)}, f32[32,2048]{1,0:T(8,128)S(1)}, u32[]{:S(2)}, u32[]{:S(2)}) collective-permute-start(f32[32,2048]{1,0:T(8,128)S(1)} %shard_map.81.over2), channel_id=1, source_target_pairs={{0,1},{1,2},{2,3},{3,7},{7,6},{6,5},{5,4},{4,8},{8,9},{9,10},{10,1... | collective-permute-start | bytes 786440 | tf_op jit(solution)/shard_map/ppermute | solution.py:653
  42.1 21.0 %copy-start = (f32[32,8192]{1,0:T(8,128)S(1)}, f32[32,8192]{1,0:T(8,128)}, u32[]{:S(2)}) copy-start(f32[32,8192]{1,0:T(8,128)} %right_side.3) | copy-start | bytes 3145732
  45.4 15.7 %collective-permute-start.10 = (f32[32,2048]{1,0:T(8,128)S(1)}, f32[32,2048]{1,0:T(8,128)S(1)}, u32[]{:S(2)}, u32[]{:S(2)}) collective-permute-start(f32[32,2048]{1,0:T(8,128)S(1)} %add.15.rest_4_), channel_id=1, source_target_pairs={{0,2},{1,3},{2,0},{3,1},{4,6},{5,7},{6,4},{7,5},{8,10},{9,11},{10,... | collective-permute-start | bytes 786440 | tf_op jit(solution)/shard_map/ppermute | solution.py:658
  47.9 13.3 %collective-permute-start.9 = (f32[32,2048]{1,0:T(8,128)S(1)}, f32[32,2048]{1,0:T(8,128)S(1)}, u32[]{:S(2)}, u32[]{:S(2)}) collective-permute-start(f32[32,2048]{1,0:T(8,128)S(1)} %add.15.rest_4_), channel_id=1, source_target_pairs={{0,1},{1,0},{2,3},{3,2},{4,5},{5,4},{6,7},{7,6},{8,9},{9,8},{10,11... | collective-permute-start | bytes 786440 | tf_op jit(solution)/shard_map/ppermute | solution.py:658
  61.1 1.5 %collective-permute-start.11 = (f32[32,2048]{1,0:T(8,128)S(1)}, f32[32,2048]{1,0:T(8,128)S(1)}, u32[]{:S(2)}, u32[]{:S(2)}) collective-permute-start(f32[32,2048]{1,0:T(8,128)S(1)} %collective-permute-done.8.rest_2_), channel_id=1, source_target_pairs={{0,1},{1,0},{2,3},{3,2},{4,5},{5,4},{6,7},{7,6},{8,9},{9,8},{10,11... | collective-permute-start | bytes 786440 | tf_op jit(solution)/shard_map/ppermute | solution.py:658
  61.4 1.7 %collective-permute-start.12 = (f32[32,2048]{1,0:T(8,128)S(1)}, f32[32,2048]{1,0:T(8,128)S(1)}, u32[]{:S(2)}, u32[]{:S(2)}) collective-permute-start(f32[32,2048]{1,0:T(8,128)S(1)} %collective-permute-done.10.rest_6_), channel_id=1, source_target_pairs={{0,1},{1,0},{2,3},{3,2},{4,5},{5,4},{6,7},{7,6},{8,9},{9,8},{10,11... | collective-permute-start | bytes 786440 | tf_op jit(solution)/shard_map/ppermute | solution.py:658

commit v8 on v7

--- a/solution.py
+++ b/solution.py
@@ -497,7 +497,7 @@
 def loading_call(features, right_side, noise_var, inv_scale, block_pairs, size):
     depth = features.shape[0]
     probes = right_side.shape[0]
-    half = min(depth, (depth + probes) // 16 * 8)
+    half = min(depth, (depth + probes) * 5 // 64 * 8)
     shapes = [
         (half, size),
         (depth + probes - half, size),

time: 66.3 us -> 66.4 us (level); the launches traced: 65.5 us -> 66.5 us
  Pallas kernels: 30 us -> 14.2 us
  starting transfers between devices: 18.3 us -> 31.4 us
  blocking collectives: 13.3 us -> 16.7 us
    ppermute x3, starting transfers between devices: 5.5 us -> 18.8 us  [moved(): return lax.ppermute(x, BOTH, route)]
    pallas_call x1, Pallas kernels: 12 us -> 0.38 us  [crossing_call(): pl.pallas_call(crossing_kernel, in_specs=[SMEM] + [VMEM] * len(arrays), o...]
    all_to_all x1, blocking collectives: 13.3 us -> 16.7 us  [own_block_body(): sums = lax.all_to_all(sums, BOTH, 0, 0)]
    pallas_call x1, Pallas kernels: 3.28 us -> 0.63 us  [second_call(): pl.pallas_call(second_kernel, in_specs=[SMEM] + [VMEM] * len(arrays), out...]
    pallas_call x1, Pallas kernels: 1.67 us -> 0.14 us  [over_call(): pl.pallas_call(over_kernel, in_specs=[SMEM] + [VMEM] * 4, out_specs=VMEM,...]
  transfers between devices with their start and end apart: 13 -> 13, of which waited for: 3 -> 3; matrix products, arithmetic and copies ran while one was open for 0% -> 0% of each run, Pallas kernels for 21% -> 15%
where the time goes in v8:
time: 66.4 us; the launch traced here: 66.5 us
  starting transfers between devices  31.4 us (47%)
  blocking collectives  16.7 us (25%)
  Pallas kernels  14.2 us (21%)
  waiting for transfers between devices  2.45 us (4%)
  between operations  1.58 us (2%)
    ppermute x3, starting transfers between devices, moved(): return lax.ppermute(x, BOTH, route)  18.8 us
    all_to_all x1, blocking collectives, own_block_body(): sums = lax.all_to_all(sums, BOTH, 0, 0)  16.7 us
    ppermute x8, starting transfers between devices, exchanged(): return lax.ppermute(x, BOTH, [(i, i ^ distance) for i in range(count)])  11.2 us
    pallas_call x1, Pallas kernels, diagonal_call(): pl.pallas_call(diagonal_kernel, in_specs=[SMEM, VMEM, VMEM, VMEM], out_sp...  3.53 us
    pallas_call x1, Pallas kernels, lower_diagonal_call(): pl.pallas_call(lower_diagonal_kernel, in_specs=[SMEM] + [VMEM] * 5, out_s...  3.46 us
    ppermute x8, waiting for transfers between devices, exchanged(): return lax.ppermute(x, BOTH, [(i, i ^ distance) for i in range(count)])  2.42 us
    pallas_call x1, Pallas kernels, final_call(): pl.pallas_call(final_kernel, in_specs=[VMEM] * (2 + 2 * members), out_spe...  2.27 us
    pallas_call x1, Pallas kernels, second_diagonal_call(): pl.pallas_call(second_diagonal_kernel, in_specs=[SMEM] + [VMEM] * 7, out_...  1.99 us
  transfers between devices with their start and end apart: 13, of which 3 were waited for; matrix products, arithmetic and copies ran while one was open for 0% of the time, Pallas kernels for 15%

profile of v8, /device:TPU:0, one launch (start us, length us, event | category | flops | bytes accessed | tf_op | source)
XLA Modules:
  0.0 66.5 jit_solution(16680929009114901269)
XLA Ops:
  0.6 1.8 %shard_map.77 = (f32[56,2048]{1,0:T(8,128)S(1)}, f32[40,2048]{1,0:T(8,128)S(1)}, f32[64,2048]{1,0:T(8,128)S(1)}, f32[32,2048]{1,0:T(8,128)S(1)}, f32[64,2048]{1,...) custom-call(f32[64,8192]{1,0:T(8,128)} %features.1, ...), custom_call_target="tpu_custom_call" | custom-call | flops 2000000000 | bytes 6000000 | tf_op jit(solution)/shard_map/pallas_call | solution.py:512
  2.4 0.7 %collective-permute-start.2 = (f32[56,2048]{1,0:T(8,128)S(1)}, f32[56,2048]{1,0:T(8,128)S(1)}, u32[]{:S(2)}, u32[]{:S(2)}) collective-permute-start(f32[56,2048]{1,0:T(8,128)S(1)} %get-tuple-element.47), channel_id=1, source_target_pairs={{7,3},{8,4},{15,11},{16,12},{23,19},{24,20},{31,27}} | collective-permute-start | bytes 1376264 | tf_op jit(solution)/shard_map/ppermute | solution.py:667
  3.1 3.0 %collective-permute-start = (f32[8,128]{1,0:T(8,128)S(1)}, f32[8,128]{1,0:T(8,128)S(1)}, u32[]{:S(2)}, u32[]{:S(2)}) collective-permute-start(f32[8,128]{1,0:T(8,128)S(1)} %get-tuple-element.39), channel_id=1, source_target_pairs={{0,2},{1,3},{2,0},{3,1},{4,6},{5,7},{6,4},{7,5},{8,10},{9,11},{10,... | collective-permute-start | bytes 12296 | tf_op jit(solution)/shard_map/ppermute | solution.py:658
  6.2 0.7 %collective-permute-start.3 = (f32[40,2048]{1,0:T(8,128)S(1)}, f32[40,2048]{1,0:T(8,128)S(1)}, u32[]{:S(2)}, u32[]{:S(2)}) collective-permute-start(f32[40,2048]{1,0:T(8,128)S(1)} %get-tuple-element.48), channel_id=1, source_target_pairs={{4,3},{11,4},{12,11},{19,12},{20,19},{27,20},{28,27}} | collective-permute-start | bytes 983048 | tf_op jit(solution)/shard_map/ppermute | solution.py:667
  7.5 3.5 %shard_map.78 = (bf16[512,2048]{1,0:T(8,128)(2,1)S(1)}, f32[32,2048]{1,0:T(8,128)S(1)}, bf16[2048,256]{1,0:T(8,128)(2,1)S(1)}, bf16[256,2048]{1,0:T(8,128)(2,1)S(1)}, bf16[32,2048]{1,0:T(8,128)(2,1)S(1)}) custom-call(f32[1]{0:T(128)S(6)} %copy.8.signal, f32[64,2048]{1,0:T(8,128)S(1)} %get-tuple-element.40.raw, f32[1,64]{1,0:T(1,128)S(1)} %get-tuple-element.41.scale, ...), custom_call_target="tpu_custom_call" | custom-call | flops 4000000000 | bytes 12000000 | tf_op jit(solution)/shard_map/pallas_call | solution.py:529
  11.0 0.0 collective-permute-done
  11.1 0.2 collective-permute-start.1
  11.3 1.0 %collective-permute-done.1 = f32[8,128]{1,0:T(8,128)S(1)} collective-permute-done((f32[8,128]{1,0:T(8,128)S(1)}, f32[8,128]{1,0:T(8,128)S(1)}, u32[]{:S(2)}, u32[]{:S(2)}) %collective-permute-start.1) | collective-permute-done | bytes 4128 | tf_op jit(solution)/shard_map/ppermute | solution.py:658
  12.3 0.0 collective-permute-done.3.sent_rest
  12.3 0.0 collective-permute-done.2.sent
  12.3 0.4 shard_map.79
  12.7 13.9 %collective-permute-start.4 = (f32[40,2048]{1,0:T(8,128)S(1)}, f32[40,2048]{1,0:T(8,128)S(1)}, u32[]{:S(2)}, u32[]{:S(2)}) collective-permute-start(f32[40,2048]{1,0:T(8,128)S(1)} %get-tuple-element.59.over), channel_id=1, source_target_pairs={{0,1},{1,2},{2,3},{3,7},{7,6},{6,5},{5,4},{4,8},{8,9},{9,10},{10,1... | collective-permute-start | bytes 983048 | tf_op jit(solution)/shard_map/ppermute | solution.py:653
  26.6 3.5 %shard_map.80 = (bf16[1536,2048]{1,0:T(8,128)(2,1)S(1)}, f32[32,2048]{1,0:T(8,128)S(1)}) custom-call(f32[1]{0:T(128)S(6)} %copy.8.signal, bf16[2048,256]{1,0:T(8,128)(2,1)S(1)} %get-tuple-element.49.left, bf16[256,2048]{1,0:T(8,128)(2,1)S(1)} %get-tuple-element.55.right, bf16[32,2048]{1,0:T(8,128)(2,1)S(1)} %get-tuple-element.50.half, ...), custom_call_target="tpu_custom_call" | custom-call | flops 4000000000 | bytes 12000000 | tf_op jit(solution)/shard_map/pallas_call | solution.py:548
  30.1 1.3 %collective-permute-start.5 = (f32[32,2048]{1,0:T(8,128)S(1)}, f32[32,2048]{1,0:T(8,128)S(1)}, u32[]{:S(2)}, u32[]{:S(2)}) collective-permute-start(f32[32,2048]{1,0:T(8,128)S(1)} %get-tuple-element.58), channel_id=1, source_target_pairs={{1,0},{2,1},{3,2},{7,3},{6,7},{5,6},{4,5},{8,4},{9,8},{10,9},{11,1... | collective-permute-start | bytes 786440 | tf_op jit(solution)/shard_map/ppermute | solution.py:653
  31.4 0.0 collective-permute-done.4.got
  31.4 1.2 %collective-permute-start.7 = (f32[32,2048]{1,0:T(8,128)S(1)}, f32[32,2048]{1,0:T(8,128)S(1)}, u32[]{:S(2)}, u32[]{:S(2)}) collective-permute-start(f32[32,2048]{1,0:T(8,128)S(1)} %slice_add_fusion.image.rest_0_), channel_id=1, source_target_pairs={{0,1},{1,0},{2,3},{3,2},{4,5},{5,4},{6,7},{7,6},{8,9},{9,8},{10,11... | collective-permute-start | bytes 786440 | tf_op jit(solution)/shard_map/ppermute | solution.py:658
  32.6 1.2 %collective-permute-start.8 = (f32[32,2048]{1,0:T(8,128)S(1)}, f32[32,2048]{1,0:T(8,128)S(1)}, u32[]{:S(2)}, u32[]{:S(2)}) collective-permute-start(f32[32,2048]{1,0:T(8,128)S(1)} %slice_add_fusion.image.rest_0_), channel_id=1, source_target_pairs={{0,2},{1,3},{2,0},{3,1},{4,6},{5,7},{6,4},{7,5},{8,10},{9,11},{10,... | collective-permute-start | bytes 786440 | tf_op jit(solution)/shard_map/ppermute | solution.py:658
  33.8 0.1 shard_map.81.over2
  33.9 3.6 %collective-permute-start.6 = (f32[32,2048]{1,0:T(8,128)S(1)}, f32[32,2048]{1,0:T(8,128)S(1)}, u32[]{:S(2)}, u32[]{:S(2)}) collective-permute-start(f32[32,2048]{1,0:T(8,128)S(1)} %shard_map.81.over2), channel_id=1, source_target_pairs={{0,1},{1,2},{2,3},{3,7},{7,6},{6,5},{5,4},{4,8},{8,9},{9,10},{10,1... | collective-permute-start | bytes 786440 | tf_op jit(solution)/shard_map/ppermute | solution.py:653
  37.6 2.0 %shard_map.82.partial = f32[32,2048]{1,0:T(8,128)S(1)} custom-call(f32[1]{0:T(128)S(6)} %copy.8.signal, bf16[512,2048]{1,0:T(8,128)(2,1)S(1)} %get-tuple-element.60.upper, bf16[1536,2048]{1,0:T(8,128)(2,1)S(1)} %get-tuple-element.61.lower, f32[8,2048]{1,0:T(8,128)S(1)} %get-tuple-element.62.row_sums, f32[1,2048]{1,0:T(1,128)S(1)} %get-tuple-element.51.noise, ...), custom_call_target="tpu_custom_call" | custom-call | flops 2000000000 | bytes 6000000 | tf_op jit(solution)/shard_map/pallas_call | solution.py:600
  39.6 0.0 collective-permute-done.5.part
  39.6 0.0 copy-start
  39.6 0.6 shard_map.83
  40.2 0.0 collective-permute-done.6
  40.3 5.1 %collective-permute-start.10 = (f32[32,2048]{1,0:T(8,128)S(1)}, f32[32,2048]{1,0:T(8,128)S(1)}, u32[]{:S(2)}, u32[]{:S(2)}) collective-permute-start(f32[32,2048]{1,0:T(8,128)S(1)} %add.15.rest_4_), channel_id=1, source_target_pairs={{0,2},{1,3},{2,0},{3,1},{4,6},{5,7},{6,4},{7,5},{8,10},{9,11},{10,... | collective-permute-start | bytes 786440 | tf_op jit(solution)/shard_map/ppermute | solution.py:658
  45.4 0.0 collective-permute-start.9
  45.4 0.0 collective-permute-done.7.rest_1_
  45.4 0.0 collective-permute-done.8.rest_2_
  45.4 16.7 %all_to_all.5.sums = f32[32,8,128]{2,1,0:T(8,128)S(1)} all-to-all(f32[32,8,128]{2,1,0:T(8,128)S(1)} %get-tuple-element.68), channel_id=1, replica_groups=mesh['blk'=8,'pair'=4] {'blk','pair'}, dimensions={0} | all-to-all | bytes 262144 | tf_op jit(solution)/shard_map/all_to_all | solution.py:714
  62.1 0.0 collective-permute-done.10.rest_6_
  62.1 0.0 collective-permute-done.9.rest_5_
  62.1 0.2 collective-permute-start.11
  62.3 0.3 collective-permute-start.12
  62.6 1.0 %collective-permute-done.11.rest_3_ = f32[32,2048]{1,0:T(8,128)S(1)} collective-permute-done((f32[32,2048]{1,0:T(8,128)S(1)}, f32[32,2048]{1,0:T(8,128)S(1)}, u32[]{:S(2)}, u32[]{:S(2)}) %collective-permute-start.11) | collective-permute-done | bytes 262176 | tf_op jit(solution)/shard_map/ppermute | solution.py:658
  63.7 0.4 collective-permute-done.12.rest_7_
  64.0 0.0 copy-done
  64.0 2.3 %shard_map.84 = (f32[32,8192]{1,0:T(8,128)}, f32[32,8192]{1,0:T(8,128)}) custom-call(f32[32,8,128]{2,1,0:T(8,128)S(1)} %all_to_all.5.sums, f32[32,8192]{1,0:T(8,128)S(1)} %copy-done, f32[32,2048]{1,0:T(8,128)S(1)} %slice_add_fusion.image.rest_0_, f32[32,2048]{1,0:T(8,128)S(1)} %collective-permute-done.7.rest_1_, ...), custom_call_target="tpu_custom_call" | custom-call | flops 3000000000 | bytes 9000000 | tf_op jit(solution)/shard_map/pallas_call | solution.py:627
  (4 shorter events, 0.1 us)
Async XLA Ops:
  2.4 9.9 %collective-permute-start.2 = (f32[56,2048]{1,0:T(8,128)S(1)}, f32[56,2048]{1,0:T(8,128)S(1)}, u32[]{:S(2)}, u32[]{:S(2)}) collective-permute-start(f32[56,2048]{1,0:T(8,128)S(1)} %get-tuple-element.47), channel_id=1, source_target_pairs={{7,3},{8,4},{15,11},{16,12},{23,19},{24,20},{31,27}} | collective-permute-start | bytes 1376264 | tf_op jit(solution)/shard_map/ppermute | solution.py:667
  3.1 7.9 %collective-permute-start = (f32[8,128]{1,0:T(8,128)S(1)}, f32[8,128]{1,0:T(8,128)S(1)}, u32[]{:S(2)}, u32[]{:S(2)}) collective-permute-start(f32[8,128]{1,0:T(8,128)S(1)} %get-tuple-element.39), channel_id=1, source_target_pairs={{0,2},{1,3},{2,0},{3,1},{4,6},{5,7},{6,4},{7,5},{8,10},{9,11},{10,... | collective-permute-start | bytes 12296 | tf_op jit(solution)/shard_map/ppermute | solution.py:658
  6.2 6.1 %collective-permute-start.3 = (f32[40,2048]{1,0:T(8,128)S(1)}, f32[40,2048]{1,0:T(8,128)S(1)}, u32[]{:S(2)}, u32[]{:S(2)}) collective-permute-start(f32[40,2048]{1,0:T(8,128)S(1)} %get-tuple-element.48), channel_id=1, source_target_pairs={{4,3},{11,4},{12,11},{19,12},{20,19},{27,20},{28,27}} | collective-permute-start | bytes 983048 | tf_op jit(solution)/shard_map/ppermute | solution.py:667
  11.1 1.2 %collective-permute-start.1 = (f32[8,128]{1,0:T(8,128)S(1)}, f32[8,128]{1,0:T(8,128)S(1)}, u32[]{:S(2)}, u32[]{:S(2)}) collective-permute-start(f32[8,128]{1,0:T(8,128)S(1)} %add.12), channel_id=1, source_target_pairs={{0,1},{1,0},{2,3},{3,2},{4,5},{5,4},{6,7},{7,6},{8,9},{9,8},{10,11... | collective-permute-start | bytes 12296 | tf_op jit(solution)/shard_map/ppermute | solution.py:658
  12.7 18.7 %collective-permute-start.4 = (f32[40,2048]{1,0:T(8,128)S(1)}, f32[40,2048]{1,0:T(8,128)S(1)}, u32[]{:S(2)}, u32[]{:S(2)}) collective-permute-start(f32[40,2048]{1,0:T(8,128)S(1)} %get-tuple-element.59.over), channel_id=1, source_target_pairs={{0,1},{1,2},{2,3},{3,7},{7,6},{6,5},{5,4},{4,8},{8,9},{9,10},{10,1... | collective-permute-start | bytes 983048 | tf_op jit(solution)/shard_map/ppermute | solution.py:653
  30.1 9.5 %collective-permute-start.5 = (f32[32,2048]{1,0:T(8,128)S(1)}, f32[32,2048]{1,0:T(8,128)S(1)}, u32[]{:S(2)}, u32[]{:S(2)}) collective-permute-start(f32[32,2048]{1,0:T(8,128)S(1)} %get-tuple-element.58), channel_id=1, source_target_pairs={{1,0},{2,1},{3,2},{7,3},{6,7},{5,6},{4,5},{8,4},{9,8},{10,9},{11,1... | collective-permute-start | bytes 786440 | tf_op jit(solution)/shard_map/ppermute | solution.py:653
  31.4 14.0 %collective-permute-start.7 = (f32[32,2048]{1,0:T(8,128)S(1)}, f32[32,2048]{1,0:T(8,128)S(1)}, u32[]{:S(2)}, u32[]{:S(2)}) collective-permute-start(f32[32,2048]{1,0:T(8,128)S(1)} %slice_add_fusion.image.rest_0_), channel_id=1, source_target_pairs={{0,1},{1,0},{2,3},{3,2},{4,5},{5,4},{6,7},{7,6},{8,9},{9,8},{10,11... | collective-permute-start | bytes 786440 | tf_op jit(solution)/shard_map/ppermute | solution.py:658
  32.6 12.8 %collective-permute-start.8 = (f32[32,2048]{1,0:T(8,128)S(1)}, f32[32,2048]{1,0:T(8,128)S(1)}, u32[]{:S(2)}, u32[]{:S(2)}) collective-permute-start(f32[32,2048]{1,0:T(8,128)S(1)} %slice_add_fusion.image.rest_0_), channel_id=1, source_target_pairs={{0,2},{1,3},{2,0},{3,1},{4,6},{5,7},{6,4},{7,5},{8,10},{9,11},{10,... | collective-permute-start | bytes 786440 | tf_op jit(solution)/shard_map/ppermute | solution.py:658
  33.9 6.3 %collective-permute-start.6 = (f32[32,2048]{1,0:T(8,128)S(1)}, f32[32,2048]{1,0:T(8,128)S(1)}, u32[]{:S(2)}, u32[]{:S(2)}) collective-permute-start(f32[32,2048]{1,0:T(8,128)S(1)} %shard_map.81.over2), channel_id=1, source_target_pairs={{0,1},{1,2},{2,3},{3,7},{7,6},{6,5},{5,4},{4,8},{8,9},{9,10},{10,1... | collective-permute-start | bytes 786440 | tf_op jit(solution)/shard_map/ppermute | solution.py:653
  39.6 24.4 %copy-start = (f32[32,8192]{1,0:T(8,128)S(1)}, f32[32,8192]{1,0:T(8,128)}, u32[]{:S(2)}) copy-start(f32[32,8192]{1,0:T(8,128)} %right_side.3) | copy-start | bytes 3145732
  40.3 21.8 %collective-permute-start.10 = (f32[32,2048]{1,0:T(8,128)S(1)}, f32[32,2048]{1,0:T(8,128)S(1)}, u32[]{:S(2)}, u32[]{:S(2)}) collective-permute-start(f32[32,2048]{1,0:T(8,128)S(1)} %add.15.rest_4_), channel_id=1, source_target_pairs={{0,2},{1,3},{2,0},{3,1},{4,6},{5,7},{6,4},{7,5},{8,10},{9,11},{10,... | collective-permute-start | bytes 786440 | tf_op jit(solution)/shard_map/ppermute | solution.py:658
  45.4 16.7 %collective-permute-start.9 = (f32[32,2048]{1,0:T(8,128)S(1)}, f32[32,2048]{1,0:T(8,128)S(1)}, u32[]{:S(2)}, u32[]{:S(2)}) collective-permute-start(f32[32,2048]{1,0:T(8,128)S(1)} %add.15.rest_4_), channel_id=1, source_target_pairs={{0,1},{1,0},{2,3},{3,2},{4,5},{5,4},{6,7},{7,6},{8,9},{9,8},{10,11... | collective-permute-start | bytes 786440 | tf_op jit(solution)/shard_map/ppermute | solution.py:658
  62.1 1.5 %collective-permute-start.11 = (f32[32,2048]{1,0:T(8,128)S(1)}, f32[32,2048]{1,0:T(8,128)S(1)}, u32[]{:S(2)}, u32[]{:S(2)}) collective-permute-start(f32[32,2048]{1,0:T(8,128)S(1)} %collective-permute-done.8.rest_2_), channel_id=1, source_target_pairs={{0,1},{1,0},{2,3},{3,2},{4,5},{5,4},{6,7},{7,6},{8,9},{9,8},{10,11... | collective-permute-start | bytes 786440 | tf_op jit(solution)/shard_map/ppermute | solution.py:658
  62.3 1.7 %collective-permute-start.12 = (f32[32,2048]{1,0:T(8,128)S(1)}, f32[32,2048]{1,0:T(8,128)S(1)}, u32[]{:S(2)}, u32[]{:S(2)}) collective-permute-start(f32[32,2048]{1,0:T(8,128)S(1)} %collective-permute-done.10.rest_6_), channel_id=1, source_target_pairs={{0,1},{1,0},{2,3},{3,2},{4,5},{5,4},{6,7},{7,6},{8,9},{9,8},{10,11... | collective-permute-start | bytes 786440 | tf_op jit(solution)/shard_map/ppermute | solution.py:658
